TPU v7x, 256 devices: a whole 4x4x8 slice. The times are simulated.
256 devices in a mesh: dp: 16 (over z_hi, x, core), fsdp: 16 (over z_lo, y).
Axes of the slice: x: 4, y: 4, z: 8 (z_hi: 2, z_lo: 4; z = z_hi * 4 + z_lo), core: 2. Of those that a mesh axis runs over, the one named last changes fastest.
Arguments:
- vlm_rows: bfloat16 [256, 32, 7168], P(('dp', 'fsdp')), may hold values from -300 to 300
- images: int32 [256], P(('dp', 'fsdp')), may hold values from 1 to 2
- action_hidden: bfloat16 [256, 128, 1536], P(('dp', 'fsdp')), may hold values from -1000 to 1000
- lengths: int32 [256], P(('dp', 'fsdp')), may hold values from 1 to 16
- vlm_weight: bfloat16 [7168, 7168], P('dp', 'fsdp'), may hold values from -0.0625 to 0.0625
- kv_weight: bfloat16 [3072, 7168], P('fsdp', 'dp'), may hold values from -0.0625 to 0.0625
- query_weight: bfloat16 [1536, 1536], replicated, may hold values from -0.15625 to 0.15625
- context_grad: bfloat16 [256, 128, 1536], P(('dp', 'fsdp')), may hold values from -0.75 to 0.75
Outputs:
- context: bfloat16 [256, 128, 1536], P(('dp', 'fsdp'))
- kv_weight_grad: float32 [3072, 7168], P('fsdp', 'dp')
Inputs may be any that keep to these rules, and one draw needn't show every extreme that they name: Rows r of sample s with r < 16 * images[s] hold image tokens, the others are padding.
All inputs are finite; a program needn't handle non-finite values.
Results may differ from a plain program's by a relative error of at most 0.025.
The roundings to bfloat16 on the way count: a program that leaves them out, or rounds other values in their place, can miss the bound.
Values may be sent and summed in bfloat16 or wider, within the bound.
No kernel may reach another device: no remote copies, remote signals or barrier semaphores. Data moves between devices by JAX's collectives and lax.ppermute only.
A program may use at most 64 MiB of HBM per device.

v0:
```python
import jax
import jax.numpy as jnp
from jax import lax
from jax.sharding import PartitionSpec as P

HEAD_DIM = 48
IMG_TOK = 16
ACT = 16


eps = 1e-06
masked_value = -1e30


def normalize(rows):
    widened = rows.astype(jnp.float32)
    return (widened * lax.rsqrt(jnp.mean(widened * widened, axis=-1, keepdims=True) + eps)).astype(
        jnp.bfloat16
    )


def cross_attention(kv_rows, queries, images, lengths, context_grad):
    samples, qrows, width_act = queries.shape
    heads = width_act // HEAD_DIM
    softmax_scale = HEAD_DIM ** (-0.5)
    keys = kv_rows[:, :width_act].reshape(samples, -1, heads, HEAD_DIM)
    values = kv_rows[:, width_act:].reshape(samples, -1, heads, HEAD_DIM)
    query_heads = queries.reshape(samples, qrows, heads, HEAD_DIM)
    scores = (
        jnp.einsum("sqhd,skhd->shqk", query_heads, keys, preferred_element_type=jnp.float32)
        * softmax_scale
    )
    key_rows = keys.shape[1]
    key_live = jnp.arange(key_rows, dtype=jnp.int32)[None, :] < images[:, None] * IMG_TOK
    scores = jnp.where(key_live[:, None, None, :], scores, masked_value)
    row_peak = jnp.max(scores, axis=-1, keepdims=True)
    exponent = jnp.exp(scores - row_peak)
    probs = exponent / jnp.sum(exponent, axis=-1, keepdims=True)
    probs_low = probs.astype(jnp.bfloat16)
    query_live = (jnp.arange(qrows, dtype=jnp.int32) % ACT)[None, :] < lengths[:, None]
    mixed_heads = jnp.einsum(
        "shqk,skhd->sqhd", probs_low, values, preferred_element_type=jnp.float32
    )
    context = jnp.where(query_live[:, :, None, None], mixed_heads, 0.0).astype(jnp.bfloat16)
    context = context.reshape(samples, qrows, width_act)
    grad_in = jnp.where(query_live[:, :, None], context_grad, jnp.zeros_like(context_grad))
    grad_in = grad_in.reshape(samples, qrows, heads, HEAD_DIM)
    value_grad = jnp.einsum(
        "shqk,sqhd->skhd", probs_low, grad_in, preferred_element_type=jnp.float32
    )
    prob_grad = jnp.einsum("sqhd,skhd->shqk", grad_in, values, preferred_element_type=jnp.float32)
    centre = jnp.sum(prob_grad * probs, axis=-1, keepdims=True)
    score_grad = (probs * (prob_grad - centre)).astype(jnp.bfloat16)
    key_grad = (
        jnp.einsum("shqk,sqhd->skhd", score_grad, query_heads, preferred_element_type=jnp.float32)
        * softmax_scale
    )
    kv_grads = jnp.concatenate(
        [key_grad.reshape(-1, width_act), value_grad.reshape(-1, width_act)], axis=1
    )
    return (context, kv_grads.astype(jnp.bfloat16))


def on_device(
    vlm_rows, images, action_hidden, lengths, vlm_weight, kv_weight, query_weight, context_grad
):
    samples, slot_rows, width = vlm_rows.shape
    col_width = vlm_weight.shape[0]
    col_start = lax.axis_index("dp") * col_width
    flat_rows = vlm_rows.reshape(samples * slot_rows, width)
    contract_last = (((1,), (1,)), ((), ()))
    group_rows = lax.all_gather(flat_rows, "dp", axis=0, tiled=True)
    normed = normalize(group_rows)
    pre_act = lax.dot_general(
        normed,
        lax.all_gather(vlm_weight, "fsdp", axis=1, tiled=True),
        contract_last,
        preferred_element_type=jnp.float32,
    )
    resid = lax.dynamic_slice_in_dim(group_rows, col_start, col_width, 1).astype(jnp.float32)
    feature = (resid + jax.nn.silu(pre_act)).astype(jnp.bfloat16)
    kv_cols = lax.all_gather(kv_weight, "fsdp", axis=0, tiled=True)
    kv_rows = lax.psum_scatter(
        lax.dot_general(feature, kv_cols, contract_last, preferred_element_type=jnp.float32),
        "dp",
        scatter_dimension=0,
        tiled=True,
    ).astype(jnp.bfloat16)
    width_act = query_weight.shape[0]
    queries = lax.dot_general(
        action_hidden.reshape(-1, width_act),
        query_weight,
        contract_last,
        preferred_element_type=jnp.float32,
    )
    queries = queries.astype(jnp.bfloat16).reshape(action_hidden.shape)
    context, kv_grads = cross_attention(kv_rows, queries, images, lengths, context_grad)
    contract_first = (((0,), (0,)), ((), ()))
    partial_grad = lax.dot_general(
        lax.all_gather(kv_grads, "dp", axis=0, tiled=True),
        feature,
        contract_first,
        preferred_element_type=jnp.float32,
    )
    kv_weight_grad = lax.psum_scatter(
        partial_grad.astype(jnp.bfloat16), "fsdp", scatter_dimension=0, tiled=True
    ).astype(jnp.float32)
    return (context, kv_weight_grad)


def solution(mesh):
    in_specs = (
        P(("dp", "fsdp"), None, None),
        P(("dp", "fsdp")),
        P(("dp", "fsdp"), None, None),
        P(("dp", "fsdp")),
        P("dp", "fsdp"),
        P("fsdp", "dp"),
        P(),
        P(("dp", "fsdp"), None, None),
    )
    out_specs = (P(("dp", "fsdp"), None, None), P("fsdp", "dp"))
    return jax.shard_map(
        on_device, mesh=mesh, in_specs=in_specs, out_specs=out_specs, check_vma=False
    )
```

profile of v0, /device:TPU:32, one launch (start us, length us, event | category | flops | bytes accessed | tf_op | source)
XLA Modules:
  0.0 584.4 jit_solution(6452653925745754943)
XLA Ops:
  7.2 0.0 copy-start
  7.2 0.0 all-gather.12.cloned.1.call-start
  7.2 0.7 all-gather.12.cloned.1.call-update
  7.9 0.0 all-gather.6.cloned.1.call-start
  8.0 2.0 copy.29
  10.0 0.0 all-gather.6.cloned.1.call-update
  10.0 0.0 all-gather.8.cloned.1.call-start
  10.0 0.7 all-gather.8.cloned.1.call-update
  10.7 0.0 reduce-scatter.3.cloned.1.call-start
  10.8 102.2 %all-gather.12.cloned.1.call-done = bf16[1,512,7168]{2,1,0:T(8,128)(2,1)} async-done(((bf16[1,32,7168]{2,1,0:T(8,128)(2,1)}), bf16[1,512,7168]{2,1,0:T(8,128)(2,1)}) %all-gather.12.cloned.1.call-update) | async-done | bytes 7340048 | tf_op jit(solution)/shard_map/all_gather | solution.py:72
  113.0 1.4 constant_dynamic-slice_fusion
  114.3 0.2 copy.38
  114.5 4.6 fusion.1
  119.1 83.1 %all-gather.6.cloned.1.call-done = bf16[448,7168]{0,1:T(8,128)(2,1)} async-done(((bf16[448,448]{0,1:T(8,128)(2,1)}), bf16[448,7168]{0,1:T(8,128)(2,1)}) %all-gather.6.cloned.1.call-update) | async-done | bytes 6422544 | tf_op jit(solution)/shard_map/all_gather | solution.py:76
  202.2 9.0 %fusion.15 = bf16[512,448]{0,1:T(8,128)(2,1)S(1)} fusion(bf16[448,7168]{0,1:T(8,128)(2,1)} %all-gather.6.cloned.1.call-done, bf16[1,512,7168]{2,1,0:T(8,128)(2,1)} %all-gather.12.cloned.1.call-done, f32[512]{0:T(512)S(1)} %add_rsqrt_fusion, bf16[1,512,448]{1,2,0:T(8,128)(2,1)S(1)} %copy.38), kind=kOutput, calls=%fused_computation.23 | convolution fusion | flops 3300950016 | bytes 14682112 | tf_op jit(solution)/shard_map/dot_general | solution.py:74
  211.2 73.5 %all-gather.8.cloned.1.call-done = bf16[3072,448]{1,0:T(8,128)(2,1)} async-done(((bf16[192,448]{1,0:T(8,128)(2,1)}), bf16[3072,448]{1,0:T(8,128)(2,1)}) %all-gather.8.cloned.1.call-update) | async-done | bytes 2752528 | tf_op jit(solution)/shard_map/all_gather | solution.py:82
  284.7 6.4 %fusion.29 = f32[512,3072]{1,0:T(8,128)} fusion(bf16[512,448]{0,1:T(8,128)(2,1)S(1)} %fusion.15, bf16[3072,448]{1,0:T(8,128)(2,1)} %all-gather.8.cloned.1.call-done), kind=kOutput, calls=%fused_computation.44 | convolution fusion | flops 1409286144 | bytes 9502720 | tf_op jit(solution)/shard_map/dot_general | solution.py:84
  291.2 0.0 copy-start.1
  291.2 0.0 reduce-scatter.3.cloned.1.call-update
  291.2 0.0 all-gather.10.cloned.1.call-start
  291.2 0.0 copy-done
  291.2 4.0 convolution_convert_fusion.1
  295.3 0.2 copy.30
  296.8 0.0 copy-done.1
  296.8 0.2 copy.33
  297.1 117.8 %reduce-scatter.3.cloned.1.call-done = f32[32,3072]{1,0:T(8,128)} async-done(((f32[512,3072]{1,0:T(8,128)}), f32[32,3072]{1,0:T(8,128)}) %reduce-scatter.3.cloned.1.call-update) | async-done | bytes 393232 | tf_op jit(solution)/shard_map/reduce_scatter | solution.py:83
  414.9 1.0 convert_element_type.43
  415.9 0.2 reshape.140
  416.2 0.3 fusion.9
  416.4 1.1 fusion.28
  417.5 0.2 reshape.137
  417.8 0.3 fusion.13
  418.1 1.1 multiply_reduce_fusion
  419.2 1.4 fusion.14
  420.5 0.1 copy.35
  420.7 0.3 reshape.143
  421.0 0.1 copy.36
  421.1 0.3 reshape.144
  421.4 0.7 pad_maximum_fusion
  422.1 0.0 all-gather.10.cloned.1.call-update
  422.1 0.2 reduce-scatter.5.cloned.1.call-start
  422.4 67.2 %all-gather.10.cloned.1.call-done = bf16[512,3072]{1,0:T(8,128)(2,1)} async-done(((bf16[32,3072]{1,0:T(8,128)(2,1)}), bf16[512,3072]{1,0:T(8,128)(2,1)}) %all-gather.10.cloned.1.call-update) | async-done | bytes 3145744 | tf_op jit(solution)/shard_map/all_gather | solution.py:100
  489.6 5.4 convolution_convert_fusion
  495.0 0.0 reduce-scatter.5.cloned.1.call-update
  495.0 0.4 fusion.11
  495.4 0.9 copy.37
  496.3 79.5 %reduce-scatter.5.cloned.1.call-done = bf16[192,448]{1,0:T(8,128)(2,1)} async-done(((bf16[3072,448]{1,0:T(8,128)(2,1)}), bf16[192,448]{1,0:T(8,128)(2,1)}) %reduce-scatter.5.cloned.1.call-update) | async-done | bytes 172048 | tf_op jit(solution)/shard_map/reduce_scatter | solution.py:105
  575.8 1.7 convert_element_type.50
  (5 shorter events, 0.1 us)
Async XLA Ops:
  7.2 284.1 %copy-start = (bf16[1,128,1536]{2,1,0:T(8,128)(2,1)S(1)}, bf16[1,128,1536]{2,1,0:T(8,128)(2,1)}, u32[]{:S(2)}) copy-start(bf16[1,128,1536]{2,1,0:T(8,128)(2,1)} %param.10) | copy-start | bytes 1179652
  7.2 105.8 %all-gather.12.cloned.1.call-start = ((), (), s32[]{:S(2)}) async-start(), calls=%async_computation.7 | async-start | bytes 7798784 | tf_op jit(solution)/shard_map/all_gather | solution.py:72
  7.9 194.3 %all-gather.6.cloned.1.call-start = ((), (), s32[]{:S(2)}) async-start(), calls=%async_computation.2 | async-start | bytes 7798784 | tf_op jit(solution)/shard_map/all_gather | solution.py:76
  10.0 274.8 %all-gather.8.cloned.1.call-start = ((), (), s32[]{:S(2)}) async-start(), calls=%async_computation.3 | async-start | bytes 3342336 | tf_op jit(solution)/shard_map/all_gather | solution.py:82
  10.7 404.2 %reduce-scatter.3.cloned.1.call-start = ((), (), s32[]{:S(2)}) async-start(), calls=%async_computation.4 | async-start | bytes 6684672 | tf_op jit(solution)/shard_map/reduce_scatter | solution.py:83
  291.2 5.6 copy-start.1
  291.2 198.4 %all-gather.10.cloned.1.call-start = ((), (), s32[]{:S(2)}) async-start(), calls=%async_computation.5 | async-start | bytes 3342336 | tf_op jit(solution)/shard_map/all_gather | solution.py:100
  422.1 153.7 %reduce-scatter.5.cloned.1.call-start = ((), (), s32[]{:S(2)}) async-start(), calls=%async_computation.6 | async-start | bytes 3342336 | tf_op jit(solution)/shard_map/reduce_scatter | solution.py:105
Sparse Core Ops, SparseCore 0:
  10.7 102.1 all-gather.11
  114.7 87.4 all-gather.5
  204.0 80.6 all-gather.7
  291.3 123.5 reduce-scatter.2
  422.3 67.2 all-gather.9
  495.1 80.6 reduce-scatter.4
where the time goes:
time: 592 us; the launch traced here: 584 us
  waiting for transfers between devices  525 us (89%)
  matrix products  28.2 us (5%)
  between operations  15.6 us (3%)
  other arithmetic  9.18 us (2%)
  local copies, waits for them, and re-layouts  6.3 us (1%)
    reduce_scatter x1, waiting for transfers between devices, on_device(): lax.psum_scatter(lax.dot_general(feature, kv_cols, contract_last, preferr...  118 us
    all_gather x1, waiting for transfers between devices, on_device(): group_rows = lax.all_gather(flat_rows, 'dp', axis=0, tiled=True)  102 us
    all_gather x1, waiting for transfers between devices, on_device(): lax.all_gather(vlm_weight, 'fsdp', axis=1, tiled=True)  83.1 us
    reduce_scatter x1, waiting for transfers between devices, on_device(): lax.psum_scatter(partial_grad.astype(jnp.bfloat16), 'fsdp', scatter_dimen...  79.5 us
    all_gather x1, waiting for transfers between devices, on_device(): kv_cols = lax.all_gather(kv_weight, 'fsdp', axis=0, tiled=True)  73.5 us
    all_gather x1, waiting for transfers between devices, on_device(): lax.all_gather(kv_grads, 'dp', axis=0, tiled=True)  67.2 us
  transfers between devices with their start and end apart: 6, of which 6 were waited for; matrix products, arithmetic and copies ran while one was open for 4% of the time, Pallas kernels for 0%

commit v1 on v0

v1 whole, which is shorter than its diff:
```python
import jax
import jax.numpy as jnp
from jax import lax
from jax.experimental import pallas as pl
from jax.experimental.pallas import tpu as pltpu
from jax.sharding import PartitionSpec as P

HEAD_DIM = 48
IMG_TOK = 16
ACT = 16
AXES = ("dp", "fsdp")

eps = 1e-06
masked_value = -1e30
bf16 = jnp.bfloat16
f32 = jnp.float32
VMEM_BYTES = 56 * 1024 * 1024


def pairs(step):
    table = []
    for i in range(256):
        h, x, c, l, y = step(i >> 7, (i >> 5) & 3, (i >> 4) & 1, (i >> 2) & 3, i & 3)
        table.append((i, h << 7 | x << 5 | c << 4 | l << 2 | y))
    return table


CORE = pairs(lambda h, x, c, l, y: (h, x, c ^ 1, l, y))
MIRROR = pairs(lambda h, x, c, l, y: (h ^ 1, x, c, l ^ 3, y))
HALF = pairs(lambda h, x, c, l, y: (h ^ 1, x, c, l, y))
ALONG_X = [pairs(lambda h, x, c, l, y, e=e: (h, x ^ e, c, l, y)) for e in range(4)]


def send(array, table):
    return lax.ppermute(array, AXES, table)


def gather_group(own, partner):
    both = jnp.stack([own, send(own, partner)])
    return jnp.concatenate([both] + [send(both, ALONG_X[e]) for e in (1, 2, 3)], axis=0)


def norm_kernel(col_ref, rows_ref, normed_ref, resid_ref):
    widened = rows_ref[0].astype(f32)
    mean = jnp.mean(widened * widened, axis=-1, keepdims=True)
    normed = (widened * lax.rsqrt(mean + eps)).astype(bf16)
    blocks, _, depth = normed_ref.shape
    for f in range(blocks):
        normed_ref[f] = normed[:, f * depth : (f + 1) * depth]

        @pl.when(col_ref[0] == f)
        def _():
            resid_ref[...] = rows_ref[0, :, f * depth : (f + 1) * depth]


def normalize(rows, col):
    slots, height, width = rows.shape
    depth = width // 16
    return pl.pallas_call(
        norm_kernel,
        grid=(slots,),
        in_specs=[
            pl.BlockSpec(memory_space=pltpu.SMEM),
            pl.BlockSpec((1, height, width), lambda i: (i, 0, 0)),
        ],
        out_specs=[
            pl.BlockSpec((16, height, depth), lambda i: (0, i, 0)),
            pl.BlockSpec((height, depth), lambda i: (i, 0)),
        ],
        out_shape=[
            jax.ShapeDtypeStruct((16, slots * height, depth), bf16),
            jax.ShapeDtypeStruct((slots * height, depth), bf16),
        ],
        compiler_params=pltpu.CompilerParams(vmem_limit_bytes=VMEM_BYTES),
        name="norm",
    )(col, rows)


def layer_kernel(na_ref, nb_ref, ra_ref, rb_ref, w_ref, featt_ref, pa_ref, pb_ref, acc, kvw):
    k = pl.program_id(0)
    half = na_ref.shape[1]
    out = ra_ref.shape[1]
    kv = w_ref.shape[2] - out

    @pl.when(k == 0)
    def _():
        acc[...] = jnp.zeros_like(acc)

    w = w_ref[0, :, :out]
    acc[:half] += jnp.dot(na_ref[0], w, preferred_element_type=f32)
    acc[half:] += jnp.dot(nb_ref[0], w, preferred_element_type=f32)
    for odd in range(2):

        @pl.when(k % 2 == odd)
        def _():
            kvw[k // 2, :, odd * kv : (odd + 1) * kv] = w_ref[0, :, out:]

    @pl.when(k == pl.num_programs(0) - 1)
    def _():
        for lo, r_ref, p_ref in ((0, ra_ref, pa_ref), (half, rb_ref, pb_ref)):
            pre = acc[lo : lo + half]
            feature = (r_ref[...].astype(f32) + pre / (1.0 + jnp.exp(-pre))).astype(bf16)
            featt_ref[:, lo : lo + half] = feature.T
            for j in range(kvw.shape[0]):
                p_ref[:, j * 2 * kv : (j + 1) * 2 * kv] = jnp.dot(
                    feature, kvw[j], preferred_element_type=f32
                ).astype(p_ref.dtype)


def layer(na, nb, ra, rb, weights):
    blocks, half, depth = na.shape
    out = ra.shape[1]
    kv = weights.shape[2] - out
    row_block = pl.BlockSpec((1, half, depth), lambda k: (k, 0, 0))

    def whole(shape):
        return pl.BlockSpec(shape, lambda k: (0, 0))

    return pl.pallas_call(
        layer_kernel,
        grid=(blocks,),
        in_specs=[
            row_block,
            row_block,
            whole(ra.shape),
            whole(rb.shape),
            pl.BlockSpec((1, depth, out + kv), lambda k: (k, 0, 0)),
        ],
        out_specs=[whole((out, 2 * half)), whole((half, blocks * kv)), whole((half, blocks * kv))],
        out_shape=[
            jax.ShapeDtypeStruct((out, 2 * half), bf16),
            jax.ShapeDtypeStruct((half, blocks * kv), f32),
            jax.ShapeDtypeStruct((half, blocks * kv), bf16),
        ],
        scratch_shapes=[
            pltpu.VMEM((2 * half, out), f32),
            pltpu.VMEM((blocks // 2, depth, 2 * kv), bf16),
        ],
        compiler_params=pltpu.CompilerParams(vmem_limit_bytes=VMEM_BYTES),
        name="layer",
    )(na, nb, ra, rb, weights)


def attention_kernel(
    images_ref, lengths_ref, own_ref, other_ref, q_ref, cg_ref, context_ref, grads_ref
):
    key_rows, width = own_ref.shape
    width_act = width // 2
    qrows = q_ref.shape[0]
    heads = 8
    cols = heads * HEAD_DIM
    scale = HEAD_DIM ** (-0.5)
    piece = grads_ref.shape[2]
    last = (((1,), (1,)), ((), ()))
    first = (((0,), (0,)), ((), ()))
    kv = (own_ref[...] + other_ref[...].astype(f32)).astype(bf16)
    row_head = lax.broadcasted_iota(jnp.int32, (heads * key_rows, cols), 0) // key_rows
    col_head = lax.broadcasted_iota(jnp.int32, (heads * key_rows, cols), 1) // HEAD_DIM
    same = row_head == col_head
    key_live = (
        lax.broadcasted_iota(jnp.int32, (heads, key_rows, qrows), 1) < images_ref[0] * IMG_TOK
    )
    query_live = lax.broadcasted_iota(jnp.int32, (qrows, cols), 0) % ACT < lengths_ref[0]

    def by_head(flat):
        return flat.reshape(heads, key_rows, qrows)

    def spread(rows):
        return jnp.where(same, jnp.concatenate([rows] * heads, axis=0), jnp.zeros((), bf16))

    def collapse(big):
        return jnp.sum(jnp.where(same, big, 0.0).reshape(heads, key_rows, cols), axis=0)

    for g in range(width_act // cols):
        at = slice(g * cols, (g + 1) * cols)
        keys = spread(kv[:, g * cols : (g + 1) * cols])
        values = spread(kv[:, width_act + g * cols : width_act + (g + 1) * cols])
        queries = q_ref[:, at]
        grad_in = jnp.where(query_live, cg_ref[:, at], jnp.zeros((), bf16))
        scores = by_head(lax.dot_general(keys, queries, last, preferred_element_type=f32) * scale)
        scores = jnp.where(key_live, scores, masked_value)
        exponent = jnp.exp(scores - jnp.max(scores, axis=1, keepdims=True))
        probs = exponent / jnp.sum(exponent, axis=1, keepdims=True)
        probs_low = probs.astype(bf16).reshape(heads * key_rows, qrows)
        mixed = lax.dot_general(probs_low, values, first, preferred_element_type=f32)
        context_ref[:, at] = jnp.where(query_live, mixed, 0.0).astype(bf16)
        prob_grad = by_head(lax.dot_general(values, grad_in, last, preferred_element_type=f32))
        centre = jnp.sum(prob_grad * probs, axis=1, keepdims=True)
        score_grad = (probs * (prob_grad - centre)).astype(bf16).reshape(heads * key_rows, qrows)
        value_grad = collapse(jnp.dot(probs_low, grad_in, preferred_element_type=f32)).astype(bf16)
        key_grad = jnp.dot(score_grad, queries, preferred_element_type=f32)
        key_grad = (collapse(key_grad) * scale).astype(bf16)
        per = cols // piece
        for start, grad in ((g * per, key_grad), (width_act // piece + g * per, value_grad)):
            for j in range(per):
                grads_ref[start + j] = grad[:, j * piece : (j + 1) * piece]


def attention(own, other, queries, images, lengths, context_grad):
    key_rows, width = own.shape
    smem, vmem = pl.BlockSpec(memory_space=pltpu.SMEM), pl.BlockSpec(memory_space=pltpu.VMEM)
    return pl.pallas_call(
        attention_kernel,
        in_specs=[smem, smem, vmem, vmem, vmem, vmem],
        out_specs=[vmem, vmem],
        out_shape=[
            jax.ShapeDtypeStruct(queries.shape, bf16),
            jax.ShapeDtypeStruct((16, key_rows, width // 16), bf16),
        ],
        compiler_params=pltpu.CompilerParams(vmem_limit_bytes=VMEM_BYTES),
        name="attention",
    )(images, lengths, own, other, queries, context_grad)


def weight_grad_kernel(a0_ref, a1_ref, b0_ref, b1_ref, featt_ref, out_ref, acc):
    f = pl.program_id(0)
    kv = out_ref.shape[0]

    @pl.when(f == 0)
    def _():
        acc[...] = jnp.zeros_like(acc)

    def rows(first_ref, second_ref):
        return jnp.stack([first_ref[:, 0, 0], second_ref[:, 0, 0]], axis=1).reshape(-1, kv)

    grads = jnp.concatenate([rows(a0_ref, a1_ref), rows(b0_ref, b1_ref)], axis=0)
    acc[...] += jnp.dot(featt_ref[0], grads, preferred_element_type=f32)

    @pl.when(f == pl.num_programs(0) - 1)
    def _():
        out_ref[...] = acc[...].T


def weight_grad(grads_a, grads_b, featt):
    blocks, out, rows = featt.shape
    slots, _, key_rows, kv = grads_a.shape
    grads_a = grads_a.reshape(slots // 2, 2, blocks, key_rows, kv)
    grads_b = grads_b.reshape(slots // 2, 2, blocks, key_rows, kv)
    block = (slots // 2, 1, 1, key_rows, kv)
    near = pl.BlockSpec(block, lambda f: (0, 0, f, 0, 0))
    far = pl.BlockSpec(block, lambda f: (0, 1, 12 - (f // 4) * 4 + f % 4, 0, 0))
    return pl.pallas_call(
        weight_grad_kernel,
        grid=(blocks,),
        in_specs=[near, far, near, far, pl.BlockSpec((1, out, rows), lambda f: (f, 0, 0))],
        out_specs=pl.BlockSpec((kv, out), lambda f: (0, 0)),
        out_shape=jax.ShapeDtypeStruct((kv, out), f32),
        scratch_shapes=[pltpu.VMEM((out, kv), f32)],
        compiler_params=pltpu.CompilerParams(vmem_limit_bytes=VMEM_BYTES),
        name="weight_grad",
    )(grads_a, grads_a, grads_b, grads_b, featt)


def on_device(
    vlm_rows, images, action_hidden, lengths, vlm_weight, kv_weight, query_weight, context_grad
):
    _, slot_rows, width = vlm_rows.shape
    width_act = query_weight.shape[0]
    col = lax.axis_index("dp").astype(jnp.int32).reshape(1)

    weights = lax.all_gather(
        jnp.concatenate([vlm_weight.T, kv_weight.T], axis=1), "fsdp", axis=0, tiled=False
    )
    rows_a = gather_group(vlm_rows[0], MIRROR)
    rows_b = send(rows_a, CORE)
    normed_a, resid_a = normalize(rows_a, col)
    normed_b, resid_b = normalize(rows_b, col)
    queries = lax.dot_general(
        action_hidden[0], query_weight, (((1,), (1,)), ((), ())), preferred_element_type=f32
    ).astype(bf16)
    featt, part_a, part_b = layer(normed_a, normed_b, resid_a, resid_b, weights)

    featt_all = lax.all_gather(featt, "fsdp", axis=0, tiled=False)

    both = part_a + send(part_b, CORE).astype(f32)
    both = both.reshape(4, 2, slot_rows, 2 * width_act)
    mine = both[0]
    for e in (1, 2, 3):
        mine = mine + send(both[e].astype(bf16), ALONG_X[e]).astype(f32)
    other = send(mine[1].astype(bf16), MIRROR)

    context, grads = attention(mine[0], other, queries, images, lengths, context_grad[0])

    grads = lax.all_to_all(grads, "fsdp", 0, 0, tiled=True)
    grads_a = gather_group(grads, HALF)
    grads_b = send(grads_a, CORE)
    kv_weight_grad = weight_grad(grads_a, grads_b, featt_all)
    return (context[None], kv_weight_grad)


def solution(mesh):
    in_specs = (
        P(("dp", "fsdp"), None, None),
        P(("dp", "fsdp")),
        P(("dp", "fsdp"), None, None),
        P(("dp", "fsdp")),
        P("dp", "fsdp"),
        P("fsdp", "dp"),
        P(),
        P(("dp", "fsdp"), None, None),
    )
    out_specs = (P(("dp", "fsdp"), None, None), P("fsdp", "dp"))
    return jax.shard_map(
        on_device, mesh=mesh, in_specs=in_specs, out_specs=out_specs, check_vma=False
    )
```

time: 592 us -> 315 us (0.53)
  the two profiles are of different devices: /device:TPU:32 before, /device:TPU:1 now
where the time goes in v1:
time: 315 us; the launch traced here: 314 us
  waiting for transfers between devices  140 us (44%)
  Pallas kernels  58.2 us (18%)
  blocking collectives  56.2 us (18%)
  starting transfers between devices  27 us (9%)
  between operations  15.5 us (5%)
  local copies, waits for them, and re-layouts  8.73 us (3%)
  matrix products  4.73 us (2%)
  other arithmetic  3.88 us (1%)
    ppermute x15, waiting for transfers between devices, send(): return lax.ppermute(array, AXES, table)  121 us
    all_to_all x1, blocking collectives, on_device(): grads = lax.all_to_all(grads, 'fsdp', 0, 0, tiled=True)  56.2 us
    ppermute x15, starting transfers between devices, send(): return lax.ppermute(array, AXES, table)  27 us
    pallas_call x2, Pallas kernels, normalize(): pl.pallas_call(norm_kernel, grid=(slots,), in_specs=[pl.BlockSpec(memory_...  20.8 us
    pallas_call x1, Pallas kernels, layer(): pl.pallas_call(layer_kernel, grid=(blocks,), in_specs=[row_block, row_blo...  19.9 us
    all_gather x1, waiting for transfers between devices, on_device(): lax.all_gather(jnp.concatenate([vlm_weight.T, kv_weight.T], axis=1), 'fsd...  18.8 us
    pallas_call x1, Pallas kernels, weight_grad(): pl.pallas_call(weight_grad_kernel, grid=(blocks,), in_specs=[near, far, n...  13.2 us
    unnamed x20, local copies, waits for them, and re-layouts  6.78 us
  transfers between devices with their start and end apart: 17, of which 15 were waited for; matrix products, arithmetic and copies ran while one was open for 4% of the time, Pallas kernels for 8%

profile of v1, /device:TPU:1, one launch (start us, length us, event | category | flops | bytes accessed | tf_op | source)
XLA Modules:
  0.0 313.9 jit_solution(732536460753101633)
XLA Ops:
  7.2 1.3 copy.11
  8.5 1.1 copy.12
  9.6 1.0 pad_maximum_fusion.1
  10.6 6.5 %collective-permute-start = (bf16[32,7168]{1,0:T(8,128)(2,1)S(1)}, bf16[32,7168]{1,0:T(8,128)(2,1)S(1)}, u32[]{:S(2)}, u32[]{:S(2)}) collective-permute-start(bf16[32,7168]{1,0:T(8,128)(2,1)S(1)} %bitcast.34), channel_id=1, source_target_pairs={{0,140},{1,141},{2,142},{3,143},{4,136},{5,137},{6,138},{7,139},{8... | collective-permute-start | bytes 1376264 | tf_op jit(solution)/shard_map/ppermute | solution.py:35
  17.1 0.8 constant_dynamic-update-slice_fusion.4
  18.0 19.7 %collective-permute-done = bf16[32,7168]{1,0:T(8,128)(2,1)S(1)} collective-permute-done((bf16[32,7168]{1,0:T(8,128)(2,1)S(1)}, bf16[32,7168]{1,0:T(8,128)(2,1)S(1)}, u32[]{:S(2)}, u32[]{:S(2)}) %collective-permute-start) | collective-permute-done | bytes 458784 | tf_op jit(solution)/shard_map/ppermute | solution.py:35
  37.7 1.3 collective-permute-start.1
  39.0 2.5 collective-permute-start.2
  41.5 0.2 collective-permute-start.3
  41.7 0.8 constant_dynamic-update-slice_fusion.3
  42.4 16.5 %collective-permute-done.1 = bf16[2,32,7168]{2,1,0:T(8,128)(2,1)S(1)} collective-permute-done((bf16[2,32,7168]{2,1,0:T(8,128)(2,1)S(1)}, bf16[2,32,7168]{2,1,0:T(8,128)(2,1)S(1)}, u32[]{:S(2)}, u32[]{:S(2)}) %collective-permute-start.1) | collective-permute-done | bytes 917536 | tf_op jit(solution)/shard_map/ppermute | solution.py:35
  59.0 1.0 constant_dynamic-update-slice_fusion.2
  60.0 20.9 %collective-permute-done.2 = bf16[2,32,7168]{2,1,0:T(8,128)(2,1)S(1)} collective-permute-done((bf16[2,32,7168]{2,1,0:T(8,128)(2,1)S(1)}, bf16[2,32,7168]{2,1,0:T(8,128)(2,1)S(1)}, u32[]{:S(2)}, u32[]{:S(2)}) %collective-permute-start.2) | collective-permute-done | bytes 917536 | tf_op jit(solution)/shard_map/ppermute | solution.py:35
  80.9 1.0 constant_dynamic-update-slice_fusion.1
  81.9 1.0 collective-permute-done.3
  82.9 1.0 constant_dynamic-update-slice_fusion.rows_ref
  83.9 2.2 collective-permute-start.4
  86.1 10.4 %norm.2 = (bf16[16,256,448]{2,1,0:T(8,128)(2,1)}, bf16[256,448]{1,0:T(8,128)(2,1)}) custom-call(s32[1]{0:T(128)} %bitcast.col_ref, bf16[8,32,7168]{2,1,0:T(8,128)(2,1)} %constant_dynamic-update-slice_fusion.rows_ref), custom_call_target="tpu_custom_call" | custom-call | tf_op jit(solution)/shard_map/norm/pallas_call | solution.py:59
  96.4 10.4 %norm.3 = (bf16[16,256,448]{2,1,0:T(8,128)(2,1)}, bf16[256,448]{1,0:T(8,128)(2,1)}) custom-call(s32[1]{0:T(128)} %bitcast.col_ref, bf16[8,32,7168]{2,1,0:T(8,128)(2,1)} %collective-permute-done.4.rows_ref), custom_call_target="tpu_custom_call" | custom-call | tf_op jit(solution)/shard_map/norm/pallas_call | solution.py:59
  106.8 18.8 %all-gather.5.cloned.1.call-done = bf16[7168,640]{1,0:T(8,128)(2,1)} async-done(((bf16[448,640]{1,0:T(8,128)(2,1)}), bf16[7168,640]{1,0:T(8,128)(2,1)}) %all-gather.5.cloned.1.call-update) | async-done | bytes 9175056 | tf_op jit(solution)/shard_map/all_gather | solution.py:261
  125.6 19.9 %layer.1 = (bf16[448,512]{1,0:T(8,128)(2,1)}, f32[256,3072]{1,0:T(8,128)}, bf16[256,3072]{1,0:T(8,128)(2,1)}) custom-call(bf16[16,256,448]{2,1,0:T(8,128)(2,1)} %get-tuple-element.11.na_ref, bf16[16,256,448]{2,1,0:T(8,128)(2,1)} %get-tuple-element.12.nb_ref, bf16[256,448]{1,0:T(8,128)(2,1)} %get-tuple-element.13.ra_ref, ...), custom_call_target="tpu_custom_call" | custom-call | tf_op jit(solution)/shard_map/layer/pallas_call | solution.py:119
  145.6 0.5 collective-permute-start.5
  146.1 3.2 %collective-permute-done.5 = bf16[256,3072]{1,0:T(8,128)(2,1)S(1)} collective-permute-done((bf16[256,3072]{1,0:T(8,128)(2,1)}, bf16[256,3072]{1,0:T(8,128)(2,1)S(1)}, u32[]{:S(2)}, u32[]{:S(2)}) %collective-permute-start.5) | collective-permute-done | bytes 1572896 | tf_op jit(solution)/shard_map/ppermute | solution.py:35
  149.4 2.5 fusion.2
  152.0 1.3 collective-permute-start.6
  153.3 2.5 collective-permute-start.7
  155.8 0.2 collective-permute-start.8
  157.3 4.7 %convolution_convert_fusion.q_ref = bf16[128,1536]{1,0:T(8,128)(2,1)} fusion(bf16[1536,1536]{1,0:T(8,128)(2,1)} %param.14, bf16[1,128,1536]{2,1,0:T(8,128)(2,1)S(1)} %copy-done), kind=kOutput, calls=%fused_computation.1 | convolution fusion | flops 604176384 | bytes 5505024 | tf_op jit(solution)/shard_map/dot_general | solution.py:268
  162.1 0.5 collective-permute-done.6
  162.5 10.6 %collective-permute-done.7 = bf16[2,32,3072]{2,1,0:T(8,128)(2,1)S(1)} collective-permute-done((bf16[2,32,3072]{2,1,0:T(8,128)(2,1)S(1)}, bf16[2,32,3072]{2,1,0:T(8,128)(2,1)S(1)}, u32[]{:S(2)}, u32[]{:S(2)}) %collective-permute-start.7) | collective-permute-done | bytes 393248 | tf_op jit(solution)/shard_map/ppermute | solution.py:35
  173.1 2.1 collective-permute-done.8
  175.4 0.6 collective-permute-start.9
  176.0 0.8 slice_bitcast_fusion.own_ref
  176.8 5.1 %collective-permute-done.9.other_ref = bf16[32,3072]{1,0:T(8,128)(2,1)S(1)} collective-permute-done((bf16[32,3072]{1,0:T(8,128)(2,1)S(1)}, bf16[32,3072]{1,0:T(8,128)(2,1)S(1)}, u32[]{:S(2)}, u32[]{:S(2)}) %collective-permute-start.9) | collective-permute-done | bytes 196640 | tf_op jit(solution)/shard_map/ppermute | solution.py:35
  181.9 0.7 copy-done.4
  182.6 4.4 %attention.1 = (bf16[128,1536]{1,0:T(8,128)(2,1)}, bf16[16,32,192]{2,1,0:T(8,128)(2,1)}) custom-call(s32[1]{0:T(128)S(6)} %copy.21.images_ref, s32[1]{0:T(128)S(6)} %copy.22.lengths_ref, f32[32,3072]{1,0:T(8,128)} %slice_bitcast_fusion.own_ref, bf16[32,3072]{1,0:T(8,128)(2,1)} %copy-done.4, bf16[128,1536]{1,0:T(8,128)(2,1)} %convolution_convert_fusion.q_ref, ...), custom_call_target="tpu_custom_call" | custom-call | tf_op jit(solution)/shard_map/attention/pallas_call | solution.py:202
  187.0 56.2 %all_to_all.5 = bf16[16,32,192]{2,1,0:T(8,128)(2,1)S(1)} all-to-all(bf16[16,32,192]{2,1,0:T(8,128)(2,1)} %get-tuple-element.18), channel_id=1, replica_groups=mesh['dp'=16,'fsdp'=16] {'fsdp'}, dimensions={0} | all-to-all | bytes 393216 | tf_op jit(solution)/shard_map/all_to_all | solution.py:284
  243.2 3.0 collective-permute-start.10
  246.2 13.1 %collective-permute-done.10 = bf16[16,32,192]{2,1,0:T(8,128)(2,1)S(1)} collective-permute-done((bf16[16,32,192]{2,1,0:T(8,128)(2,1)S(1)}, bf16[16,32,192]{2,1,0:T(8,128)(2,1)S(1)}, u32[]{:S(2)}, u32[]{:S(2)}) %collective-permute-start.10) | collective-permute-done | bytes 196640 | tf_op jit(solution)/shard_map/ppermute | solution.py:35
  259.4 0.9 collective-permute-start.11
  260.3 2.6 collective-permute-start.12
  263.0 0.5 collective-permute-start.13
  263.4 8.8 %collective-permute-done.11 = bf16[2,16,32,192]{3,2,1,0:T(8,128)(2,1)S(1)} collective-permute-done((bf16[2,16,32,192]{3,2,1,0:T(8,128)(2,1)S(1)}, bf16[2,16,32,192]{3,2,1,0:T(8,128)(2,1)S(1)}, u32[]{:S(2)}, u32[]{:S(2)}) %collective-permute-start.11) | collective-permute-done | bytes 393248 | tf_op jit(solution)/shard_map/ppermute | solution.py:35
  272.3 13.2 %collective-permute-done.12 = bf16[2,16,32,192]{3,2,1,0:T(8,128)(2,1)S(1)} collective-permute-done((bf16[2,16,32,192]{3,2,1,0:T(8,128)(2,1)S(1)}, bf16[2,16,32,192]{3,2,1,0:T(8,128)(2,1)S(1)}, u32[]{:S(2)}, u32[]{:S(2)}) %collective-permute-start.12) | collective-permute-done | bytes 393248 | tf_op jit(solution)/shard_map/ppermute | solution.py:35
  285.5 2.1 collective-permute-done.13
  287.7 2.3 collective-permute-start.14
  290.0 3.9 %collective-permute-done.14 = bf16[8,16,32,192]{3,2,1,0:T(8,128)(2,1)} collective-permute-done((bf16[8,16,32,192]{3,2,1,0:T(8,128)(2,1)S(1)}, bf16[8,16,32,192]{3,2,1,0:T(8,128)(2,1)}, u32[]{:S(2)}, u32[]{:S(2)}) %collective-permute-start.14) | collective-permute-done | bytes 1572896 | tf_op jit(solution)/shard_map/ppermute | solution.py:35
  293.9 13.2 %weight_grad.1 = f32[192,448]{1,0:T(8,128)} custom-call(bf16[4,2,16,32,192]{4,3,2,1,0:T(8,128)(2,1)} %bitcast.28, bf16[4,2,16,32,192]{4,3,2,1,0:T(8,128)(2,1)} %bitcast.29, bf16[4,2,16,32,192]{4,3,2,1,0:T(8,128)(2,1)} %bitcast.18.b0_ref.b1_ref, bf16[4,2,16,32,192]{4,3,2,1,0:T(8,128)(2,1)} %bitcast.18.b0_ref.b1_ref, bf16[16,448,512]{2,1,0:T(8,128)(2,1)} %bitcast.31), custom_call_target="tpu_custom_call" | custom-call | tf_op jit(solution)/shard_map/weight_grad/pallas_call | solution.py:242
  (26 shorter events, 0.8 us)
Async XLA Ops:
  7.2 150.1 %copy-start = (bf16[1,128,1536]{2,1,0:T(8,128)(2,1)S(1)}, bf16[1,128,1536]{2,1,0:T(8,128)(2,1)}, u32[]{:S(2)}) copy-start(bf16[1,128,1536]{2,1,0:T(8,128)(2,1)} %param.10) | copy-start | bytes 1179652
  7.2 3.5 %copy-start.3 = (bf16[1,32,7168]{2,1,0:T(8,128)(2,1)S(1)}, bf16[1,32,7168]{2,1,0:T(8,128)(2,1)}, u32[]{:S(2)}) copy-start(bf16[1,32,7168]{2,1,0:T(8,128)(2,1)} %param.8) | copy-start | bytes 1376260
  7.2 118.4 %all-gather.5.cloned.1.call-start = ((), (), s32[]{:S(2)}) async-start(), calls=%async_computation.1 | async-start | bytes 9748480 | tf_op jit(solution)/shard_map/all_gather | solution.py:261
  10.6 283.3 %all-gather.7.cloned.1.call-start = ((), (), s32[]{:S(2)}) async-start(), calls=%async_computation.2 | async-start | bytes 7798784 | tf_op jit(solution)/shard_map/all_gather | solution.py:273
  10.6 27.0 %collective-permute-start = (bf16[32,7168]{1,0:T(8,128)(2,1)S(1)}, bf16[32,7168]{1,0:T(8,128)(2,1)S(1)}, u32[]{:S(2)}, u32[]{:S(2)}) collective-permute-start(bf16[32,7168]{1,0:T(8,128)(2,1)S(1)} %bitcast.34), channel_id=1, source_target_pairs={{0,140},{1,141},{2,142},{3,143},{4,136},{5,137},{6,138},{7,139},{8... | collective-permute-start | bytes 1376264 | tf_op jit(solution)/shard_map/ppermute | solution.py:35
  37.7 21.2 %collective-permute-start.1 = (bf16[2,32,7168]{2,1,0:T(8,128)(2,1)S(1)}, bf16[2,32,7168]{2,1,0:T(8,128)(2,1)S(1)}, u32[]{:S(2)}, u32[]{:S(2)}) collective-permute-start(bf16[2,32,7168]{2,1,0:T(8,128)(2,1)S(1)} %pad_maximum_fusion), channel_id=1, source_target_pairs={{0,32},{1,33},{2,34},{3,35},{4,36},{5,37},{6,38},{7,39},{8,40},{9,... | collective-permute-start | bytes 2752520 | tf_op jit(solution)/shard_map/ppermute | solution.py:35
  39.0 41.8 %collective-permute-start.2 = (bf16[2,32,7168]{2,1,0:T(8,128)(2,1)S(1)}, bf16[2,32,7168]{2,1,0:T(8,128)(2,1)S(1)}, u32[]{:S(2)}, u32[]{:S(2)}) collective-permute-start(bf16[2,32,7168]{2,1,0:T(8,128)(2,1)S(1)} %pad_maximum_fusion), channel_id=1, source_target_pairs={{0,64},{1,65},{2,66},{3,67},{4,68},{5,69},{6,70},{7,71},{8,72},{9,... | collective-permute-start | bytes 2752520 | tf_op jit(solution)/shard_map/ppermute | solution.py:35
  41.5 41.4 %collective-permute-start.3 = (bf16[2,32,7168]{2,1,0:T(8,128)(2,1)S(1)}, bf16[2,32,7168]{2,1,0:T(8,128)(2,1)S(1)}, u32[]{:S(2)}, u32[]{:S(2)}) collective-permute-start(bf16[2,32,7168]{2,1,0:T(8,128)(2,1)S(1)} %pad_maximum_fusion), channel_id=1, source_target_pairs={{0,96},{1,97},{2,98},{3,99},{4,100},{5,101},{6,102},{7,103},{8,104... | collective-permute-start | bytes 2752520 | tf_op jit(solution)/shard_map/ppermute | solution.py:35
  83.9 12.6 %collective-permute-start.4 = (bf16[8,32,7168]{2,1,0:T(8,128)(2,1)}, bf16[8,32,7168]{2,1,0:T(8,128)(2,1)}, u32[]{:S(2)}, u32[]{:S(2)}) collective-permute-start(bf16[8,32,7168]{2,1,0:T(8,128)(2,1)} %constant_dynamic-update-slice_fusion.rows_ref), channel_id=1, source_target_pairs={{0,16},{1,17},{2,18},{3,19},{4,20},{5,21},{6,22},{7,23},{8,24},{9,... | collective-permute-start | bytes 11010056 | tf_op jit(solution)/shard_map/ppermute | solution.py:35
  145.6 3.8 %collective-permute-start.5 = (bf16[256,3072]{1,0:T(8,128)(2,1)}, bf16[256,3072]{1,0:T(8,128)(2,1)S(1)}, u32[]{:S(2)}, u32[]{:S(2)}) collective-permute-start(bf16[256,3072]{1,0:T(8,128)(2,1)} %get-tuple-element.16), channel_id=1, source_target_pairs={{0,16},{1,17},{2,18},{3,19},{4,20},{5,21},{6,22},{7,23},{8,24},{9,... | collective-permute-start | bytes 4718600 | tf_op jit(solution)/shard_map/ppermute | solution.py:35
  152.0 10.5 %collective-permute-start.6 = (bf16[2,32,3072]{2,1,0:T(8,128)(2,1)S(1)}, bf16[2,32,3072]{2,1,0:T(8,128)(2,1)S(1)}, u32[]{:S(2)}, u32[]{:S(2)}) collective-permute-start(bf16[2,32,3072]{2,1,0:T(8,128)(2,1)S(1)} %bitcast.41), channel_id=1, source_target_pairs={{0,32},{1,33},{2,34},{3,35},{4,36},{5,37},{6,38},{7,39},{8,40},{9,... | collective-permute-start | bytes 1179656 | tf_op jit(solution)/shard_map/ppermute | solution.py:35
  153.3 19.8 %collective-permute-start.7 = (bf16[2,32,3072]{2,1,0:T(8,128)(2,1)S(1)}, bf16[2,32,3072]{2,1,0:T(8,128)(2,1)S(1)}, u32[]{:S(2)}, u32[]{:S(2)}) collective-permute-start(bf16[2,32,3072]{2,1,0:T(8,128)(2,1)S(1)} %bitcast.40), channel_id=1, source_target_pairs={{0,64},{1,65},{2,66},{3,67},{4,68},{5,69},{6,70},{7,71},{8,72},{9,... | collective-permute-start | bytes 1179656 | tf_op jit(solution)/shard_map/ppermute | solution.py:35
  155.8 19.4 %collective-permute-start.8 = (bf16[2,32,3072]{2,1,0:T(8,128)(2,1)S(1)}, bf16[2,32,3072]{2,1,0:T(8,128)(2,1)S(1)}, u32[]{:S(2)}, u32[]{:S(2)}) collective-permute-start(bf16[2,32,3072]{2,1,0:T(8,128)(2,1)S(1)} %bitcast.39), channel_id=1, source_target_pairs={{0,96},{1,97},{2,98},{3,99},{4,100},{5,101},{6,102},{7,103},{8,104... | collective-permute-start | bytes 1179656 | tf_op jit(solution)/shard_map/ppermute | solution.py:35
  175.4 6.5 %collective-permute-start.9 = (bf16[32,3072]{1,0:T(8,128)(2,1)S(1)}, bf16[32,3072]{1,0:T(8,128)(2,1)S(1)}, u32[]{:S(2)}, u32[]{:S(2)}) collective-permute-start(bf16[32,3072]{1,0:T(8,128)(2,1)S(1)} %fusion.1), channel_id=1, source_target_pairs={{0,140},{1,141},{2,142},{3,143},{4,136},{5,137},{6,138},{7,139},{8... | collective-permute-start | bytes 589832 | tf_op jit(solution)/shard_map/ppermute | solution.py:35
  181.9 0.7 copy-start.4
  243.2 16.0 %collective-permute-start.10 = (bf16[16,32,192]{2,1,0:T(8,128)(2,1)S(1)}, bf16[16,32,192]{2,1,0:T(8,128)(2,1)S(1)}, u32[]{:S(2)}, u32[]{:S(2)}) collective-permute-start(bf16[16,32,192]{2,1,0:T(8,128)(2,1)S(1)} %all_to_all.5), channel_id=1, source_target_pairs={{0,128},{1,129},{2,130},{3,131},{4,132},{5,133},{6,134},{7,135},{8... | collective-permute-start | bytes 589832 | tf_op jit(solution)/shard_map/ppermute | solution.py:35
  259.4 12.9 %collective-permute-start.11 = (bf16[2,16,32,192]{3,2,1,0:T(8,128)(2,1)S(1)}, bf16[2,16,32,192]{3,2,1,0:T(8,128)(2,1)S(1)}, u32[]{:S(2)}, u32[]{:S(2)}) collective-permute-start(bf16[2,16,32,192]{3,2,1,0:T(8,128)(2,1)S(1)} %pad_maximum_fusion.2), channel_id=1, source_target_pairs={{0,32},{1,33},{2,34},{3,35},{4,36},{5,37},{6,38},{7,39},{8,40},{9,... | collective-permute-start | bytes 1179656 | tf_op jit(solution)/shard_map/ppermute | solution.py:35
  260.3 25.2 %collective-permute-start.12 = (bf16[2,16,32,192]{3,2,1,0:T(8,128)(2,1)S(1)}, bf16[2,16,32,192]{3,2,1,0:T(8,128)(2,1)S(1)}, u32[]{:S(2)}, u32[]{:S(2)}) collective-permute-start(bf16[2,16,32,192]{3,2,1,0:T(8,128)(2,1)S(1)} %pad_maximum_fusion.2), channel_id=1, source_target_pairs={{0,64},{1,65},{2,66},{3,67},{4,68},{5,69},{6,70},{7,71},{8,72},{9,... | collective-permute-start | bytes 1179656 | tf_op jit(solution)/shard_map/ppermute | solution.py:35
  263.0 24.7 %collective-permute-start.13 = (bf16[2,16,32,192]{3,2,1,0:T(8,128)(2,1)S(1)}, bf16[2,16,32,192]{3,2,1,0:T(8,128)(2,1)S(1)}, u32[]{:S(2)}, u32[]{:S(2)}) collective-permute-start(bf16[2,16,32,192]{3,2,1,0:T(8,128)(2,1)S(1)} %pad_maximum_fusion.2), channel_id=1, source_target_pairs={{0,96},{1,97},{2,98},{3,99},{4,100},{5,101},{6,102},{7,103},{8,104... | collective-permute-start | bytes 1179656 | tf_op jit(solution)/shard_map/ppermute | solution.py:35
  287.7 6.2 %copy-start.2 = (bf16[8,16,32,192]{3,2,1,0:T(8,128)(2,1)}, bf16[8,16,32,192]{3,2,1,0:T(8,128)(2,1)S(1)}, u32[]{:S(2)}) copy-start(bf16[8,16,32,192]{3,2,1,0:T(8,128)(2,1)S(1)} %constant_dynamic-update-slice_fusion.5) | copy-start | bytes 4718596
  287.7 6.2 %collective-permute-start.14 = (bf16[8,16,32,192]{3,2,1,0:T(8,128)(2,1)S(1)}, bf16[8,16,32,192]{3,2,1,0:T(8,128)(2,1)}, u32[]{:S(2)}, u32[]{:S(2)}) collective-permute-start(bf16[8,16,32,192]{3,2,1,0:T(8,128)(2,1)S(1)} %constant_dynamic-update-slice_fusion.5), channel_id=1, source_target_pairs={{0,16},{1,17},{2,18},{3,19},{4,20},{5,21},{6,22},{7,23},{8,24},{9,... | collective-permute-start | bytes 4718600 | tf_op jit(solution)/shard_map/ppermute | solution.py:35
  293.9 13.2 %copy-start.1 = (bf16[1,128,1536]{2,1,0:T(8,128)(2,1)S(1)}, bf16[1,128,1536]{2,1,0:T(8,128)(2,1)}, u32[]{:S(2)}) copy-start(bf16[1,128,1536]{2,1,0:T(8,128)(2,1)} %param.10) | copy-start | bytes 1179652
Sparse Core Ops, SparseCore 0:
  10.7 114.8 all-gather.4
  145.7 97.8 all-gather.6

commit v2 on v1

v2 whole, which is shorter than its diff:
```python
import jax
import jax.numpy as jnp
from jax import lax
from jax.experimental import pallas as pl
from jax.experimental.pallas import tpu as pltpu
from jax.sharding import PartitionSpec as P

HEAD_DIM = 48
IMG_TOK = 16
ACT = 16
AXES = ("dp", "fsdp")

eps = 1e-06
masked_value = -1e30
bf16 = jnp.bfloat16
f32 = jnp.float32
MIB = 1024 * 1024


def pairs(step):
    table = []
    for i in range(256):
        h, x, c, l, y = step(i >> 7, (i >> 5) & 3, (i >> 4) & 1, (i >> 2) & 3, i & 3)
        table.append((i, h << 7 | x << 5 | c << 4 | l << 2 | y))
    return table


CORE = pairs(lambda h, x, c, l, y: (h, x, c ^ 1, l, y))
MIRROR = pairs(lambda h, x, c, l, y: (h ^ 1, x, c, l ^ 3, y))
HALF = pairs(lambda h, x, c, l, y: (h ^ 1, x, c, l, y))
ALONG_X = [pairs(lambda h, x, c, l, y, e=e: (h, x ^ e, c, l, y)) for e in range(4)]
ALONG_Y = [pairs(lambda h, x, c, l, y, e=e: (h, x, c, l, y ^ e)) for e in range(4)]
ALONG_Z = [pairs(lambda h, x, c, l, y, e=e: (h, x, c, l ^ e, y)) for e in range(4)]


def send(array, table):
    return lax.ppermute(array, AXES, table)


def gather_along(own, tables):
    return jnp.stack([own] + [send(own, tables[e]) for e in (1, 2, 3)])


def params(mib):
    return pltpu.CompilerParams(vmem_limit_bytes=mib * MIB)


def norm_kernel(place_ref, rows_ref, normed_ref, resid_ref):
    widened = rows_ref[0].astype(f32)
    mean = jnp.mean(widened * widened, axis=-1, keepdims=True)
    normed = (widened * lax.rsqrt(mean + eps)).astype(bf16)
    blocks, _, depth = normed_ref.shape
    for f in range(blocks):
        normed_ref[f] = normed[:, f * depth : (f + 1) * depth]

        @pl.when(place_ref[0] == f)
        def _():
            resid_ref[...] = rows_ref[0, :, f * depth : (f + 1) * depth]


def normalize(rows, place):
    slots, height, width = rows.shape
    depth = width // 16
    return pl.pallas_call(
        norm_kernel,
        grid=(slots,),
        in_specs=[
            pl.BlockSpec(memory_space=pltpu.SMEM),
            pl.BlockSpec((1, height, width), lambda i: (i, 0, 0)),
        ],
        out_specs=[
            pl.BlockSpec((16, height, depth), lambda i: (0, i, 0)),
            pl.BlockSpec((height, depth), lambda i: (i, 0)),
        ],
        out_shape=[
            jax.ShapeDtypeStruct((16, slots * height, depth), bf16),
            jax.ShapeDtypeStruct((slots * height, depth), bf16),
        ],
        compiler_params=params(12),
        name="norm",
    )(place, rows)


def layer_kernel(*refs):
    normed_refs, resid_refs = refs[:4], refs[4:8]
    w_ref, feature_ref, featt_ref, kvw_ref, acc = refs[8:]
    step = pl.program_id(0)
    out = feature_ref.shape[1]
    total = None
    for k in range(w_ref.shape[0]):
        rows = jnp.concatenate([ref[k] for ref in normed_refs], axis=0)
        term = jnp.dot(rows, w_ref[k, :, :out], preferred_element_type=f32)
        total = term if total is None else total + term
    kvw_ref[0] = jnp.concatenate([w_ref[k, :, out:] for k in range(w_ref.shape[0])], axis=1)

    @pl.when(step == 0)
    def _():
        acc[...] = total

    @pl.when(step > 0)
    def _():
        acc[...] += total

    @pl.when(step == pl.num_programs(0) - 1)
    def _():
        pre = acc[...]
        resid = jnp.concatenate([ref[...] for ref in resid_refs], axis=0).astype(f32)
        feature = (resid + pre / (1.0 + jnp.exp(-pre))).astype(bf16)
        feature_ref[...] = feature
        featt_ref[...] = feature.T


def layer(normed, resid, weights):
    blocks, height, depth = normed[0].shape
    rows, out, wide, per = 4 * height, resid[0].shape[1], weights.shape[2], 4
    kv = (wide - out) * per

    def whole(shape):
        return pl.BlockSpec(shape, lambda k: (0, 0))

    return pl.pallas_call(
        layer_kernel,
        grid=(blocks // per,),
        in_specs=[pl.BlockSpec((per, height, depth), lambda k: (k, 0, 0))] * 4
        + [whole(resid[0].shape)] * 4
        + [pl.BlockSpec((per, depth, wide), lambda k: (k, 0, 0))],
        out_specs=[
            whole((rows, out)),
            whole((out, rows)),
            pl.BlockSpec((1, depth, kv), lambda k: (k, 0, 0)),
        ],
        out_shape=[
            jax.ShapeDtypeStruct((rows, out), bf16),
            jax.ShapeDtypeStruct((out, rows), bf16),
            jax.ShapeDtypeStruct((blocks // per, depth, kv), bf16),
        ],
        scratch_shapes=[pltpu.VMEM((rows, out), f32)],
        compiler_params=params(56),
        name="layer",
    )(*normed, *resid, weights)


def project_kernel(feature_ref, w_ref, out_ref):
    out_ref[...] = jnp.dot(feature_ref[...], w_ref[0], preferred_element_type=f32).astype(
        out_ref.dtype
    )


def project(feature, half, weights, dtype):
    rows, depth = feature.shape[0] // 2, feature.shape[1]
    blocks, _, kv = weights.shape
    return pl.pallas_call(
        project_kernel,
        grid=(blocks,),
        in_specs=[
            pl.BlockSpec((rows, depth), lambda i: (half, 0)),
            pl.BlockSpec((1, depth, kv), lambda i: (i, 0, 0)),
        ],
        out_specs=pl.BlockSpec((rows, kv), lambda i: (0, i)),
        out_shape=jax.ShapeDtypeStruct((rows, blocks * kv), dtype),
        compiler_params=params(16),
        name="project",
    )(feature, weights)


def attention_kernel(
    place_ref, images_ref, lengths_ref, own_ref, other_ref, q_ref, cg_ref, context_ref, grads_ref
):
    key_rows, width = own_ref.shape
    width_act = width // 2
    qrows = q_ref.shape[0]
    heads = 8
    cols = heads * HEAD_DIM
    scale = HEAD_DIM ** (-0.5)
    piece = width // 16
    y = place_ref[2]
    last = (((1,), (1,)), ((), ()))
    first = (((0,), (0,)), ((), ()))
    kv = (own_ref[...] + other_ref[...].astype(f32)).astype(bf16)
    row_head = lax.broadcasted_iota(jnp.int32, (heads * key_rows, cols), 0) // key_rows
    col_head = lax.broadcasted_iota(jnp.int32, (heads * key_rows, cols), 1) // HEAD_DIM
    same = row_head == col_head
    key_live = (
        lax.broadcasted_iota(jnp.int32, (heads, key_rows, qrows), 1) < images_ref[0] * IMG_TOK
    )
    query_live = lax.broadcasted_iota(jnp.int32, (qrows, cols), 0) % ACT < lengths_ref[0]

    def by_head(flat):
        return flat.reshape(heads, key_rows, qrows)

    def spread(rows):
        return jnp.where(same, jnp.concatenate([rows] * heads, axis=0), jnp.zeros((), bf16))

    def collapse(big):
        return jnp.sum(jnp.where(same, big, 0.0).reshape(heads, key_rows, cols), axis=0)

    for g in range(width_act // cols):
        at = slice(g * cols, (g + 1) * cols)
        keys = spread(kv[:, g * cols : (g + 1) * cols])
        values = spread(kv[:, width_act + g * cols : width_act + (g + 1) * cols])
        queries = q_ref[:, at]
        grad_in = jnp.where(query_live, cg_ref[:, at], jnp.zeros((), bf16))
        scores = by_head(lax.dot_general(keys, queries, last, preferred_element_type=f32) * scale)
        scores = jnp.where(key_live, scores, masked_value)
        exponent = jnp.exp(scores - jnp.max(scores, axis=1, keepdims=True))
        probs = exponent / jnp.sum(exponent, axis=1, keepdims=True)
        probs_low = probs.astype(bf16).reshape(heads * key_rows, qrows)
        mixed = lax.dot_general(probs_low, values, first, preferred_element_type=f32)
        context_ref[:, at] = jnp.where(query_live, mixed, 0.0).astype(bf16)
        prob_grad = by_head(lax.dot_general(values, grad_in, last, preferred_element_type=f32))
        centre = jnp.sum(prob_grad * probs, axis=1, keepdims=True)
        score_grad = (probs * (prob_grad - centre)).astype(bf16).reshape(heads * key_rows, qrows)
        value_grad = collapse(jnp.dot(probs_low, grad_in, preferred_element_type=f32)).astype(bf16)
        key_grad = jnp.dot(score_grad, queries, preferred_element_type=f32)
        key_grad = (collapse(key_grad) * scale).astype(bf16)
        per = cols // piece
        for start, grad in ((g * per, key_grad), (width_act // piece + g * per, value_grad)):
            for j in range(per):
                f = start + j
                column = f // 4 * piece
                grads_ref[(f % 4) ^ y, :, column : column + piece] = grad[
                    :, j * piece : (j + 1) * piece
                ]


def attention(own, other, queries, images, lengths, context_grad, place):
    key_rows, width = own.shape
    smem, vmem = pl.BlockSpec(memory_space=pltpu.SMEM), pl.BlockSpec(memory_space=pltpu.VMEM)
    return pl.pallas_call(
        attention_kernel,
        in_specs=[smem, smem, smem, vmem, vmem, vmem, vmem],
        out_specs=[vmem, vmem],
        out_shape=[
            jax.ShapeDtypeStruct(queries.shape, bf16),
            jax.ShapeDtypeStruct((4, key_rows, width // 4), bf16),
        ],
        compiler_params=params(24),
        name="attention",
    )(place, images, lengths, own, other, queries, context_grad)


def weight_grad_kernel(place_ref, a_ref, b_ref, featt_ref, own_ref, sends_ref, acc):
    step = pl.program_id(0)
    l, y = place_ref[1], place_ref[2]
    wide = acc.shape[1]
    packed = [ref[:, m, 0] for ref in (a_ref, b_ref) for m in range(2)]
    grads = jnp.concatenate(packed, axis=0).reshape(-1, wide)
    term = jnp.dot(featt_ref[0], grads, preferred_element_type=f32)

    @pl.when(step == 0)
    def _():
        acc[...] = term

    @pl.when(step > 0)
    def _():
        acc[...] += term

    @pl.when(step == pl.num_programs(0) - 1)
    def _():
        total = acc[...].T
        kv = wide // 4
        for fl in range(4):
            block = total[fl * kv : (fl + 1) * kv]
            sends_ref[fl ^ l] = block.astype(bf16)

            @pl.when(l == fl)
            def _():
                own_ref[...] = block


def weight_grad(grads_a, grads_b, featt, place):
    blocks, out, rows = featt.shape
    key_rows, wide = grads_a.shape[-2:]
    kv = wide // 4
    near = pl.BlockSpec((4, 2, 1, key_rows, wide), lambda i, place: (0, 0, i ^ place[2], 0, 0))
    return pl.pallas_call(
        weight_grad_kernel,
        grid_spec=pltpu.PrefetchScalarGridSpec(
            num_scalar_prefetch=1,
            grid=(blocks,),
            in_specs=[
                near,
                near,
                pl.BlockSpec((1, out, rows), lambda i, place: (i, 0, 0)),
            ],
            out_specs=[
                pl.BlockSpec((kv, out), lambda i, place: (0, 0)),
                pl.BlockSpec((4, kv, out), lambda i, place: (0, 0, 0)),
            ],
            scratch_shapes=[pltpu.VMEM((out, wide), f32)],
        ),
        out_shape=[
            jax.ShapeDtypeStruct((kv, out), f32),
            jax.ShapeDtypeStruct((4, kv, out), bf16),
        ],
        compiler_params=params(16),
        name="weight_grad",
    )(place, grads_a, grads_b, featt)


Y_GROUPS = [[l * 4 + y for y in range(4)] for l in range(4)]


def on_device(
    vlm_rows, images, action_hidden, lengths, vlm_weight, kv_weight, query_weight, context_grad
):
    _, slot_rows, width = vlm_rows.shape
    width_act = query_weight.shape[0]
    dp, fsdp = lax.axis_index("dp"), lax.axis_index("fsdp")
    place = jnp.stack([dp, fsdp // 4, fsdp % 4]).astype(jnp.int32)

    weights = lax.all_gather(
        jnp.concatenate([vlm_weight.T, kv_weight.T], axis=1), "fsdp", axis=0, tiled=False
    )
    mirrored = send(vlm_rows[0], MIRROR)
    own_a = gather_along(vlm_rows[0], ALONG_X)
    mirrored, own_a = lax.optimization_barrier((mirrored, own_a))
    far_a = gather_along(mirrored, ALONG_X)
    own_b = send(own_a, CORE)
    normed, resid = zip(normalize(own_a, place), normalize(own_b, place))
    far_a, normed, resid = lax.optimization_barrier((far_a, normed, resid))
    far_b = send(far_a, CORE)
    more, rest = zip(normalize(far_a, place), normalize(far_b, place))
    normed = (normed[0], more[0], normed[1], more[1])
    resid = (resid[0], rest[0], resid[1], rest[1])
    queries = lax.dot_general(
        action_hidden[0], query_weight, (((1,), (1,)), ((), ())), preferred_element_type=f32
    ).astype(bf16)
    queries, normed = lax.optimization_barrier((queries, normed))
    feature, featt, kv_weights = layer(normed, resid, weights)
    featt_all = lax.all_gather(
        featt, "fsdp", axis=0, tiled=False, axis_index_groups=Y_GROUPS
    )

    part_b = project(feature, 1, kv_weights, bf16)
    swapped = send(part_b, CORE)
    part_a = project(feature, 0, kv_weights, f32)
    both = (part_a + swapped.astype(f32)).reshape(2, 4, slot_rows, 2 * width_act)
    mine = both[:, 0]
    for e in (1, 2, 3):
        mine = mine + send(both[:, e].astype(bf16), ALONG_X[e]).astype(f32)
    other = send(mine[1].astype(bf16), MIRROR)

    context, grads = attention(
        mine[0], other, queries, images, lengths, context_grad[0], place
    )

    by_y = jnp.stack([grads[0]] + [send(grads[e], ALONG_Y[e]) for e in (1, 2, 3)])
    grads_a = gather_along(jnp.stack([by_y, send(by_y, MIRROR)]), ALONG_X)
    grads_b = send(grads_a, CORE)
    kv_weight_grad, sums = weight_grad(grads_a, grads_b, featt_all, place)
    for e in (1, 2, 3):
        kv_weight_grad = kv_weight_grad + send(sums[e], ALONG_Z[e]).astype(f32)
    return (context[None], kv_weight_grad)


def solution(mesh):
    in_specs = (
        P(("dp", "fsdp"), None, None),
        P(("dp", "fsdp")),
        P(("dp", "fsdp"), None, None),
        P(("dp", "fsdp")),
        P("dp", "fsdp"),
        P("fsdp", "dp"),
        P(),
        P(("dp", "fsdp"), None, None),
    )
    out_specs = (P(("dp", "fsdp"), None, None), P("fsdp", "dp"))
    return jax.shard_map(
        on_device, mesh=mesh, in_specs=in_specs, out_specs=out_specs, check_vma=False
    )
```

time: 315 us -> 265 us (0.84)
  the two profiles are of different devices: /device:TPU:1 before, /device:TPU:32 now
where the time goes in v2:
time: 265 us; the launch traced here: 264 us
  waiting for transfers between devices  141 us (53%)
  starting transfers between devices  44.7 us (17%)
  Pallas kernels  39.4 us (15%)
  local copies, waits for them, and re-layouts  16.5 us (6%)
  between operations  15.6 us (6%)
  other arithmetic  5.79 us (2%)
    ppermute x25, waiting for transfers between devices, send(): return lax.ppermute(array, AXES, table)  99.2 us
    ppermute x25, starting transfers between devices, send(): return lax.ppermute(array, AXES, table)  44.6 us
    all_gather x1, waiting for transfers between devices, on_device(): lax.all_gather(jnp.concatenate([vlm_weight.T, kv_weight.T], axis=1), 'fsd...  41.4 us
    pallas_call x4, Pallas kernels, normalize(): pl.pallas_call(norm_kernel, grid=(slots,), in_specs=[pl.BlockSpec(memory_...  17.8 us
    unnamed x34, local copies, waits for them, and re-layouts  16.2 us
    pallas_call x1, Pallas kernels, layer(): pl.pallas_call(layer_kernel, grid=(blocks // per,), in_specs=[pl.BlockSpe...  11.1 us
  transfers between devices with their start and end apart: 27, of which 22 were waited for; matrix products, arithmetic and copies ran while one was open for 2% of the time, Pallas kernels for 9%

profile of v2, /device:TPU:32, one launch (start us, length us, event | category | flops | bytes accessed | tf_op | source)
XLA Modules:
  0.0 264.3 jit_solution(13619678196474553867)
XLA Ops:
  10.6 1.6 collective-permute-start.1
  12.2 2.7 %collective-permute-start.2 = (bf16[32,7168]{1,0:T(8,128)(2,1)S(1)}, bf16[32,7168]{1,0:T(8,128)(2,1)S(1)}, u32[]{:S(2)}, u32[]{:S(2)}) collective-permute-start(bf16[32,7168]{1,0:T(8,128)(2,1)S(1)} %bitcast.71), channel_id=1, source_target_pairs={{0,64},{1,65},{2,66},{3,67},{4,68},{5,69},{6,70},{7,71},{8,72},{9,... | collective-permute-start | bytes 1376264 | tf_op jit(solution)/shard_map/ppermute | solution.py:37
  15.4 5.8 %collective-permute-start = (bf16[32,7168]{1,0:T(8,128)(2,1)S(1)}, bf16[32,7168]{1,0:T(8,128)(2,1)S(1)}, u32[]{:S(2)}, u32[]{:S(2)}) collective-permute-start(bf16[32,7168]{1,0:T(8,128)(2,1)S(1)} %bitcast.73), channel_id=1, source_target_pairs={{0,140},{1,141},{2,142},{3,143},{4,136},{5,137},{6,138},{7,139},{8... | collective-permute-start | bytes 1376264 | tf_op jit(solution)/shard_map/ppermute | solution.py:37
  21.3 2.9 %collective-permute-done.1 = bf16[32,7168]{1,0:T(8,128)(2,1)S(1)} collective-permute-done((bf16[32,7168]{1,0:T(8,128)(2,1)S(1)}, bf16[32,7168]{1,0:T(8,128)(2,1)S(1)}, u32[]{:S(2)}, u32[]{:S(2)}) %collective-permute-start.1) | collective-permute-done | bytes 458784 | tf_op jit(solution)/shard_map/ppermute | solution.py:37
  24.1 11.0 %collective-permute-done.2 = bf16[32,7168]{1,0:T(8,128)(2,1)S(1)} collective-permute-done((bf16[32,7168]{1,0:T(8,128)(2,1)S(1)}, bf16[32,7168]{1,0:T(8,128)(2,1)S(1)}, u32[]{:S(2)}, u32[]{:S(2)}) %collective-permute-start.2) | collective-permute-done | bytes 458784 | tf_op jit(solution)/shard_map/ppermute | solution.py:37
  35.1 2.6 collective-permute-done.3
  38.6 2.2 collective-permute-start.6
  41.7 4.2 %norm.4 = (bf16[16,128,448]{2,1,0:T(8,128)(2,1)S(1)}, bf16[128,448]{1,0:T(8,128)(2,1)S(1)}) custom-call(s32[3]{0:T(128)S(1)} %pad_add_fusion.place_ref, bf16[4,32,7168]{2,1,0:T(8,128)(2,1)S(1)} %pad_maximum_fusion.rows_ref), custom_call_target="tpu_custom_call" | custom-call | tf_op jit(solution)/shard_map/norm/pallas_call | solution.py:64
  46.0 1.3 copy-done.2
  47.9 5.1 %collective-permute-done.5 = bf16[32,7168]{1,0:T(8,128)(2,1)S(1)} collective-permute-done((bf16[32,7168]{1,0:T(8,128)(2,1)S(1)}, bf16[32,7168]{1,0:T(8,128)(2,1)S(1)}, u32[]{:S(2)}, u32[]{:S(2)}) %collective-permute-start.5) | collective-permute-done | bytes 458784 | tf_op jit(solution)/shard_map/ppermute | solution.py:37
  53.0 9.4 %collective-permute-done.6 = bf16[32,7168]{1,0:T(8,128)(2,1)} collective-permute-done((bf16[32,7168]{1,0:T(8,128)(2,1)S(1)}, bf16[32,7168]{1,0:T(8,128)(2,1)}, u32[]{:S(2)}, u32[]{:S(2)}) %collective-permute-start.6) | collective-permute-done | bytes 458784 | tf_op jit(solution)/shard_map/ppermute | solution.py:37
  62.5 1.5 pad_maximum_fusion.1.rows_ref
  64.1 5.0 %norm.5 = (bf16[16,128,448]{2,1,0:T(8,128)(2,1)S(1)}, bf16[128,448]{1,0:T(8,128)(2,1)S(1)}) custom-call(s32[3]{0:T(128)S(1)} %pad_add_fusion.place_ref, bf16[4,32,7168]{2,1,0:T(8,128)(2,1)} %collective-permute-done.7.rows_ref), custom_call_target="tpu_custom_call" | custom-call | tf_op jit(solution)/shard_map/norm/pallas_call | solution.py:64
  69.1 1.3 copy-done.3
  71.2 1.6 convolution_convert_fusion.q_ref
  72.8 4.3 %norm.6 = (bf16[16,128,448]{2,1,0:T(8,128)(2,1)S(1)}, bf16[128,448]{1,0:T(8,128)(2,1)S(1)}) custom-call(s32[3]{0:T(128)S(1)} %pad_add_fusion.place_ref, bf16[4,32,7168]{2,1,0:T(8,128)(2,1)S(1)} %pad_maximum_fusion.1.rows_ref), custom_call_target="tpu_custom_call" | custom-call | tf_op jit(solution)/shard_map/norm/pallas_call | solution.py:64
  79.0 4.2 %norm.7 = (bf16[16,128,448]{2,1,0:T(8,128)(2,1)S(1)}, bf16[128,448]{1,0:T(8,128)(2,1)S(1)}) custom-call(s32[3]{0:T(128)S(1)} %pad_add_fusion.place_ref, bf16[4,32,7168]{2,1,0:T(8,128)(2,1)S(1)} %collective-permute-done.8.rows_ref), custom_call_target="tpu_custom_call" | custom-call | tf_op jit(solution)/shard_map/norm/pallas_call | solution.py:64
  83.3 1.3 copy-done.5
  85.3 41.4 %all-gather.5.cloned.1.call-done = bf16[7168,640]{1,0:T(8,128)(2,1)} async-done(((bf16[448,640]{1,0:T(8,128)(2,1)}), bf16[7168,640]{1,0:T(8,128)(2,1)}) %all-gather.5.cloned.1.call-update) | async-done | bytes 9175056 | tf_op jit(solution)/shard_map/all_gather | solution.py:312
  126.6 11.1 %layer.1 = (bf16[512,448]{1,0:T(8,128)(2,1)}, bf16[448,512]{1,0:T(8,128)(2,1)}, bf16[4,448,768]{2,1,0:T(8,128)(2,1)}) custom-call(bf16[16,128,448]{2,1,0:T(8,128)(2,1)} %copy-done.2, bf16[16,128,448]{2,1,0:T(8,128)(2,1)} %copy-done.4, bf16[16,128,448]{2,1,0:T(8,128)(2,1)} %copy-done.3, bf16[16,128,448]{2,1,0:T(8,128)(2,1)} %copy-done.5, ...), custom_call_target="tpu_custom_call" | custom-call | tf_op jit(solution)/shard_map/layer/pallas_call | solution.py:121
  137.7 1.8 copy-done.1
  140.6 1.6 project.3
  142.5 1.7 project.2
  144.1 1.7 collective-permute-done.9
  146.4 1.6 copy-done.13
  148.5 3.9 %collective-permute-start.11 = (bf16[2,32,3072]{2,1,0:T(8,128)(2,1)S(1)}, bf16[2,32,3072]{2,1,0:T(8,128)(2,1)S(1)}, u32[]{:S(2)}, u32[]{:S(2)}) collective-permute-start(bf16[2,32,3072]{2,1,0:T(8,128)(2,1)S(1)} %get-tuple-element.58), channel_id=1, source_target_pairs={{0,64},{1,65},{2,66},{3,67},{4,68},{5,69},{6,70},{7,71},{8,72},{9,... | collective-permute-start | bytes 1179656 | tf_op jit(solution)/shard_map/ppermute | solution.py:37
  154.3 5.9 %collective-permute-done.10 = bf16[2,32,3072]{2,1,0:T(8,128)(2,1)S(1)} collective-permute-done((bf16[2,32,3072]{2,1,0:T(8,128)(2,1)S(1)}, bf16[2,32,3072]{2,1,0:T(8,128)(2,1)S(1)}, u32[]{:S(2)}, u32[]{:S(2)}) %collective-permute-start.10) | collective-permute-done | bytes 393248 | tf_op jit(solution)/shard_map/ppermute | solution.py:37
  160.2 9.9 %collective-permute-done.11 = bf16[2,32,3072]{2,1,0:T(8,128)(2,1)S(1)} collective-permute-done((bf16[2,32,3072]{2,1,0:T(8,128)(2,1)S(1)}, bf16[2,32,3072]{2,1,0:T(8,128)(2,1)S(1)}, u32[]{:S(2)}, u32[]{:S(2)}) %collective-permute-start.11) | collective-permute-done | bytes 393248 | tf_op jit(solution)/shard_map/ppermute | solution.py:37
  170.1 2.6 collective-permute-done.12
  172.7 1.3 fusion.2
  174.2 8.7 %collective-permute-done.13.other_ref = bf16[32,3072]{1,0:T(8,128)(2,1)S(1)} collective-permute-done((bf16[32,3072]{1,0:T(8,128)(2,1)S(1)}, bf16[32,3072]{1,0:T(8,128)(2,1)S(1)}, u32[]{:S(2)}, u32[]{:S(2)}) %collective-permute-start.13) | collective-permute-done | bytes 196640 | tf_op jit(solution)/shard_map/ppermute | solution.py:37
  182.9 3.4 %attention.1 = (bf16[128,1536]{1,0:T(8,128)(2,1)}, bf16[4,32,768]{2,1,0:T(8,128)(2,1)S(1)}) custom-call(s32[3]{0:T(128)S(1)} %pad_add_fusion.place_ref, s32[1]{0:T(128)S(6)} %copy.24.images_ref, s32[1]{0:T(128)S(6)} %copy.25.lengths_ref, f32[32,3072]{1,0:T(8,128)S(1)} %slice_bitcast_fusion.1.own_ref, bf16[32,3072]{1,0:T(8,128)(2,1)S(1)} %collective-permute-done.13.other_ref, ...), custom_call_target="tpu_custom_call" | custom-call | tf_op jit(solution)/shard_map/attention/pallas_call | solution.py:229
  186.3 1.6 collective-permute-start.15
  187.9 3.1 %collective-permute-start.16 = (bf16[32,768]{1,0:T(8,128)(2,1)S(1)}, bf16[32,768]{1,0:T(8,128)(2,1)S(1)}, u32[]{:S(2)}, u32[]{:S(2)}) collective-permute-start(bf16[32,768]{1,0:T(8,128)(2,1)S(1)} %get-tuple-element.67), channel_id=1, source_target_pairs={{0,3},{1,2},{2,1},{3,0},{4,7},{5,6},{6,5},{7,4},{8,11},{9,10},{10,... | collective-permute-start | bytes 147464 | tf_op jit(solution)/shard_map/ppermute | solution.py:37
  193.3 4.9 %collective-permute-start.17 = (bf16[4,32,768]{2,1,0:T(8,128)(2,1)S(1)}, bf16[4,32,768]{2,1,0:T(8,128)(2,1)S(1)}, u32[]{:S(2)}, u32[]{:S(2)}) collective-permute-start(bf16[4,32,768]{2,1,0:T(8,128)(2,1)S(1)} %get-tuple-element.65), channel_id=1, source_target_pairs={{0,140},{1,141},{2,142},{3,143},{4,136},{5,137},{6,138},{7,139},{8... | collective-permute-start | bytes 589832 | tf_op jit(solution)/shard_map/ppermute | solution.py:37
  198.2 4.0 %collective-permute-done.17 = bf16[4,32,768]{2,1,0:T(8,128)(2,1)S(1)} collective-permute-done((bf16[4,32,768]{2,1,0:T(8,128)(2,1)S(1)}, bf16[4,32,768]{2,1,0:T(8,128)(2,1)S(1)}, u32[]{:S(2)}, u32[]{:S(2)}) %collective-permute-start.17) | collective-permute-done | bytes 196640 | tf_op jit(solution)/shard_map/ppermute | solution.py:37
  202.3 1.8 collective-permute-start.19
  204.1 2.9 %collective-permute-start.20 = (bf16[2,4,32,768]{3,2,1,0:T(8,128)(2,1)S(1)}, bf16[2,4,32,768]{3,2,1,0:T(8,128)(2,1)S(1)}, u32[]{:S(2)}, u32[]{:S(2)}) collective-permute-start(bf16[2,4,32,768]{3,2,1,0:T(8,128)(2,1)S(1)} %get-tuple-element.63), channel_id=1, source_target_pairs={{0,96},{1,97},{2,98},{3,99},{4,100},{5,101},{6,102},{7,103},{8,104... | collective-permute-start | bytes 1179656 | tf_op jit(solution)/shard_map/ppermute | solution.py:37
  207.0 5.6 %collective-permute-done.18 = bf16[2,4,32,768]{3,2,1,0:T(8,128)(2,1)S(1)} collective-permute-done((bf16[2,4,32,768]{3,2,1,0:T(8,128)(2,1)S(1)}, bf16[2,4,32,768]{3,2,1,0:T(8,128)(2,1)S(1)}, u32[]{:S(2)}, u32[]{:S(2)}) %collective-permute-start.18) | collective-permute-done | bytes 393248 | tf_op jit(solution)/shard_map/ppermute | solution.py:37
  212.6 4.0 %collective-permute-done.19 = bf16[2,4,32,768]{3,2,1,0:T(8,128)(2,1)S(1)} collective-permute-done((bf16[2,4,32,768]{3,2,1,0:T(8,128)(2,1)S(1)}, bf16[2,4,32,768]{3,2,1,0:T(8,128)(2,1)S(1)}, u32[]{:S(2)}, u32[]{:S(2)}) %collective-permute-start.19) | collective-permute-done | bytes 393248 | tf_op jit(solution)/shard_map/ppermute | solution.py:37
  216.7 2.5 collective-permute-done.20
  219.5 3.4 %collective-permute-done.21.b_ref = bf16[4,2,4,32,768]{4,3,2,1,0:T(8,128)(2,1)S(1)} collective-permute-done((bf16[4,2,4,32,768]{4,3,2,1,0:T(8,128)(2,1)S(1)}, bf16[4,2,4,32,768]{4,3,2,1,0:T(8,128)(2,1)S(1)}, u32[]{:S(2)}, u32[]{:S(2)}) %collective-permute-start.21) | collective-permute-done | bytes 1572896 | tf_op jit(solution)/shard_map/ppermute | solution.py:37
  222.9 1.5 copy-done.7
  224.4 4.0 %weight_grad.1 = (f32[192,448]{1,0:T(8,128)S(1)}, bf16[4,192,448]{2,1,0:T(8,128)(2,1)S(1)}) custom-call(s32[3]{0:T(128)S(1)} %pad_add_fusion.place_ref, bf16[4,2,4,32,768]{4,3,2,1,0:T(8,128)(2,1)S(1)} %pad_maximum_fusion.2.a_ref, bf16[4,2,4,32,768]{4,3,2,1,0:T(8,128)(2,1)S(1)} %collective-permute-done.21.b_ref, bf16[4,448,512]{2,1,0:T(8,128)(2,1)S(1)} %bitcast.63), custom_call_target="tpu_custom_call" | custom-call | tf_op jit(solution)/shard_map/weight_grad/pallas_call | solution.py:276
  228.4 9.0 %collective-permute-start.22 = (bf16[192,448]{1,0:T(8,128)(2,1)S(1)}, bf16[192,448]{1,0:T(8,128)(2,1)S(1)}, u32[]{:S(2)}, u32[]{:S(2)}) collective-permute-start(bf16[192,448]{1,0:T(8,128)(2,1)S(1)} %get-tuple-element.59), channel_id=1, source_target_pairs={{0,4},{1,5},{2,6},{3,7},{4,0},{5,1},{6,2},{7,3},{8,12},{9,13},{10,... | collective-permute-start | bytes 516104 | tf_op jit(solution)/shard_map/ppermute | solution.py:37
  239.0 6.6 %collective-permute-done.22 = bf16[192,448]{1,0:T(8,128)(2,1)S(1)} collective-permute-done((bf16[192,448]{1,0:T(8,128)(2,1)S(1)}, bf16[192,448]{1,0:T(8,128)(2,1)S(1)}, u32[]{:S(2)}, u32[]{:S(2)}) %collective-permute-start.22) | collective-permute-done | bytes 172064 | tf_op jit(solution)/shard_map/ppermute | solution.py:37
  245.5 6.6 %collective-permute-done.23 = bf16[192,448]{1,0:T(8,128)(2,1)S(1)} collective-permute-done((bf16[192,448]{1,0:T(8,128)(2,1)S(1)}, bf16[192,448]{1,0:T(8,128)(2,1)S(1)}, u32[]{:S(2)}, u32[]{:S(2)}) %collective-permute-start.23) | collective-permute-done | bytes 172064 | tf_op jit(solution)/shard_map/ppermute | solution.py:37
  252.2 4.4 %collective-permute-done.24 = bf16[192,448]{1,0:T(8,128)(2,1)S(1)} collective-permute-done((bf16[192,448]{1,0:T(8,128)(2,1)S(1)}, bf16[192,448]{1,0:T(8,128)(2,1)S(1)}, u32[]{:S(2)}, u32[]{:S(2)}) %collective-permute-start.24) | collective-permute-done | bytes 172064 | tf_op jit(solution)/shard_map/ppermute | solution.py:37
  (67 shorter events, 18.2 us)
Async XLA Ops:
  7.2 64.0 %copy-start = (bf16[1,128,1536]{2,1,0:T(8,128)(2,1)S(1)}, bf16[1,128,1536]{2,1,0:T(8,128)(2,1)}, u32[]{:S(2)}) copy-start(bf16[1,128,1536]{2,1,0:T(8,128)(2,1)} %param.10) | copy-start | bytes 1179652
  7.2 3.5 %copy-start.15 = (bf16[1,32,7168]{2,1,0:T(8,128)(2,1)S(1)}, bf16[1,32,7168]{2,1,0:T(8,128)(2,1)}, u32[]{:S(2)}) copy-start(bf16[1,32,7168]{2,1,0:T(8,128)(2,1)} %param.8) | copy-start | bytes 1376260
  7.2 119.4 %all-gather.5.cloned.1.call-start = ((), (), s32[]{:S(2)}) async-start(), calls=%async_computation | async-start | bytes 9748480 | tf_op jit(solution)/shard_map/all_gather | solution.py:312
  10.6 209.0 %all-gather.7.cloned.1.call-start = ((), (), s32[]{:S(2)}) async-start(), calls=%async_computation.1 | async-start | bytes 2293760 | tf_op jit(solution)/shard_map/all_gather | solution.py:331
  10.6 13.5 %collective-permute-start.1 = (bf16[32,7168]{1,0:T(8,128)(2,1)S(1)}, bf16[32,7168]{1,0:T(8,128)(2,1)S(1)}, u32[]{:S(2)}, u32[]{:S(2)}) collective-permute-start(bf16[32,7168]{1,0:T(8,128)(2,1)S(1)} %bitcast.70), channel_id=1, source_target_pairs={{0,32},{1,33},{2,34},{3,35},{4,36},{5,37},{6,38},{7,39},{8,40},{9,... | collective-permute-start | bytes 1376264 | tf_op jit(solution)/shard_map/ppermute | solution.py:37
  12.2 22.9 %collective-permute-start.2 = (bf16[32,7168]{1,0:T(8,128)(2,1)S(1)}, bf16[32,7168]{1,0:T(8,128)(2,1)S(1)}, u32[]{:S(2)}, u32[]{:S(2)}) collective-permute-start(bf16[32,7168]{1,0:T(8,128)(2,1)S(1)} %bitcast.71), channel_id=1, source_target_pairs={{0,64},{1,65},{2,66},{3,67},{4,68},{5,69},{6,70},{7,71},{8,72},{9,... | collective-permute-start | bytes 1376264 | tf_op jit(solution)/shard_map/ppermute | solution.py:37
  14.9 22.7 %collective-permute-start.3 = (bf16[32,7168]{1,0:T(8,128)(2,1)S(1)}, bf16[32,7168]{1,0:T(8,128)(2,1)S(1)}, u32[]{:S(2)}, u32[]{:S(2)}) collective-permute-start(bf16[32,7168]{1,0:T(8,128)(2,1)S(1)} %bitcast.72), channel_id=1, source_target_pairs={{0,96},{1,97},{2,98},{3,99},{4,100},{5,101},{6,102},{7,103},{8,104... | collective-permute-start | bytes 1376264 | tf_op jit(solution)/shard_map/ppermute | solution.py:37
  15.4 22.5 %collective-permute-start = (bf16[32,7168]{1,0:T(8,128)(2,1)S(1)}, bf16[32,7168]{1,0:T(8,128)(2,1)S(1)}, u32[]{:S(2)}, u32[]{:S(2)}) collective-permute-start(bf16[32,7168]{1,0:T(8,128)(2,1)S(1)} %bitcast.73), channel_id=1, source_target_pairs={{0,140},{1,141},{2,142},{3,143},{4,136},{5,137},{6,138},{7,139},{8... | collective-permute-start | bytes 1376264 | tf_op jit(solution)/shard_map/ppermute | solution.py:37
  37.9 26.1 %collective-permute-start.7 = (bf16[4,32,7168]{2,1,0:T(8,128)(2,1)S(1)}, bf16[4,32,7168]{2,1,0:T(8,128)(2,1)}, u32[]{:S(2)}, u32[]{:S(2)}) collective-permute-start(bf16[4,32,7168]{2,1,0:T(8,128)(2,1)S(1)} %pad_maximum_fusion.rows_ref), channel_id=1, source_target_pairs={{0,16},{1,17},{2,18},{3,19},{4,20},{5,21},{6,22},{7,23},{8,24},{9,... | collective-permute-start | bytes 5505032 | tf_op jit(solution)/shard_map/ppermute | solution.py:37
  38.0 15.0 %collective-permute-start.5 = (bf16[32,7168]{1,0:T(8,128)(2,1)S(1)}, bf16[32,7168]{1,0:T(8,128)(2,1)S(1)}, u32[]{:S(2)}, u32[]{:S(2)}) collective-permute-start(bf16[32,7168]{1,0:T(8,128)(2,1)S(1)} %collective-permute-done), channel_id=1, source_target_pairs={{0,64},{1,65},{2,66},{3,67},{4,68},{5,69},{6,70},{7,71},{8,72},{9,... | collective-permute-start | bytes 1376264 | tf_op jit(solution)/shard_map/ppermute | solution.py:37
  38.6 23.8 %collective-permute-start.6 = (bf16[32,7168]{1,0:T(8,128)(2,1)S(1)}, bf16[32,7168]{1,0:T(8,128)(2,1)}, u32[]{:S(2)}, u32[]{:S(2)}) collective-permute-start(bf16[32,7168]{1,0:T(8,128)(2,1)S(1)} %collective-permute-done), channel_id=1, source_target_pairs={{0,96},{1,97},{2,98},{3,99},{4,100},{5,101},{6,102},{7,103},{8,104... | collective-permute-start | bytes 1376264 | tf_op jit(solution)/shard_map/ppermute | solution.py:37
  40.8 21.7 %collective-permute-start.4 = (bf16[32,7168]{1,0:T(8,128)(2,1)S(1)}, bf16[32,7168]{1,0:T(8,128)(2,1)}, u32[]{:S(2)}, u32[]{:S(2)}) collective-permute-start(bf16[32,7168]{1,0:T(8,128)(2,1)S(1)} %collective-permute-done), channel_id=1, source_target_pairs={{0,32},{1,33},{2,34},{3,35},{4,36},{5,37},{6,38},{7,39},{8,40},{9,... | collective-permute-start | bytes 1376264 | tf_op jit(solution)/shard_map/ppermute | solution.py:37
  45.9 1.3 copy-start.2
  47.3 0.7 copy-start.9
  62.5 8.7 %copy-start.14 = (bf16[1536,1536]{1,0:T(8,128)(2,1)S(1)}, bf16[1536,1536]{1,0:T(8,128)(2,1)}, u32[]{:S(2)}) copy-start(bf16[1536,1536]{1,0:T(8,128)(2,1)} %param.14) | copy-start | bytes 14155780
  69.1 1.3 copy-start.3
  70.4 0.7 copy-start.10
  71.1 7.9 %collective-permute-start.8 = (bf16[4,32,7168]{2,1,0:T(8,128)(2,1)S(1)}, bf16[4,32,7168]{2,1,0:T(8,128)(2,1)S(1)}, u32[]{:S(2)}, u32[]{:S(2)}) collective-permute-start(bf16[4,32,7168]{2,1,0:T(8,128)(2,1)S(1)} %pad_maximum_fusion.1.rows_ref), channel_id=1, source_target_pairs={{0,16},{1,17},{2,18},{3,19},{4,20},{5,21},{6,22},{7,23},{8,24},{9,... | collective-permute-start | bytes 5505032 | tf_op jit(solution)/shard_map/ppermute | solution.py:37
  77.1 1.3 copy-start.4
  78.4 0.7 copy-start.11
  83.3 1.3 copy-start.5
  84.6 0.7 copy-start.12
  137.7 1.8 copy-start.1
  139.5 1.0 copy-start.6
  142.1 3.7 %collective-permute-start.9 = (bf16[256,3072]{1,0:T(8,128)(2,1)S(1)}, bf16[256,3072]{1,0:T(8,128)(2,1)S(1)}, u32[]{:S(2)}, u32[]{:S(2)}) collective-permute-start(bf16[256,3072]{1,0:T(8,128)(2,1)S(1)} %project.3), channel_id=1, source_target_pairs={{0,16},{1,17},{2,18},{3,19},{4,20},{5,21},{6,22},{7,23},{8,24},{9,... | collective-permute-start | bytes 4718600 | tf_op jit(solution)/shard_map/ppermute | solution.py:37
  146.4 1.6 copy-start.13
  148.2 12.0 %collective-permute-start.10 = (bf16[2,32,3072]{2,1,0:T(8,128)(2,1)S(1)}, bf16[2,32,3072]{2,1,0:T(8,128)(2,1)S(1)}, u32[]{:S(2)}, u32[]{:S(2)}) collective-permute-start(bf16[2,32,3072]{2,1,0:T(8,128)(2,1)S(1)} %get-tuple-element.56), channel_id=1, source_target_pairs={{0,32},{1,33},{2,34},{3,35},{4,36},{5,37},{6,38},{7,39},{8,40},{9,... | collective-permute-start | bytes 1179656 | tf_op jit(solution)/shard_map/ppermute | solution.py:37
  148.5 21.6 %collective-permute-start.11 = (bf16[2,32,3072]{2,1,0:T(8,128)(2,1)S(1)}, bf16[2,32,3072]{2,1,0:T(8,128)(2,1)S(1)}, u32[]{:S(2)}, u32[]{:S(2)}) collective-permute-start(bf16[2,32,3072]{2,1,0:T(8,128)(2,1)S(1)} %get-tuple-element.58), channel_id=1, source_target_pairs={{0,64},{1,65},{2,66},{3,67},{4,68},{5,69},{6,70},{7,71},{8,72},{9,... | collective-permute-start | bytes 1179656 | tf_op jit(solution)/shard_map/ppermute | solution.py:37
  152.5 20.2 %collective-permute-start.12 = (bf16[2,32,3072]{2,1,0:T(8,128)(2,1)S(1)}, bf16[2,32,3072]{2,1,0:T(8,128)(2,1)S(1)}, u32[]{:S(2)}, u32[]{:S(2)}) collective-permute-start(bf16[2,32,3072]{2,1,0:T(8,128)(2,1)S(1)} %get-tuple-element.57), channel_id=1, source_target_pairs={{0,96},{1,97},{2,98},{3,99},{4,100},{5,101},{6,102},{7,103},{8,104... | collective-permute-start | bytes 1179656 | tf_op jit(solution)/shard_map/ppermute | solution.py:37
  154.3 28.6 %copy-start.8 = (bf16[1,128,1536]{2,1,0:T(8,128)(2,1)S(1)}, bf16[1,128,1536]{2,1,0:T(8,128)(2,1)}, u32[]{:S(2)}) copy-start(bf16[1,128,1536]{2,1,0:T(8,128)(2,1)} %param.15) | copy-start | bytes 1179652
  174.0 8.8 %collective-permute-start.13 = (bf16[32,3072]{1,0:T(8,128)(2,1)S(1)}, bf16[32,3072]{1,0:T(8,128)(2,1)S(1)}, u32[]{:S(2)}, u32[]{:S(2)}) collective-permute-start(bf16[32,3072]{1,0:T(8,128)(2,1)S(1)} %fusion.4), channel_id=1, source_target_pairs={{0,140},{1,141},{2,142},{3,143},{4,136},{5,137},{6,138},{7,139},{8... | collective-permute-start | bytes 589832 | tf_op jit(solution)/shard_map/ppermute | solution.py:37
  186.2 4.8 %collective-permute-start.14 = (bf16[32,768]{1,0:T(8,128)(2,1)S(1)}, bf16[32,768]{1,0:T(8,128)(2,1)S(1)}, u32[]{:S(2)}, u32[]{:S(2)}) collective-permute-start(bf16[32,768]{1,0:T(8,128)(2,1)S(1)} %get-tuple-element.69), channel_id=1, source_target_pairs={{0,1},{1,0},{2,3},{3,2},{4,5},{5,4},{6,7},{7,6},{8,9},{9,8},{10,11... | collective-permute-start | bytes 147464 | tf_op jit(solution)/shard_map/ppermute | solution.py:37
  186.3 5.7 %collective-permute-start.15 = (bf16[32,768]{1,0:T(8,128)(2,1)S(1)}, bf16[32,768]{1,0:T(8,128)(2,1)S(1)}, u32[]{:S(2)}, u32[]{:S(2)}) collective-permute-start(bf16[32,768]{1,0:T(8,128)(2,1)S(1)} %get-tuple-element.68), channel_id=1, source_target_pairs={{0,2},{1,3},{2,0},{3,1},{4,6},{5,7},{6,4},{7,5},{8,10},{9,11},{10,... | collective-permute-start | bytes 147464 | tf_op jit(solution)/shard_map/ppermute | solution.py:37
  187.9 5.3 %collective-permute-start.16 = (bf16[32,768]{1,0:T(8,128)(2,1)S(1)}, bf16[32,768]{1,0:T(8,128)(2,1)S(1)}, u32[]{:S(2)}, u32[]{:S(2)}) collective-permute-start(bf16[32,768]{1,0:T(8,128)(2,1)S(1)} %get-tuple-element.67), channel_id=1, source_target_pairs={{0,3},{1,2},{2,1},{3,0},{4,7},{5,6},{6,5},{7,4},{8,11},{9,10},{10,... | collective-permute-start | bytes 147464 | tf_op jit(solution)/shard_map/ppermute | solution.py:37
  193.3 8.9 %collective-permute-start.17 = (bf16[4,32,768]{2,1,0:T(8,128)(2,1)S(1)}, bf16[4,32,768]{2,1,0:T(8,128)(2,1)S(1)}, u32[]{:S(2)}, u32[]{:S(2)}) collective-permute-start(bf16[4,32,768]{2,1,0:T(8,128)(2,1)S(1)} %get-tuple-element.65), channel_id=1, source_target_pairs={{0,140},{1,141},{2,142},{3,143},{4,136},{5,137},{6,138},{7,139},{8... | collective-permute-start | bytes 589832 | tf_op jit(solution)/shard_map/ppermute | solution.py:37
  202.2 10.4 %collective-permute-start.18 = (bf16[2,4,32,768]{3,2,1,0:T(8,128)(2,1)S(1)}, bf16[2,4,32,768]{3,2,1,0:T(8,128)(2,1)S(1)}, u32[]{:S(2)}, u32[]{:S(2)}) collective-permute-start(bf16[2,4,32,768]{3,2,1,0:T(8,128)(2,1)S(1)} %get-tuple-element.63), channel_id=1, source_target_pairs={{0,32},{1,33},{2,34},{3,35},{4,36},{5,37},{6,38},{7,39},{8,40},{9,... | collective-permute-start | bytes 1179656 | tf_op jit(solution)/shard_map/ppermute | solution.py:37
  202.3 14.4 %collective-permute-start.19 = (bf16[2,4,32,768]{3,2,1,0:T(8,128)(2,1)S(1)}, bf16[2,4,32,768]{3,2,1,0:T(8,128)(2,1)S(1)}, u32[]{:S(2)}, u32[]{:S(2)}) collective-permute-start(bf16[2,4,32,768]{3,2,1,0:T(8,128)(2,1)S(1)} %get-tuple-element.63), channel_id=1, source_target_pairs={{0,64},{1,65},{2,66},{3,67},{4,68},{5,69},{6,70},{7,71},{8,72},{9,... | collective-permute-start | bytes 1179656 | tf_op jit(solution)/shard_map/ppermute | solution.py:37
  204.1 15.1 %collective-permute-start.20 = (bf16[2,4,32,768]{3,2,1,0:T(8,128)(2,1)S(1)}, bf16[2,4,32,768]{3,2,1,0:T(8,128)(2,1)S(1)}, u32[]{:S(2)}, u32[]{:S(2)}) collective-permute-start(bf16[2,4,32,768]{3,2,1,0:T(8,128)(2,1)S(1)} %get-tuple-element.63), channel_id=1, source_target_pairs={{0,96},{1,97},{2,98},{3,99},{4,100},{5,101},{6,102},{7,103},{8,104... | collective-permute-start | bytes 1179656 | tf_op jit(solution)/shard_map/ppermute | solution.py:37
  219.4 3.5 %collective-permute-start.21 = (bf16[4,2,4,32,768]{4,3,2,1,0:T(8,128)(2,1)S(1)}, bf16[4,2,4,32,768]{4,3,2,1,0:T(8,128)(2,1)S(1)}, u32[]{:S(2)}, u32[]{:S(2)}) collective-permute-start(bf16[4,2,4,32,768]{4,3,2,1,0:T(8,128)(2,1)S(1)} %pad_maximum_fusion.2.a_ref), channel_id=1, source_target_pairs={{0,16},{1,17},{2,18},{3,19},{4,20},{5,21},{6,22},{7,23},{8,24},{9,... | collective-permute-start | bytes 4718600 | tf_op jit(solution)/shard_map/ppermute | solution.py:37
  222.9 1.5 copy-start.7
  228.4 17.1 %collective-permute-start.22 = (bf16[192,448]{1,0:T(8,128)(2,1)S(1)}, bf16[192,448]{1,0:T(8,128)(2,1)S(1)}, u32[]{:S(2)}, u32[]{:S(2)}) collective-permute-start(bf16[192,448]{1,0:T(8,128)(2,1)S(1)} %get-tuple-element.59), channel_id=1, source_target_pairs={{0,4},{1,5},{2,6},{3,7},{4,0},{5,1},{6,2},{7,3},{8,12},{9,13},{10,... | collective-permute-start | bytes 516104 | tf_op jit(solution)/shard_map/ppermute | solution.py:37
  237.4 14.8 %collective-permute-start.23 = (bf16[192,448]{1,0:T(8,128)(2,1)S(1)}, bf16[192,448]{1,0:T(8,128)(2,1)S(1)}, u32[]{:S(2)}, u32[]{:S(2)}) collective-permute-start(bf16[192,448]{1,0:T(8,128)(2,1)S(1)} %get-tuple-element.61), channel_id=1, source_target_pairs={{0,8},{1,9},{2,10},{3,11},{4,12},{5,13},{6,14},{7,15},{8,0},{9,1},... | collective-permute-start | bytes 516104 | tf_op jit(solution)/shard_map/ppermute | solution.py:37
  238.4 18.1 %collective-permute-start.24 = (bf16[192,448]{1,0:T(8,128)(2,1)S(1)}, bf16[192,448]{1,0:T(8,128)(2,1)S(1)}, u32[]{:S(2)}, u32[]{:S(2)}) collective-permute-start(bf16[192,448]{1,0:T(8,128)(2,1)S(1)} %get-tuple-element.60), channel_id=1, source_target_pairs={{0,12},{1,13},{2,14},{3,15},{4,8},{5,9},{6,10},{7,11},{8,4},{9,5},... | collective-permute-start | bytes 516104 | tf_op jit(solution)/shard_map/ppermute | solution.py:37
Sparse Core Ops, SparseCore 0:
  10.7 115.8 all-gather.4
  154.4 30.7 all-gather.6

commit v3 on v2

--- a/solution.py
+++ b/solution.py
@@ -1,3 +1,5 @@
+import functools
+
 import jax
 import jax.numpy as jnp
 from jax import lax
@@ -46,125 +48,134 @@
 
 
 def norm_kernel(place_ref, rows_ref, normed_ref, resid_ref):
-    widened = rows_ref[0].astype(f32)
+    widened = rows_ref[...].astype(f32)
     mean = jnp.mean(widened * widened, axis=-1, keepdims=True)
-    normed = (widened * lax.rsqrt(mean + eps)).astype(bf16)
-    blocks, _, depth = normed_ref.shape
-    for f in range(blocks):
-        normed_ref[f] = normed[:, f * depth : (f + 1) * depth]
+    normed_ref[...] = (widened * lax.rsqrt(mean + eps)).astype(bf16)
+    depth = resid_ref.shape[1]
+    for f in range(rows_ref.shape[1] // depth):
 
         @pl.when(place_ref[0] == f)
         def _():
-            resid_ref[...] = rows_ref[0, :, f * depth : (f + 1) * depth]
+            resid_ref[...] = rows_ref[:, f * depth : (f + 1) * depth]
 
 
 def normalize(rows, place):
-    slots, height, width = rows.shape
-    depth = width // 16
+    height, width = rows.shape
+    depth, per = width // 16, 64
     return pl.pallas_call(
         norm_kernel,
-        grid=(slots,),
+        grid=(height // per,),
         in_specs=[
             pl.BlockSpec(memory_space=pltpu.SMEM),
-            pl.BlockSpec((1, height, width), lambda i: (i, 0, 0)),
+            pl.BlockSpec((per, width), lambda i: (i, 0)),
         ],
         out_specs=[
-            pl.BlockSpec((16, height, depth), lambda i: (0, i, 0)),
-            pl.BlockSpec((height, depth), lambda i: (i, 0)),
+            pl.BlockSpec((per, width), lambda i: (i, 0)),
+            pl.BlockSpec((per, depth), lambda i: (i, 0)),
         ],
         out_shape=[
-            jax.ShapeDtypeStruct((16, slots * height, depth), bf16),
-            jax.ShapeDtypeStruct((slots * height, depth), bf16),
+            jax.ShapeDtypeStruct((height, width), bf16),
+            jax.ShapeDtypeStruct((height, depth), bf16),
         ],
-        compiler_params=params(12),
+        compiler_params=params(56),
         name="norm",
     )(place, rows)
 
 
-def layer_kernel(*refs):
-    normed_refs, resid_refs = refs[:4], refs[4:8]
-    w_ref, feature_ref, featt_ref, kvw_ref, acc = refs[8:]
-    step = pl.program_id(0)
-    out = feature_ref.shape[1]
-    total = None
-    for k in range(w_ref.shape[0]):
-        rows = jnp.concatenate([ref[k] for ref in normed_refs], axis=0)
-        term = jnp.dot(rows, w_ref[k, :, :out], preferred_element_type=f32)
-        total = term if total is None else total + term
-    kvw_ref[0] = jnp.concatenate([w_ref[k, :, out:] for k in range(w_ref.shape[0])], axis=1)
-
-    @pl.when(step == 0)
-    def _():
-        acc[...] = total
-
-    @pl.when(step > 0)
-    def _():
-        acc[...] += total
-
-    @pl.when(step == pl.num_programs(0) - 1)
-    def _():
-        pre = acc[...]
-        resid = jnp.concatenate([ref[...] for ref in resid_refs], axis=0).astype(f32)
-        feature = (resid + pre / (1.0 + jnp.exp(-pre))).astype(bf16)
-        feature_ref[...] = feature
-        featt_ref[...] = feature.T
-
-
-def layer(normed, resid, weights):
-    blocks, height, depth = normed[0].shape
-    rows, out, wide, per = 4 * height, resid[0].shape[1], weights.shape[2], 4
-    kv = (wide - out) * per
+def layer_kernel(place_ref, *refs, finish):
+    normed_refs, piece_refs = refs[:2], refs[2:10]
+    resid_refs, acc_ref = refs[10:12], refs[12]
+    kvw_ref, *out_refs, weights = refs[13:]
+    y = place_ref[2]
+    out = acc_ref.shape[1]
+    half = piece_refs[0].shape[0]
+    depth = 2 * half
+    for i, ref in enumerate(piece_refs):
+        at = pl.multiple_of((y ^ (i // 2)) * depth + i % 2 * half, 32)
+        weights[pl.ds(at, half)] = ref[...]
+    kvw_ref[...] = jnp.concatenate(
+        [weights[f * depth : (f + 1) * depth, out:] for f in range(4)], axis=1
+    )
+    rows = normed_refs[0].shape[0]
+    for i, (normed_ref, resid_ref) in enumerate(zip(normed_refs, resid_refs)):
+        at = slice(i * rows, (i + 1) * rows)
+        total = acc_ref[at] + jnp.dot(
+            normed_ref[...], weights[:, :out], preferred_element_type=f32
+        )
+        if finish:
+            feature_ref, featt_ref = out_refs
+            silu = total / (1.0 + jnp.exp(-total))
+            feature = (resid_ref[...].astype(f32) + silu).astype(bf16)
+            feature_ref[at] = feature
+            featt_ref[:, at] = feature.T
+        else:
+            out_refs[0][at] = total
+
+
+def layer(place, normed, pieces, resid, acc, e, finish):
+    rows, out = acc.shape
+    wide = pieces[0][0].shape[1]
+    kv = wide - out
+    depth = normed[0].shape[1] // 16
+    half = depth // 2
 
     def whole(shape):
-        return pl.BlockSpec(shape, lambda k: (0, 0))
-
+        return pl.BlockSpec(shape, lambda i, place: (0, 0))
+
+    if finish:
+        shapes = [((rows, out), bf16), ((out, rows), bf16)]
+    else:
+        shapes = [((rows, out), f32)]
+    shapes = [((depth, 4 * kv), bf16)] + shapes
     return pl.pallas_call(
-        layer_kernel,
-        grid=(blocks // per,),
-        in_specs=[pl.BlockSpec((per, height, depth), lambda k: (k, 0, 0))] * 4
-        + [whole(resid[0].shape)] * 4
-        + [pl.BlockSpec((per, depth, wide), lambda k: (k, 0, 0))],
-        out_specs=[
-            whole((rows, out)),
-            whole((out, rows)),
-            pl.BlockSpec((1, depth, kv), lambda k: (k, 0, 0)),
-        ],
-        out_shape=[
-            jax.ShapeDtypeStruct((rows, out), bf16),
-            jax.ShapeDtypeStruct((out, rows), bf16),
-            jax.ShapeDtypeStruct((blocks // per, depth, kv), bf16),
-        ],
-        scratch_shapes=[pltpu.VMEM((rows, out), f32)],
-        compiler_params=params(56),
+        functools.partial(layer_kernel, finish=finish),
+        grid_spec=pltpu.PrefetchScalarGridSpec(
+            num_scalar_prefetch=1,
+            grid=(1,),
+            in_specs=[
+                pl.BlockSpec((rows // 2, 4 * depth), lambda i, place: (0, place[1] ^ e)),
+            ]
+            * 2
+            + [
+                pl.BlockSpec((half, wide), lambda i, place, at=at: (at, 0)) for _, at in pieces
+            ]
+            + [whole(r.shape) for r in resid]
+            + [whole(acc.shape)],
+            out_specs=[whole(shape) for shape, _ in shapes],
+            scratch_shapes=[pltpu.VMEM((4 * depth, wide), bf16)],
+        ),
+        out_shape=[jax.ShapeDtypeStruct(shape, dtype) for shape, dtype in shapes],
+        compiler_params=params(32),
         name="layer",
-    )(*normed, *resid, weights)
-
-
-def project_kernel(feature_ref, w_ref, out_ref):
-    out_ref[...] = jnp.dot(feature_ref[...], w_ref[0], preferred_element_type=f32).astype(
-        out_ref.dtype
-    )
+    )(place, *normed, *[array for array, _ in pieces], *resid, acc)
+
+
+def project_kernel(feature_ref, *refs):
+    out_ref = refs[-1]
+    kv = refs[0].shape[1]
+    for e, w_ref in enumerate(refs[:-1]):
+        out_ref[:, e * kv : (e + 1) * kv] = jnp.dot(
+            feature_ref[...], w_ref[...], preferred_element_type=f32
+        ).astype(out_ref.dtype)
 
 
 def project(feature, half, weights, dtype):
     rows, depth = feature.shape[0] // 2, feature.shape[1]
-    blocks, _, kv = weights.shape
+    kv = weights[0].shape[1]
     return pl.pallas_call(
         project_kernel,
-        grid=(blocks,),
-        in_specs=[
-            pl.BlockSpec((rows, depth), lambda i: (half, 0)),
-            pl.BlockSpec((1, depth, kv), lambda i: (i, 0, 0)),
-        ],
-        out_specs=pl.BlockSpec((rows, kv), lambda i: (0, i)),
-        out_shape=jax.ShapeDtypeStruct((rows, blocks * kv), dtype),
-        compiler_params=params(16),
+        grid=(1,),
+        in_specs=[pl.BlockSpec((rows, depth), lambda i: (half, 0))]
+        + [pl.BlockSpec((depth, kv), lambda i: (0, 0))] * 4,
+        out_specs=pl.BlockSpec((rows, 4 * kv), lambda i: (0, 0)),
+        out_shape=jax.ShapeDtypeStruct((rows, 4 * kv), dtype),
+        compiler_params=params(20),
         name="project",
-    )(feature, weights)
+    )(feature, *weights)
 
 
 def attention_kernel(
-    place_ref, images_ref, lengths_ref, own_ref, other_ref, q_ref, cg_ref, context_ref, grads_ref
+    place_ref, images_ref, lengths_ref, own_ref, other_ref, q_ref, cg_ref, context_ref, grads_ref, kvs
 ):
     key_rows, width = own_ref.shape
     width_act = width // 2
@@ -173,10 +184,14 @@
     cols = heads * HEAD_DIM
     scale = HEAD_DIM ** (-0.5)
     piece = width // 16
-    y = place_ref[2]
+    l, y = place_ref[1], place_ref[2]
     last = (((1,), (1,)), ((), ()))
     first = (((0,), (0,)), ((), ()))
-    kv = (own_ref[...] + other_ref[...].astype(f32)).astype(bf16)
+    wide = width // 4
+    for e in range(4):
+        own = own_ref[:, e * wide : (e + 1) * wide]
+        other = other_ref[:, (3 - e) * wide : (4 - e) * wide].astype(f32)
+        kvs[e] = (own + other).astype(bf16)
     row_head = lax.broadcasted_iota(jnp.int32, (heads * key_rows, cols), 0) // key_rows
     col_head = lax.broadcasted_iota(jnp.int32, (heads * key_rows, cols), 1) // HEAD_DIM
     same = row_head == col_head
@@ -196,8 +211,9 @@
 
     for g in range(width_act // cols):
         at = slice(g * cols, (g + 1) * cols)
-        keys = spread(kv[:, g * cols : (g + 1) * cols])
-        values = spread(kv[:, width_act + g * cols : width_act + (g + 1) * cols])
+        column = slice(g % 2 * cols, (g % 2 + 1) * cols)
+        keys = spread(kvs[(g // 2) ^ l, :, column])
+        values = spread(kvs[(2 + g // 2) ^ l, :, column])
         queries = q_ref[:, at]
         grad_in = jnp.where(query_live, cg_ref[:, at], jnp.zeros((), bf16))
         scores = by_head(lax.dot_general(keys, queries, last, preferred_element_type=f32) * scale)
@@ -234,6 +250,7 @@
             jax.ShapeDtypeStruct(queries.shape, bf16),
             jax.ShapeDtypeStruct((4, key_rows, width // 4), bf16),
         ],
+        scratch_shapes=[pltpu.VMEM((4, key_rows, width // 4), bf16)],
         compiler_params=params(24),
         name="attention",
     )(place, images, lengths, own, other, queries, context_grad)
@@ -243,8 +260,7 @@
     step = pl.program_id(0)
     l, y = place_ref[1], place_ref[2]
     wide = acc.shape[1]
-    packed = [ref[:, m, 0] for ref in (a_ref, b_ref) for m in range(2)]
-    grads = jnp.concatenate(packed, axis=0).reshape(-1, wide)
+    grads = jnp.concatenate([ref[:, :, 0].reshape(-1, wide) for ref in (a_ref, b_ref)], axis=0)
     term = jnp.dot(featt_ref[0], grads, preferred_element_type=f32)
 
     @pl.when(step == 0)
@@ -272,7 +288,7 @@
     blocks, out, rows = featt.shape
     key_rows, wide = grads_a.shape[-2:]
     kv = wide // 4
-    near = pl.BlockSpec((4, 2, 1, key_rows, wide), lambda i, place: (0, 0, i ^ place[2], 0, 0))
+    near = pl.BlockSpec((4, 2, 1, key_rows, wide), lambda i, place: (0, 0, i, 0, 0))
     return pl.pallas_call(
         weight_grad_kernel,
         grid_spec=pltpu.PrefetchScalarGridSpec(
@@ -298,9 +314,6 @@
     )(place, grads_a, grads_b, featt)
 
 
-Y_GROUPS = [[l * 4 + y for y in range(4)] for l in range(4)]
-
-
 def on_device(
     vlm_rows, images, action_hidden, lengths, vlm_weight, kv_weight, query_weight, context_grad
 ):
@@ -309,36 +322,67 @@
     dp, fsdp = lax.axis_index("dp"), lax.axis_index("fsdp")
     place = jnp.stack([dp, fsdp // 4, fsdp % 4]).astype(jnp.int32)
 
-    weights = lax.all_gather(
-        jnp.concatenate([vlm_weight.T, kv_weight.T], axis=1), "fsdp", axis=0, tiled=False
-    )
-    mirrored = send(vlm_rows[0], MIRROR)
-    own_a = gather_along(vlm_rows[0], ALONG_X)
-    mirrored, own_a = lax.optimization_barrier((mirrored, own_a))
-    far_a = gather_along(mirrored, ALONG_X)
-    own_b = send(own_a, CORE)
-    normed, resid = zip(normalize(own_a, place), normalize(own_b, place))
-    far_a, normed, resid = lax.optimization_barrier((far_a, normed, resid))
-    far_b = send(far_a, CORE)
-    more, rest = zip(normalize(far_a, place), normalize(far_b, place))
-    normed = (normed[0], more[0], normed[1], more[1])
-    resid = (resid[0], rest[0], resid[1], rest[1])
+    block = jnp.concatenate([vlm_weight.T, kv_weight.T], axis=1)
+    half = block.shape[0] // 2
+
+    def around(before, w):
+        up, down = before
+        low, high = down[-2 * half : -half], up[-half:]
+        if w is not None:
+            low, high = jnp.concatenate([low, w]), jnp.concatenate([high, w])
+        return send(low, ALONG_Y[1]), send(high, ALONG_Y[3])
+
+    rows = vlm_rows[0]
+    y0 = send(block, ALONG_Y[1]), send(block, ALONG_Y[3])
+    z1, mirrored = send(block, ALONG_Z[1]), send(rows, MIRROR)
+    y0, z1, mirrored, block = lax.optimization_barrier((y0, z1, mirrored, block))
+
+    rows = jnp.stack([rows, mirrored])
+    y1, z2 = around(y0, z1), send(block, ALONG_Z[2])
+    x1, x3 = send(rows, ALONG_X[1]), send(rows, ALONG_X[3])
+    y1, z2, x1, x3, block, rows = lax.optimization_barrier((y1, z2, x1, x3, block, rows))
+
+    y2, z3 = around(y1, z2), send(block, ALONG_Z[3])
+    x2 = send(rows, ALONG_X[2])
     queries = lax.dot_general(
         action_hidden[0], query_weight, (((1,), (1,)), ((), ())), preferred_element_type=f32
     ).astype(bf16)
-    queries, normed = lax.optimization_barrier((queries, normed))
-    feature, featt, kv_weights = layer(normed, resid, weights)
-    featt_all = lax.all_gather(
-        featt, "fsdp", axis=0, tiled=False, axis_index_groups=Y_GROUPS
-    )
+    y2, z3, x2, queries = lax.optimization_barrier((y2, z3, x2, queries))
+
+    y3 = around(y2, z3)
+    rows_a = jnp.stack([rows, x1, x2, x3]).reshape(-1, width)
+    rows_b = send(rows_a, CORE)
+    normed, resid = zip(normalize(rows_a, place), normalize(rows_b, place))
+    acc = jnp.zeros((16 * slot_rows, vlm_weight.shape[0]), f32)
+    kv_weights = []
+
+    def add(e, own, near, after, acc):
+        first = near[0].shape[0] // half - 2
+        pieces = [(own, 0), (own, 1), (near[0], first), (near[0], first + 1)]
+        pieces += [(after[0], 0), (after[1], 0), (near[1], first), (near[1], first + 1)]
+        kvw, *rest = layer(place, normed, pieces, resid, acc, e, e == 3)
+        kv_weights.append(kvw)
+        return rest
+
+    (acc,) = add(0, block, y0, y1, acc)
+    (acc,) = add(1, z1, y1, y2, acc)
+    y3, acc = lax.optimization_barrier((y3, acc))
+
+    y4 = around(y3, None)
+    (acc,) = add(2, z2, y2, y3, acc)
+    feature, featt = add(3, z3, y3, y4, acc)
 
     part_b = project(feature, 1, kv_weights, bf16)
     swapped = send(part_b, CORE)
     part_a = project(feature, 0, kv_weights, f32)
-    both = (part_a + swapped.astype(f32)).reshape(2, 4, slot_rows, 2 * width_act)
-    mine = both[:, 0]
-    for e in (1, 2, 3):
-        mine = mine + send(both[:, e].astype(bf16), ALONG_X[e]).astype(f32)
+    both = (part_a + swapped.astype(f32)).reshape(4, 2, slot_rows, 2 * width_act)
+    both, featt = lax.optimization_barrier((both, featt))
+    sums = [send(both[e].astype(bf16), ALONG_X[e]) for e in (1, 2, 3)]
+    featt_all = gather_along(featt, ALONG_Y)
+    sums, featt_all = lax.optimization_barrier((sums, featt_all))
+    mine = both[0]
+    for term in sums:
+        mine = mine + term.astype(f32)
     other = send(mine[1].astype(bf16), MIRROR)
 
     context, grads = attention(

time: 265 us -> 250 us (0.943)
  between operations: 15.6 us -> 2.48 us
  Pallas kernels: 39.4 us -> 28.3 us
  starting transfers between devices: 44.7 us -> 52.4 us
  local copies, waits for them, and re-layouts: 16.5 us -> 10.3 us
  waiting for transfers between devices: 141 us -> 147 us
    ppermute x25 -> x37, waiting for transfers between devices: 99.2 us -> 147 us  [send(): return lax.ppermute(array, AXES, table)]
    all_gather x2 -> x0, waiting for transfers between devices: 41.4 us -> none  [the longest x1 41.4 us: on_device(): lax.all_gather(jnp.concatenate([vlm_weight.T, kv_weight.T], axis=1), 'fsd...]
    pallas_call x7 -> x8, Pallas kernels: 32.1 us -> 21 us  [the longest x2 11.2 us: normalize(): pl.pallas_call(norm_kernel, grid=(height // per,), in_specs=[pl.BlockSpec...]
    ppermute x25 -> x37, starting transfers between devices: 44.6 us -> 52.4 us  [send(): return lax.ppermute(array, AXES, table)]
    unnamed x34 -> x58, local copies, waits for them, and re-layouts: 16.2 us -> 9.75 us
  transfers between devices with their start and end apart: 27 -> 37, of which waited for: 22 -> 21; matrix products, arithmetic and copies ran while one was open for 2% -> 2% of each run, Pallas kernels for 9% -> 7%
where the time goes in v3:
time: 250 us
  waiting for transfers between devices  147 us (59%)
  starting transfers between devices  52.4 us (21%)
  Pallas kernels  28.3 us (11%)
  local copies, waits for them, and re-layouts  10.3 us (4%)
  other arithmetic  7.06 us (3%)
    ppermute x37, waiting for transfers between devices, send(): return lax.ppermute(array, AXES, table)  147 us
    ppermute x37, starting transfers between devices, send(): return lax.ppermute(array, AXES, table)  52.4 us
    pallas_call x2, Pallas kernels, normalize(): pl.pallas_call(norm_kernel, grid=(height // per,), in_specs=[pl.BlockSpec...  11.2 us
    unnamed x58, local copies, waits for them, and re-layouts  9.75 us
    pallas_call x4, Pallas kernels, layer(): pl.pallas_call(functools.partial(layer_kernel, finish=finish), grid_spec=...  7.82 us
  transfers between devices with their start and end apart: 37, of which 21 were waited for; matrix products, arithmetic and copies ran while one was open for 2% of the time, Pallas kernels for 7%

profile of v3, /device:TPU:32, one launch (start us, length us, event | category | flops | bytes accessed | tf_op | source)
XLA Modules:
  0.0 250.0 jit_solution(3439564304677879190)
XLA Ops:
  3.2 1.7 collective-permute-start
  4.8 2.2 collective-permute-start.1
  7.1 6.8 %collective-permute-start.3 = (bf16[32,7168]{1,0:T(8,128)(2,1)S(1)}, bf16[32,7168]{1,0:T(8,128)(2,1)S(1)}, u32[]{:S(2)}, u32[]{:S(2)}) collective-permute-start(bf16[32,7168]{1,0:T(8,128)(2,1)S(1)} %bitcast.72), channel_id=1, source_target_pairs={{0,140},{1,141},{2,142},{3,143},{4,136},{5,137},{6,138},{7,139},{8... | collective-permute-start | bytes 1376264 | tf_op jit(solution)/shard_map/ppermute | solution.py:39
  13.9 22.0 %collective-permute-done.3 = bf16[32,7168]{1,0:T(8,128)(2,1)S(1)} collective-permute-done((bf16[32,7168]{1,0:T(8,128)(2,1)S(1)}, bf16[32,7168]{1,0:T(8,128)(2,1)S(1)}, u32[]{:S(2)}, u32[]{:S(2)}) %collective-permute-start.3) | collective-permute-done | bytes 458784 | tf_op jit(solution)/shard_map/ppermute | solution.py:39
  36.0 1.6 collective-permute-start.7
  37.6 2.1 collective-permute-start.8
  41.6 22.5 %collective-permute-done.6.refs_2_.refs_3_ = bf16[448,640]{1,0:T(8,128)(2,1)S(1)} collective-permute-done((bf16[448,640]{1,0:T(8,128)(2,1)S(1)}, bf16[448,640]{1,0:T(8,128)(2,1)S(1)}, u32[]{:S(2)}, u32[]{:S(2)}) %collective-permute-start.6) | collective-permute-done | bytes 573472 | tf_op jit(solution)/shard_map/ppermute | solution.py:39
  65.3 2.1 collective-permute-start.10
  68.6 2.4 convolution_convert_fusion.q_ref
  71.0 21.4 %collective-permute-done.11.refs_2_.refs_3_ = bf16[448,640]{1,0:T(8,128)(2,1)S(1)} collective-permute-done((bf16[448,640]{1,0:T(8,128)(2,1)S(1)}, bf16[448,640]{1,0:T(8,128)(2,1)S(1)}, u32[]{:S(2)}, u32[]{:S(2)}) %collective-permute-start.11) | collective-permute-done | bytes 573472 | tf_op jit(solution)/shard_map/ppermute | solution.py:39
  92.5 2.3 pad_maximum_fusion
  95.0 1.4 pad_maximum_fusion.8
  96.4 1.7 collective-permute-start.14
  100.0 5.5 %norm.2 = (bf16[256,7168]{1,0:T(8,128)(2,1)}, bf16[256,448]{1,0:T(8,128)(2,1)}) custom-call(s32[3]{0:T(128)} %pad_add_fusion.place_ref, bf16[256,7168]{1,0:T(8,128)(2,1)} %bitcast.12.rows_ref), custom_call_target="tpu_custom_call" | custom-call | tf_op jit(solution)/shard_map/norm/pallas_call | solution.py:65
  105.5 5.7 %norm.3 = (bf16[256,7168]{1,0:T(8,128)(2,1)}, bf16[256,448]{1,0:T(8,128)(2,1)}) custom-call(s32[3]{0:T(128)} %pad_add_fusion.place_ref, bf16[256,7168]{1,0:T(8,128)(2,1)} %collective-permute-done.13.rows_ref), custom_call_target="tpu_custom_call" | custom-call | tf_op jit(solution)/shard_map/norm/pallas_call | solution.py:65
  111.4 2.0 copy-done.3
  118.5 1.9 layer.4
  120.4 1.9 layer.5
  122.5 2.1 collective-permute-start.17
  124.6 1.9 layer.6
  126.5 4.6 %collective-permute-done.16.refs_6_ = bf16[224,640]{1,0:T(8,128)(2,1)S(1)} collective-permute-done((bf16[224,640]{1,0:T(8,128)(2,1)S(1)}, bf16[224,640]{1,0:T(8,128)(2,1)S(1)}, u32[]{:S(2)}, u32[]{:S(2)}) %collective-permute-start.16) | collective-permute-done | bytes 286752 | tf_op jit(solution)/shard_map/ppermute | solution.py:39
  132.5 2.2 layer.7
  136.8 2.4 collective-permute-done.18
  140.2 3.0 %collective-permute-start.23 = (bf16[448,512]{1,0:T(8,128)(2,1)S(1)}, bf16[448,512]{1,0:T(8,128)(2,1)S(1)}, u32[]{:S(2)}, u32[]{:S(2)}) collective-permute-start(bf16[448,512]{1,0:T(8,128)(2,1)S(1)} %get-tuple-element.78), channel_id=1, source_target_pairs={{0,2},{1,3},{2,0},{3,1},{4,6},{5,7},{6,4},{7,5},{8,10},{9,11},{10,... | collective-permute-start | bytes 1376264 | tf_op jit(solution)/shard_map/ppermute | solution.py:39
  144.7 1.4 collective-permute-start.19
  146.1 2.7 %collective-permute-start.20 = (bf16[2,32,3072]{2,1,0:T(8,128)(2,1)S(1)}, bf16[2,32,3072]{2,1,0:T(8,128)(2,1)S(1)}, u32[]{:S(2)}, u32[]{:S(2)}) collective-permute-start(bf16[2,32,3072]{2,1,0:T(8,128)(2,1)S(1)} %get-tuple-element.89), channel_id=1, source_target_pairs={{0,64},{1,65},{2,66},{3,67},{4,68},{5,69},{6,70},{7,71},{8,72},{9,... | collective-permute-start | bytes 1179656 | tf_op jit(solution)/shard_map/ppermute | solution.py:39
  148.8 4.2 %collective-permute-done.22 = bf16[448,512]{1,0:T(8,128)(2,1)S(1)} collective-permute-done((bf16[448,512]{1,0:T(8,128)(2,1)S(1)}, bf16[448,512]{1,0:T(8,128)(2,1)S(1)}, u32[]{:S(2)}, u32[]{:S(2)}) %collective-permute-start.22) | collective-permute-done | bytes 458784 | tf_op jit(solution)/shard_map/ppermute | solution.py:39
  153.1 2.3 collective-permute-start.21
  156.7 7.0 %collective-permute-done.23 = bf16[448,512]{1,0:T(8,128)(2,1)S(1)} collective-permute-done((bf16[448,512]{1,0:T(8,128)(2,1)S(1)}, bf16[448,512]{1,0:T(8,128)(2,1)S(1)}, u32[]{:S(2)}, u32[]{:S(2)}) %collective-permute-start.23) | collective-permute-done | bytes 458784 | tf_op jit(solution)/shard_map/ppermute | solution.py:39
  163.7 2.6 %collective-permute-done.24 = bf16[448,512]{1,0:T(8,128)(2,1)S(1)} collective-permute-done((bf16[448,512]{1,0:T(8,128)(2,1)S(1)}, bf16[448,512]{1,0:T(8,128)(2,1)S(1)}, u32[]{:S(2)}, u32[]{:S(2)}) %collective-permute-start.24) | collective-permute-done | bytes 458784 | tf_op jit(solution)/shard_map/ppermute | solution.py:39
  166.5 5.7 %collective-permute-done.21 = bf16[2,32,3072]{2,1,0:T(8,128)(2,1)S(1)} collective-permute-done((bf16[2,32,3072]{2,1,0:T(8,128)(2,1)S(1)}, bf16[2,32,3072]{2,1,0:T(8,128)(2,1)S(1)}, u32[]{:S(2)}, u32[]{:S(2)}) %collective-permute-start.21) | collective-permute-done | bytes 393248 | tf_op jit(solution)/shard_map/ppermute | solution.py:39
  173.6 7.6 %collective-permute-done.25.other_ref = bf16[32,3072]{1,0:T(8,128)(2,1)S(1)} collective-permute-done((bf16[32,3072]{1,0:T(8,128)(2,1)S(1)}, bf16[32,3072]{1,0:T(8,128)(2,1)S(1)}, u32[]{:S(2)}, u32[]{:S(2)}) %collective-permute-start.25) | collective-permute-done | bytes 196640 | tf_op jit(solution)/shard_map/ppermute | solution.py:39
  181.2 3.4 %attention.1 = (bf16[128,1536]{1,0:T(8,128)(2,1)}, bf16[4,32,768]{2,1,0:T(8,128)(2,1)S(1)}) custom-call(s32[3]{0:T(128)S(1)} %copy-done.25, s32[1]{0:T(128)S(6)} %copy.12.images_ref, s32[1]{0:T(128)S(6)} %copy.13.lengths_ref, f32[32,3072]{1,0:T(8,128)S(1)} %slice_bitcast_fusion.own_ref, bf16[32,3072]{1,0:T(8,128)(2,1)S(1)} %collective-permute-done.25.other_ref, ...), custom_call_target="tpu_custom_call" | custom-call | tf_op jit(solution)/shard_map/attention/pallas_call | solution.py:245
  184.7 3.5 %collective-permute-start.27 = (bf16[32,768]{1,0:T(8,128)(2,1)S(1)}, bf16[32,768]{1,0:T(8,128)(2,1)S(1)}, u32[]{:S(2)}, u32[]{:S(2)}) collective-permute-start(bf16[32,768]{1,0:T(8,128)(2,1)S(1)} %get-tuple-element.106), channel_id=1, source_target_pairs={{0,2},{1,3},{2,0},{3,1},{4,6},{5,7},{6,4},{7,5},{8,10},{9,11},{10,... | collective-permute-start | bytes 147464 | tf_op jit(solution)/shard_map/ppermute | solution.py:39
  189.4 1.4 collective-permute-done.27
  190.8 2.7 %collective-permute-done.28 = bf16[32,768]{1,0:T(8,128)(2,1)S(1)} collective-permute-done((bf16[32,768]{1,0:T(8,128)(2,1)S(1)}, bf16[32,768]{1,0:T(8,128)(2,1)S(1)}, u32[]{:S(2)}, u32[]{:S(2)}) %collective-permute-start.28) | collective-permute-done | bytes 49184 | tf_op jit(solution)/shard_map/ppermute | solution.py:39
  194.7 7.6 %collective-permute-done.29 = bf16[4,32,768]{2,1,0:T(8,128)(2,1)S(1)} collective-permute-done((bf16[4,32,768]{2,1,0:T(8,128)(2,1)S(1)}, bf16[4,32,768]{2,1,0:T(8,128)(2,1)S(1)}, u32[]{:S(2)}, u32[]{:S(2)}) %collective-permute-start.29) | collective-permute-done | bytes 196640 | tf_op jit(solution)/shard_map/ppermute | solution.py:39
  202.5 3.1 %collective-permute-start.31 = (bf16[2,4,32,768]{3,2,1,0:T(8,128)(2,1)S(1)}, bf16[2,4,32,768]{3,2,1,0:T(8,128)(2,1)S(1)}, u32[]{:S(2)}, u32[]{:S(2)}) collective-permute-start(bf16[2,4,32,768]{3,2,1,0:T(8,128)(2,1)S(1)} %get-tuple-element.101), channel_id=1, source_target_pairs={{0,64},{1,65},{2,66},{3,67},{4,68},{5,69},{6,70},{7,71},{8,72},{9,... | collective-permute-start | bytes 1179656 | tf_op jit(solution)/shard_map/ppermute | solution.py:39
  205.6 1.6 collective-permute-start.32
  207.1 5.4 %collective-permute-done.30 = bf16[2,4,32,768]{3,2,1,0:T(8,128)(2,1)S(1)} collective-permute-done((bf16[2,4,32,768]{3,2,1,0:T(8,128)(2,1)S(1)}, bf16[2,4,32,768]{3,2,1,0:T(8,128)(2,1)S(1)}, u32[]{:S(2)}, u32[]{:S(2)}) %collective-permute-start.30) | collective-permute-done | bytes 393248 | tf_op jit(solution)/shard_map/ppermute | solution.py:39
  212.5 5.5 %collective-permute-done.31 = bf16[2,4,32,768]{3,2,1,0:T(8,128)(2,1)S(1)} collective-permute-done((bf16[2,4,32,768]{3,2,1,0:T(8,128)(2,1)S(1)}, bf16[2,4,32,768]{3,2,1,0:T(8,128)(2,1)S(1)}, u32[]{:S(2)}, u32[]{:S(2)}) %collective-permute-start.31) | collective-permute-done | bytes 393248 | tf_op jit(solution)/shard_map/ppermute | solution.py:39
  218.0 2.5 %collective-permute-done.32 = bf16[2,4,32,768]{3,2,1,0:T(8,128)(2,1)S(1)} collective-permute-done((bf16[2,4,32,768]{3,2,1,0:T(8,128)(2,1)S(1)}, bf16[2,4,32,768]{3,2,1,0:T(8,128)(2,1)S(1)}, u32[]{:S(2)}, u32[]{:S(2)}) %collective-permute-start.32) | collective-permute-done | bytes 393248 | tf_op jit(solution)/shard_map/ppermute | solution.py:39
  220.8 3.4 %collective-permute-done.33.b_ref = bf16[4,2,4,32,768]{4,3,2,1,0:T(8,128)(2,1)S(1)} collective-permute-done((bf16[4,2,4,32,768]{4,3,2,1,0:T(8,128)(2,1)S(1)}, bf16[4,2,4,32,768]{4,3,2,1,0:T(8,128)(2,1)S(1)}, u32[]{:S(2)}, u32[]{:S(2)}) %collective-permute-start.33) | collective-permute-done | bytes 1572896 | tf_op jit(solution)/shard_map/ppermute | solution.py:39
  224.2 3.9 %weight_grad.1 = (f32[192,448]{1,0:T(8,128)S(1)}, bf16[4,192,448]{2,1,0:T(8,128)(2,1)S(1)}) custom-call(s32[3]{0:T(128)S(1)} %copy-done.25, bf16[4,2,4,32,768]{4,3,2,1,0:T(8,128)(2,1)S(1)} %pad_maximum_fusion.2.a_ref, bf16[4,2,4,32,768]{4,3,2,1,0:T(8,128)(2,1)S(1)} %collective-permute-done.33.b_ref, bf16[4,448,512]{2,1,0:T(8,128)(2,1)S(1)} %pad_maximum_fusion.1.featt_ref), custom_call_target="tpu_custom_call" | custom-call | tf_op jit(solution)/shard_map/weight_grad/pallas_call | solution.py:292
  228.3 2.7 %collective-permute-start.35 = (bf16[192,448]{1,0:T(8,128)(2,1)S(1)}, bf16[192,448]{1,0:T(8,128)(2,1)S(1)}, u32[]{:S(2)}, u32[]{:S(2)}) collective-permute-start(bf16[192,448]{1,0:T(8,128)(2,1)S(1)} %get-tuple-element.93), channel_id=1, source_target_pairs={{0,8},{1,9},{2,10},{3,11},{4,12},{5,13},{6,14},{7,15},{8,0},{9,1},... | collective-permute-start | bytes 516104 | tf_op jit(solution)/shard_map/ppermute | solution.py:39
  231.8 4.7 %collective-permute-done.34 = bf16[192,448]{1,0:T(8,128)(2,1)S(1)} collective-permute-done((bf16[192,448]{1,0:T(8,128)(2,1)S(1)}, bf16[192,448]{1,0:T(8,128)(2,1)S(1)}, u32[]{:S(2)}, u32[]{:S(2)}) %collective-permute-start.34) | collective-permute-done | bytes 172064 | tf_op jit(solution)/shard_map/ppermute | solution.py:39
  236.5 8.3 %collective-permute-done.35 = bf16[192,448]{1,0:T(8,128)(2,1)S(1)} collective-permute-done((bf16[192,448]{1,0:T(8,128)(2,1)S(1)}, bf16[192,448]{1,0:T(8,128)(2,1)S(1)}, u32[]{:S(2)}, u32[]{:S(2)}) %collective-permute-start.35) | collective-permute-done | bytes 172064 | tf_op jit(solution)/shard_map/ppermute | solution.py:39
  244.8 4.3 %collective-permute-done.36 = bf16[192,448]{1,0:T(8,128)(2,1)S(1)} collective-permute-done((bf16[192,448]{1,0:T(8,128)(2,1)S(1)}, bf16[192,448]{1,0:T(8,128)(2,1)S(1)}, u32[]{:S(2)}, u32[]{:S(2)}) %collective-permute-start.36) | collective-permute-done | bytes 172064 | tf_op jit(solution)/shard_map/ppermute | solution.py:39
  (124 shorter events, 26.7 us)
Async XLA Ops:
  0.6 68.0 %copy-start = (bf16[1,128,1536]{2,1,0:T(8,128)(2,1)S(1)}, bf16[1,128,1536]{2,1,0:T(8,128)(2,1)}, u32[]{:S(2)}) copy-start(bf16[1,128,1536]{2,1,0:T(8,128)(2,1)} %param.10) | copy-start | bytes 1179652
  0.6 6.5 %copy-start.27 = (bf16[1,32,7168]{2,1,0:T(8,128)(2,1)S(1)}, bf16[1,32,7168]{2,1,0:T(8,128)(2,1)}, u32[]{:S(2)}) copy-start(bf16[1,32,7168]{2,1,0:T(8,128)(2,1)} %param.8) | copy-start | bytes 1376260
  3.2 64.5 %copy-start.8 = (bf16[448,640]{1,0:T(8,128)(2,1)}, bf16[448,640]{1,0:T(8,128)(2,1)S(1)}, u32[]{:S(2)}) copy-start(bf16[448,640]{1,0:T(8,128)(2,1)S(1)} %pad_maximum_fusion.10.refs_2_.refs_3_) | copy-start | bytes 1720324
  3.2 32.7 %collective-permute-start = (bf16[448,640]{1,0:T(8,128)(2,1)S(1)}, bf16[448,640]{1,0:T(8,128)(2,1)S(1)}, u32[]{:S(2)}, u32[]{:S(2)}) collective-permute-start(bf16[448,640]{1,0:T(8,128)(2,1)S(1)} %pad_maximum_fusion.10.refs_2_.refs_3_), channel_id=1, source_target_pairs={{0,1},{1,0},{2,3},{3,2},{4,5},{5,4},{6,7},{7,6},{8,9},{9,8},{10,11... | collective-permute-start | bytes 1720328 | tf_op jit(solution)/shard_map/ppermute | solution.py:39
  4.8 31.0 %collective-permute-start.1 = (bf16[448,640]{1,0:T(8,128)(2,1)S(1)}, bf16[448,640]{1,0:T(8,128)(2,1)S(1)}, u32[]{:S(2)}, u32[]{:S(2)}) collective-permute-start(bf16[448,640]{1,0:T(8,128)(2,1)S(1)} %pad_maximum_fusion.10.refs_2_.refs_3_), channel_id=1, source_target_pairs={{0,3},{1,2},{2,1},{3,0},{4,7},{5,6},{6,5},{7,4},{8,11},{9,10},{10,... | collective-permute-start | bytes 1720328 | tf_op jit(solution)/shard_map/ppermute | solution.py:39
  7.0 28.9 %collective-permute-start.2 = (bf16[448,640]{1,0:T(8,128)(2,1)S(1)}, bf16[448,640]{1,0:T(8,128)(2,1)S(1)}, u32[]{:S(2)}, u32[]{:S(2)}) collective-permute-start(bf16[448,640]{1,0:T(8,128)(2,1)S(1)} %pad_maximum_fusion.10.refs_2_.refs_3_), channel_id=1, source_target_pairs={{0,4},{1,5},{2,6},{3,7},{4,0},{5,1},{6,2},{7,3},{8,12},{9,13},{10,... | collective-permute-start | bytes 1720328 | tf_op jit(solution)/shard_map/ppermute | solution.py:39
  7.1 28.7 %collective-permute-start.3 = (bf16[32,7168]{1,0:T(8,128)(2,1)S(1)}, bf16[32,7168]{1,0:T(8,128)(2,1)S(1)}, u32[]{:S(2)}, u32[]{:S(2)}) collective-permute-start(bf16[32,7168]{1,0:T(8,128)(2,1)S(1)} %bitcast.72), channel_id=1, source_target_pairs={{0,140},{1,141},{2,142},{3,143},{4,136},{5,137},{6,138},{7,139},{8... | collective-permute-start | bytes 1376264 | tf_op jit(solution)/shard_map/ppermute | solution.py:39
  36.0 28.1 %collective-permute-start.7 = (bf16[2,32,7168]{2,1,0:T(8,128)(2,1)S(1)}, bf16[2,32,7168]{2,1,0:T(8,128)(2,1)S(1)}, u32[]{:S(2)}, u32[]{:S(2)}) collective-permute-start(bf16[2,32,7168]{2,1,0:T(8,128)(2,1)S(1)} %pad_maximum_fusion.3), channel_id=1, source_target_pairs={{0,32},{1,33},{2,34},{3,35},{4,36},{5,37},{6,38},{7,39},{8,40},{9,... | collective-permute-start | bytes 2752520 | tf_op jit(solution)/shard_map/ppermute | solution.py:39
  37.6 26.5 %collective-permute-start.8 = (bf16[2,32,7168]{2,1,0:T(8,128)(2,1)S(1)}, bf16[2,32,7168]{2,1,0:T(8,128)(2,1)S(1)}, u32[]{:S(2)}, u32[]{:S(2)}) collective-permute-start(bf16[2,32,7168]{2,1,0:T(8,128)(2,1)S(1)} %pad_maximum_fusion.3), channel_id=1, source_target_pairs={{0,96},{1,97},{2,98},{3,99},{4,100},{5,101},{6,102},{7,103},{8,104... | collective-permute-start | bytes 2752520 | tf_op jit(solution)/shard_map/ppermute | solution.py:39
  39.7 28.9 %copy-start.26 = (bf16[1536,1536]{1,0:T(8,128)(2,1)S(1)}, bf16[1536,1536]{1,0:T(8,128)(2,1)}, u32[]{:S(2)}) copy-start(bf16[1536,1536]{1,0:T(8,128)(2,1)} %param.14) | copy-start | bytes 14155780
  39.9 24.2 %collective-permute-start.4 = (bf16[672,640]{1,0:T(8,128)(2,1)S(1)}, bf16[672,640]{1,0:T(8,128)(2,1)S(1)}, u32[]{:S(2)}, u32[]{:S(2)}) collective-permute-start(bf16[672,640]{1,0:T(8,128)(2,1)S(1)} %get-tuple-element.99), channel_id=1, source_target_pairs={{0,1},{1,0},{2,3},{3,2},{4,5},{5,4},{6,7},{7,6},{8,9},{9,8},{10,11... | collective-permute-start | bytes 2580488 | tf_op jit(solution)/shard_map/ppermute | solution.py:39
  40.7 23.4 %collective-permute-start.5 = (bf16[672,640]{1,0:T(8,128)(2,1)S(1)}, bf16[672,640]{1,0:T(8,128)(2,1)S(1)}, u32[]{:S(2)}, u32[]{:S(2)}) collective-permute-start(bf16[672,640]{1,0:T(8,128)(2,1)S(1)} %get-tuple-element.98), channel_id=1, source_target_pairs={{0,3},{1,2},{2,1},{3,0},{4,7},{5,6},{6,5},{7,4},{8,11},{9,10},{10,... | collective-permute-start | bytes 2580488 | tf_op jit(solution)/shard_map/ppermute | solution.py:39
  41.6 22.5 %collective-permute-start.6 = (bf16[448,640]{1,0:T(8,128)(2,1)S(1)}, bf16[448,640]{1,0:T(8,128)(2,1)S(1)}, u32[]{:S(2)}, u32[]{:S(2)}) collective-permute-start(bf16[448,640]{1,0:T(8,128)(2,1)S(1)} %pad_maximum_fusion.10.refs_2_.refs_3_), channel_id=1, source_target_pairs={{0,8},{1,9},{2,10},{3,11},{4,12},{5,13},{6,14},{7,15},{8,0},{9,1},... | collective-permute-start | bytes 1720328 | tf_op jit(solution)/shard_map/ppermute | solution.py:39
  64.2 28.3 %collective-permute-start.12 = (bf16[2,32,7168]{2,1,0:T(8,128)(2,1)S(1)}, bf16[2,32,7168]{2,1,0:T(8,128)(2,1)S(1)}, u32[]{:S(2)}, u32[]{:S(2)}) collective-permute-start(bf16[2,32,7168]{2,1,0:T(8,128)(2,1)S(1)} %pad_maximum_fusion.3), channel_id=1, source_target_pairs={{0,64},{1,65},{2,66},{3,67},{4,68},{5,69},{6,70},{7,71},{8,72},{9,... | collective-permute-start | bytes 2752520 | tf_op jit(solution)/shard_map/ppermute | solution.py:39
  65.3 27.1 %collective-permute-start.10 = (bf16[672,640]{1,0:T(8,128)(2,1)S(1)}, bf16[672,640]{1,0:T(8,128)(2,1)S(1)}, u32[]{:S(2)}, u32[]{:S(2)}) collective-permute-start(bf16[672,640]{1,0:T(8,128)(2,1)S(1)} %get-tuple-element.96), channel_id=1, source_target_pairs={{0,3},{1,2},{2,1},{3,0},{4,7},{5,6},{6,5},{7,4},{8,11},{9,10},{10,... | collective-permute-start | bytes 2580488 | tf_op jit(solution)/shard_map/ppermute | solution.py:39
  67.5 25.0 %collective-permute-start.9 = (bf16[672,640]{1,0:T(8,128)(2,1)S(1)}, bf16[672,640]{1,0:T(8,128)(2,1)S(1)}, u32[]{:S(2)}, u32[]{:S(2)}) collective-permute-start(bf16[672,640]{1,0:T(8,128)(2,1)S(1)} %get-tuple-element.97), channel_id=1, source_target_pairs={{0,1},{1,0},{2,3},{3,2},{4,5},{5,4},{6,7},{7,6},{8,9},{9,8},{10,11... | collective-permute-start | bytes 2580488 | tf_op jit(solution)/shard_map/ppermute | solution.py:39
  67.6 24.8 %collective-permute-start.11 = (bf16[448,640]{1,0:T(8,128)(2,1)S(1)}, bf16[448,640]{1,0:T(8,128)(2,1)S(1)}, u32[]{:S(2)}, u32[]{:S(2)}) collective-permute-start(bf16[448,640]{1,0:T(8,128)(2,1)S(1)} %pad_maximum_fusion.10.refs_2_.refs_3_), channel_id=1, source_target_pairs={{0,12},{1,13},{2,14},{3,15},{4,8},{5,9},{6,10},{7,11},{8,4},{9,5},... | collective-permute-start | bytes 1720328 | tf_op jit(solution)/shard_map/ppermute | solution.py:39
  94.7 10.8 %collective-permute-start.13 = (bf16[256,7168]{1,0:T(8,128)(2,1)}, bf16[256,7168]{1,0:T(8,128)(2,1)}, u32[]{:S(2)}, u32[]{:S(2)}) collective-permute-start(bf16[256,7168]{1,0:T(8,128)(2,1)} %bitcast.12.rows_ref), channel_id=1, source_target_pairs={{0,16},{1,17},{2,18},{3,19},{4,20},{5,21},{6,22},{7,23},{8,24},{9,... | collective-permute-start | bytes 11010056 | tf_op jit(solution)/shard_map/ppermute | solution.py:39
  96.4 25.9 %collective-permute-start.14 = (bf16[672,640]{1,0:T(8,128)(2,1)}, bf16[672,640]{1,0:T(8,128)(2,1)S(1)}, u32[]{:S(2)}, u32[]{:S(2)}) collective-permute-start(bf16[672,640]{1,0:T(8,128)(2,1)} %get-tuple-element.95), channel_id=1, source_target_pairs={{0,1},{1,0},{2,3},{3,2},{4,5},{5,4},{6,7},{7,6},{8,9},{9,8},{10,11... | collective-permute-start | bytes 2580488 | tf_op jit(solution)/shard_map/ppermute | solution.py:39
  98.2 24.1 %collective-permute-start.15 = (bf16[672,640]{1,0:T(8,128)(2,1)}, bf16[672,640]{1,0:T(8,128)(2,1)S(1)}, u32[]{:S(2)}, u32[]{:S(2)}) collective-permute-start(bf16[672,640]{1,0:T(8,128)(2,1)} %get-tuple-element.94), channel_id=1, source_target_pairs={{0,3},{1,2},{2,1},{3,0},{4,7},{5,6},{6,5},{7,4},{8,11},{9,10},{10,... | collective-permute-start | bytes 2580488 | tf_op jit(solution)/shard_map/ppermute | solution.py:39
  105.5 5.9 %copy-start.2 = (bf16[256,7168]{1,0:T(8,128)(2,1)S(1)}, bf16[256,7168]{1,0:T(8,128)(2,1)}, u32[]{:S(2)}) copy-start(bf16[256,7168]{1,0:T(8,128)(2,1)} %get-tuple-element.58.refs_0_) | copy-start | bytes 11010052
  105.5 5.9 %copy-start.25 = (s32[3]{0:T(128)S(1)}, s32[3]{0:T(128)}, u32[]{:S(2)}) copy-start(s32[3]{0:T(128)} %pad_add_fusion.place_ref) | copy-start | bytes 40
  120.4 4.2 %copy-start.15 = (bf16[448,640]{1,0:T(8,128)(2,1)S(1)}, bf16[448,640]{1,0:T(8,128)(2,1)}, u32[]{:S(2)}) copy-start(bf16[448,640]{1,0:T(8,128)(2,1)} %copy-done.14) | copy-start | bytes 1720324
  122.4 8.8 %collective-permute-start.16 = (bf16[224,640]{1,0:T(8,128)(2,1)S(1)}, bf16[224,640]{1,0:T(8,128)(2,1)S(1)}, u32[]{:S(2)}, u32[]{:S(2)}) collective-permute-start(bf16[224,640]{1,0:T(8,128)(2,1)S(1)} %slice.73), channel_id=1, source_target_pairs={{0,1},{1,0},{2,3},{3,2},{4,5},{5,4},{6,7},{7,6},{8,9},{9,8},{10,11... | collective-permute-start | bytes 860168 | tf_op jit(solution)/shard_map/ppermute | solution.py:39
  122.5 10.0 %copy-start.11 = (bf16[448,640]{1,0:T(8,128)(2,1)S(1)}, bf16[448,640]{1,0:T(8,128)(2,1)}, u32[]{:S(2)}) copy-start(bf16[448,640]{1,0:T(8,128)(2,1)} %copy-done.10) | copy-start | bytes 1720324
  122.5 10.0 %collective-permute-start.17 = (bf16[224,640]{1,0:T(8,128)(2,1)S(1)}, bf16[224,640]{1,0:T(8,128)(2,1)S(1)}, u32[]{:S(2)}, u32[]{:S(2)}) collective-permute-start(bf16[224,640]{1,0:T(8,128)(2,1)S(1)} %slice.74), channel_id=1, source_target_pairs={{0,3},{1,2},{2,1},{3,0},{4,7},{5,6},{6,5},{7,4},{8,11},{9,10},{10,... | collective-permute-start | bytes 860168 | tf_op jit(solution)/shard_map/ppermute | solution.py:39
  135.7 3.5 %collective-permute-start.18 = (bf16[256,3072]{1,0:T(8,128)(2,1)S(1)}, bf16[256,3072]{1,0:T(8,128)(2,1)S(1)}, u32[]{:S(2)}, u32[]{:S(2)}) collective-permute-start(bf16[256,3072]{1,0:T(8,128)(2,1)S(1)} %project.3), channel_id=1, source_target_pairs={{0,16},{1,17},{2,18},{3,19},{4,20},{5,21},{6,22},{7,23},{8,24},{9,... | collective-permute-start | bytes 4718600 | tf_op jit(solution)/shard_map/ppermute | solution.py:39
  139.6 13.4 %collective-permute-start.22 = (bf16[448,512]{1,0:T(8,128)(2,1)S(1)}, bf16[448,512]{1,0:T(8,128)(2,1)S(1)}, u32[]{:S(2)}, u32[]{:S(2)}) collective-permute-start(bf16[448,512]{1,0:T(8,128)(2,1)S(1)} %get-tuple-element.78), channel_id=1, source_target_pairs={{0,1},{1,0},{2,3},{3,2},{4,5},{5,4},{6,7},{7,6},{8,9},{9,8},{10,11... | collective-permute-start | bytes 1376264 | tf_op jit(solution)/shard_map/ppermute | solution.py:39
  140.2 23.5 %collective-permute-start.23 = (bf16[448,512]{1,0:T(8,128)(2,1)S(1)}, bf16[448,512]{1,0:T(8,128)(2,1)S(1)}, u32[]{:S(2)}, u32[]{:S(2)}) collective-permute-start(bf16[448,512]{1,0:T(8,128)(2,1)S(1)} %get-tuple-element.78), channel_id=1, source_target_pairs={{0,2},{1,3},{2,0},{3,1},{4,6},{5,7},{6,4},{7,5},{8,10},{9,11},{10,... | collective-permute-start | bytes 1376264 | tf_op jit(solution)/shard_map/ppermute | solution.py:39
  143.2 23.0 %collective-permute-start.24 = (bf16[448,512]{1,0:T(8,128)(2,1)S(1)}, bf16[448,512]{1,0:T(8,128)(2,1)S(1)}, u32[]{:S(2)}, u32[]{:S(2)}) collective-permute-start(bf16[448,512]{1,0:T(8,128)(2,1)S(1)} %get-tuple-element.78), channel_id=1, source_target_pairs={{0,3},{1,2},{2,1},{3,0},{4,7},{5,6},{6,5},{7,4},{8,11},{9,10},{10,... | collective-permute-start | bytes 1376264 | tf_op jit(solution)/shard_map/ppermute | solution.py:39
  144.7 21.8 %collective-permute-start.19 = (bf16[2,32,3072]{2,1,0:T(8,128)(2,1)S(1)}, bf16[2,32,3072]{2,1,0:T(8,128)(2,1)S(1)}, u32[]{:S(2)}, u32[]{:S(2)}) collective-permute-start(bf16[2,32,3072]{2,1,0:T(8,128)(2,1)S(1)} %get-tuple-element.90), channel_id=1, source_target_pairs={{0,32},{1,33},{2,34},{3,35},{4,36},{5,37},{6,38},{7,39},{8,40},{9,... | collective-permute-start | bytes 1179656 | tf_op jit(solution)/shard_map/ppermute | solution.py:39
  146.1 20.4 %collective-permute-start.20 = (bf16[2,32,3072]{2,1,0:T(8,128)(2,1)S(1)}, bf16[2,32,3072]{2,1,0:T(8,128)(2,1)S(1)}, u32[]{:S(2)}, u32[]{:S(2)}) collective-permute-start(bf16[2,32,3072]{2,1,0:T(8,128)(2,1)S(1)} %get-tuple-element.89), channel_id=1, source_target_pairs={{0,64},{1,65},{2,66},{3,67},{4,68},{5,69},{6,70},{7,71},{8,72},{9,... | collective-permute-start | bytes 1179656 | tf_op jit(solution)/shard_map/ppermute | solution.py:39
  153.1 19.2 %collective-permute-start.21 = (bf16[2,32,3072]{2,1,0:T(8,128)(2,1)S(1)}, bf16[2,32,3072]{2,1,0:T(8,128)(2,1)S(1)}, u32[]{:S(2)}, u32[]{:S(2)}) collective-permute-start(bf16[2,32,3072]{2,1,0:T(8,128)(2,1)S(1)} %get-tuple-element.88), channel_id=1, source_target_pairs={{0,96},{1,97},{2,98},{3,99},{4,100},{5,101},{6,102},{7,103},{8,104... | collective-permute-start | bytes 1179656 | tf_op jit(solution)/shard_map/ppermute | solution.py:39
  166.5 14.7 %copy-start.23 = (bf16[128,1536]{1,0:T(8,128)(2,1)S(1)}, bf16[128,1536]{1,0:T(8,128)(2,1)}, u32[]{:S(2)}) copy-start(bf16[128,1536]{1,0:T(8,128)(2,1)} %convolution_convert_fusion.q_ref) | copy-start | bytes 1179652
  166.5 14.7 %copy-start.24 = (bf16[1,128,1536]{2,1,0:T(8,128)(2,1)S(1)}, bf16[1,128,1536]{2,1,0:T(8,128)(2,1)}, u32[]{:S(2)}) copy-start(bf16[1,128,1536]{2,1,0:T(8,128)(2,1)} %param.15) | copy-start | bytes 1179652
  172.4 8.8 %collective-permute-start.25 = (bf16[32,3072]{1,0:T(8,128)(2,1)S(1)}, bf16[32,3072]{1,0:T(8,128)(2,1)S(1)}, u32[]{:S(2)}, u32[]{:S(2)}) collective-permute-start(bf16[32,3072]{1,0:T(8,128)(2,1)S(1)} %fusion.3), channel_id=1, source_target_pairs={{0,140},{1,141},{2,142},{3,143},{4,136},{5,137},{6,138},{7,139},{8... | collective-permute-start | bytes 589832 | tf_op jit(solution)/shard_map/ppermute | solution.py:39
  184.6 4.8 %collective-permute-start.26 = (bf16[32,768]{1,0:T(8,128)(2,1)S(1)}, bf16[32,768]{1,0:T(8,128)(2,1)S(1)}, u32[]{:S(2)}, u32[]{:S(2)}) collective-permute-start(bf16[32,768]{1,0:T(8,128)(2,1)S(1)} %get-tuple-element.107), channel_id=1, source_target_pairs={{0,1},{1,0},{2,3},{3,2},{4,5},{5,4},{6,7},{7,6},{8,9},{9,8},{10,11... | collective-permute-start | bytes 147464 | tf_op jit(solution)/shard_map/ppermute | solution.py:39
  184.7 6.1 %collective-permute-start.27 = (bf16[32,768]{1,0:T(8,128)(2,1)S(1)}, bf16[32,768]{1,0:T(8,128)(2,1)S(1)}, u32[]{:S(2)}, u32[]{:S(2)}) collective-permute-start(bf16[32,768]{1,0:T(8,128)(2,1)S(1)} %get-tuple-element.106), channel_id=1, source_target_pairs={{0,2},{1,3},{2,0},{3,1},{4,6},{5,7},{6,4},{7,5},{8,10},{9,11},{10,... | collective-permute-start | bytes 147464 | tf_op jit(solution)/shard_map/ppermute | solution.py:39
  188.2 5.3 %collective-permute-start.28 = (bf16[32,768]{1,0:T(8,128)(2,1)S(1)}, bf16[32,768]{1,0:T(8,128)(2,1)S(1)}, u32[]{:S(2)}, u32[]{:S(2)}) collective-permute-start(bf16[32,768]{1,0:T(8,128)(2,1)S(1)} %get-tuple-element.105), channel_id=1, source_target_pairs={{0,3},{1,2},{2,1},{3,0},{4,7},{5,6},{6,5},{7,4},{8,11},{9,10},{10,... | collective-permute-start | bytes 147464 | tf_op jit(solution)/shard_map/ppermute | solution.py:39
  193.5 8.8 %collective-permute-start.29 = (bf16[4,32,768]{2,1,0:T(8,128)(2,1)S(1)}, bf16[4,32,768]{2,1,0:T(8,128)(2,1)S(1)}, u32[]{:S(2)}, u32[]{:S(2)}) collective-permute-start(bf16[4,32,768]{2,1,0:T(8,128)(2,1)S(1)} %get-tuple-element.103), channel_id=1, source_target_pairs={{0,140},{1,141},{2,142},{3,143},{4,136},{5,137},{6,138},{7,139},{8... | collective-permute-start | bytes 589832 | tf_op jit(solution)/shard_map/ppermute | solution.py:39
  202.4 10.2 %collective-permute-start.30 = (bf16[2,4,32,768]{3,2,1,0:T(8,128)(2,1)S(1)}, bf16[2,4,32,768]{3,2,1,0:T(8,128)(2,1)S(1)}, u32[]{:S(2)}, u32[]{:S(2)}) collective-permute-start(bf16[2,4,32,768]{3,2,1,0:T(8,128)(2,1)S(1)} %get-tuple-element.101), channel_id=1, source_target_pairs={{0,32},{1,33},{2,34},{3,35},{4,36},{5,37},{6,38},{7,39},{8,40},{9,... | collective-permute-start | bytes 1179656 | tf_op jit(solution)/shard_map/ppermute | solution.py:39
  202.5 15.6 %collective-permute-start.31 = (bf16[2,4,32,768]{3,2,1,0:T(8,128)(2,1)S(1)}, bf16[2,4,32,768]{3,2,1,0:T(8,128)(2,1)S(1)}, u32[]{:S(2)}, u32[]{:S(2)}) collective-permute-start(bf16[2,4,32,768]{3,2,1,0:T(8,128)(2,1)S(1)} %get-tuple-element.101), channel_id=1, source_target_pairs={{0,64},{1,65},{2,66},{3,67},{4,68},{5,69},{6,70},{7,71},{8,72},{9,... | collective-permute-start | bytes 1179656 | tf_op jit(solution)/shard_map/ppermute | solution.py:39
  205.6 15.0 %collective-permute-start.32 = (bf16[2,4,32,768]{3,2,1,0:T(8,128)(2,1)S(1)}, bf16[2,4,32,768]{3,2,1,0:T(8,128)(2,1)S(1)}, u32[]{:S(2)}, u32[]{:S(2)}) collective-permute-start(bf16[2,4,32,768]{3,2,1,0:T(8,128)(2,1)S(1)} %get-tuple-element.101), channel_id=1, source_target_pairs={{0,96},{1,97},{2,98},{3,99},{4,100},{5,101},{6,102},{7,103},{8,104... | collective-permute-start | bytes 1179656 | tf_op jit(solution)/shard_map/ppermute | solution.py:39
  220.7 3.5 %collective-permute-start.33 = (bf16[4,2,4,32,768]{4,3,2,1,0:T(8,128)(2,1)S(1)}, bf16[4,2,4,32,768]{4,3,2,1,0:T(8,128)(2,1)S(1)}, u32[]{:S(2)}, u32[]{:S(2)}) collective-permute-start(bf16[4,2,4,32,768]{4,3,2,1,0:T(8,128)(2,1)S(1)} %pad_maximum_fusion.2.a_ref), channel_id=1, source_target_pairs={{0,16},{1,17},{2,18},{3,19},{4,20},{5,21},{6,22},{7,23},{8,24},{9,... | collective-permute-start | bytes 4718600 | tf_op jit(solution)/shard_map/ppermute | solution.py:39
  224.2 25.7 %copy-start.1 = (bf16[1,128,1536]{2,1,0:T(8,128)(2,1)S(1)}, bf16[1,128,1536]{2,1,0:T(8,128)(2,1)}, u32[]{:S(2)}) copy-start(bf16[1,128,1536]{2,1,0:T(8,128)(2,1)} %param.10) | copy-start | bytes 1179652
  228.2 8.3 %collective-permute-start.34 = (bf16[192,448]{1,0:T(8,128)(2,1)S(1)}, bf16[192,448]{1,0:T(8,128)(2,1)S(1)}, u32[]{:S(2)}, u32[]{:S(2)}) collective-permute-start(bf16[192,448]{1,0:T(8,128)(2,1)S(1)} %get-tuple-element.91), channel_id=1, source_target_pairs={{0,4},{1,5},{2,6},{3,7},{4,0},{5,1},{6,2},{7,3},{8,12},{9,13},{10,... | collective-permute-start | bytes 516104 | tf_op jit(solution)/shard_map/ppermute | solution.py:39
  228.3 16.5 %collective-permute-start.35 = (bf16[192,448]{1,0:T(8,128)(2,1)S(1)}, bf16[192,448]{1,0:T(8,128)(2,1)S(1)}, u32[]{:S(2)}, u32[]{:S(2)}) collective-permute-start(bf16[192,448]{1,0:T(8,128)(2,1)S(1)} %get-tuple-element.93), channel_id=1, source_target_pairs={{0,8},{1,9},{2,10},{3,11},{4,12},{5,13},{6,14},{7,15},{8,0},{9,1},... | collective-permute-start | bytes 516104 | tf_op jit(solution)/shard_map/ppermute | solution.py:39
  231.1 18.1 %collective-permute-start.36 = (bf16[192,448]{1,0:T(8,128)(2,1)S(1)}, bf16[192,448]{1,0:T(8,128)(2,1)S(1)}, u32[]{:S(2)}, u32[]{:S(2)}) collective-permute-start(bf16[192,448]{1,0:T(8,128)(2,1)S(1)} %get-tuple-element.92), channel_id=1, source_target_pairs={{0,12},{1,13},{2,14},{3,15},{4,8},{5,9},{6,10},{7,11},{8,4},{9,5},... | collective-permute-start | bytes 516104 | tf_op jit(solution)/shard_map/ppermute | solution.py:39
  (17 other events, 35.0 us)

commit v4 on v3

--- a/solution.py
+++ b/solution.py
@@ -77,15 +77,15 @@
             jax.ShapeDtypeStruct((height, width), bf16),
             jax.ShapeDtypeStruct((height, depth), bf16),
         ],
-        compiler_params=params(56),
+        compiler_params=params(12),
         name="norm",
     )(place, rows)
 
 
 def layer_kernel(place_ref, *refs, finish):
-    normed_refs, piece_refs = refs[:2], refs[2:10]
-    resid_refs, acc_ref = refs[10:12], refs[12]
-    kvw_ref, *out_refs, weights = refs[13:]
+    normed_refs, piece_refs = refs[:4], refs[4:12]
+    resid_refs, acc_ref = refs[12:16], refs[16]
+    kvw_ref, *out_refs, weights = refs[17:]
     y = place_ref[2]
     out = acc_ref.shape[1]
     half = piece_refs[0].shape[0]
@@ -96,20 +96,16 @@
     kvw_ref[...] = jnp.concatenate(
         [weights[f * depth : (f + 1) * depth, out:] for f in range(4)], axis=1
     )
-    rows = normed_refs[0].shape[0]
-    for i, (normed_ref, resid_ref) in enumerate(zip(normed_refs, resid_refs)):
-        at = slice(i * rows, (i + 1) * rows)
-        total = acc_ref[at] + jnp.dot(
-            normed_ref[...], weights[:, :out], preferred_element_type=f32
-        )
-        if finish:
-            feature_ref, featt_ref = out_refs
-            silu = total / (1.0 + jnp.exp(-total))
-            feature = (resid_ref[...].astype(f32) + silu).astype(bf16)
-            feature_ref[at] = feature
-            featt_ref[:, at] = feature.T
-        else:
-            out_refs[0][at] = total
+    normed = jnp.concatenate([ref[...] for ref in normed_refs], axis=0)
+    total = acc_ref[...] + jnp.dot(normed, weights[:, :out], preferred_element_type=f32)
+    if finish:
+        feature_ref, featt_ref = out_refs
+        resid = jnp.concatenate([ref[...] for ref in resid_refs], axis=0).astype(f32)
+        feature = (resid + total / (1.0 + jnp.exp(-total))).astype(bf16)
+        feature_ref[...] = feature
+        featt_ref[...] = feature.T
+    else:
+        out_refs[0][...] = total
 
 
 def layer(place, normed, pieces, resid, acc, e, finish):
@@ -133,9 +129,9 @@
             num_scalar_prefetch=1,
             grid=(1,),
             in_specs=[
-                pl.BlockSpec((rows // 2, 4 * depth), lambda i, place: (0, place[1] ^ e)),
+                pl.BlockSpec((rows // 4, 4 * depth), lambda i, place: (0, place[1] ^ e)),
             ]
-            * 2
+            * 4
             + [
                 pl.BlockSpec((half, wide), lambda i, place, at=at: (at, 0)) for _, at in pieces
             ]
@@ -145,7 +141,7 @@
             scratch_shapes=[pltpu.VMEM((4 * depth, wide), bf16)],
         ),
         out_shape=[jax.ShapeDtypeStruct(shape, dtype) for shape, dtype in shapes],
-        compiler_params=params(32),
+        compiler_params=params(24),
         name="layer",
     )(place, *normed, *[array for array, _ in pieces], *resid, acc)
 
@@ -169,7 +165,7 @@
         + [pl.BlockSpec((depth, kv), lambda i: (0, 0))] * 4,
         out_specs=pl.BlockSpec((rows, 4 * kv), lambda i: (0, 0)),
         out_shape=jax.ShapeDtypeStruct((rows, 4 * kv), dtype),
-        compiler_params=params(20),
+        compiler_params=params(16),
         name="project",
     )(feature, *weights)
 
@@ -260,7 +256,8 @@
     step = pl.program_id(0)
     l, y = place_ref[1], place_ref[2]
     wide = acc.shape[1]
-    grads = jnp.concatenate([ref[:, :, 0].reshape(-1, wide) for ref in (a_ref, b_ref)], axis=0)
+    packed = [ref[:, m, 0] for ref in (a_ref, b_ref) for m in range(2)]
+    grads = jnp.concatenate(packed, axis=0).reshape(-1, wide)
     term = jnp.dot(featt_ref[0], grads, preferred_element_type=f32)
 
     @pl.when(step == 0)
@@ -332,27 +329,41 @@
             low, high = jnp.concatenate([low, w]), jnp.concatenate([high, w])
         return send(low, ALONG_Y[1]), send(high, ALONG_Y[3])
 
+    def along_x(rows, e):
+        return send(rows, ALONG_X[e])
+
     rows = vlm_rows[0]
     y0 = send(block, ALONG_Y[1]), send(block, ALONG_Y[3])
-    z1, mirrored = send(block, ALONG_Z[1]), send(rows, MIRROR)
-    y0, z1, mirrored, block = lax.optimization_barrier((y0, z1, mirrored, block))
-
-    rows = jnp.stack([rows, mirrored])
+    z1, own1, own3 = send(block, ALONG_Z[1]), along_x(rows, 1), along_x(rows, 3)
+    y0, z1, own1, own3, block, rows = lax.optimization_barrier(
+        (y0, z1, own1, own3, block, rows)
+    )
+
     y1, z2 = around(y0, z1), send(block, ALONG_Z[2])
-    x1, x3 = send(rows, ALONG_X[1]), send(rows, ALONG_X[3])
-    y1, z2, x1, x3, block, rows = lax.optimization_barrier((y1, z2, x1, x3, block, rows))
+    mirrored, own2 = send(rows, MIRROR), along_x(rows, 2)
+    y1, z2, mirrored, own2, block = lax.optimization_barrier((y1, z2, mirrored, own2, block))
 
     y2, z3 = around(y1, z2), send(block, ALONG_Z[3])
-    x2 = send(rows, ALONG_X[2])
+    far1, far3 = along_x(mirrored, 1), along_x(mirrored, 3)
+    own_a = jnp.concatenate([rows, own1, own2, own3])
     queries = lax.dot_general(
         action_hidden[0], query_weight, (((1,), (1,)), ((), ())), preferred_element_type=f32
     ).astype(bf16)
-    y2, z3, x2, queries = lax.optimization_barrier((y2, z3, x2, queries))
-
-    y3 = around(y2, z3)
-    rows_a = jnp.stack([rows, x1, x2, x3]).reshape(-1, width)
-    rows_b = send(rows_a, CORE)
-    normed, resid = zip(normalize(rows_a, place), normalize(rows_b, place))
+    own_a_normed = normalize(own_a, place)
+    y2, z3, far1, far3, mirrored, queries, own_a, own_a_normed = lax.optimization_barrier(
+        (y2, z3, far1, far3, mirrored, queries, own_a, own_a_normed)
+    )
+
+    y3, far2 = around(y2, z3), along_x(mirrored, 2)
+    own_b = send(own_a, CORE)
+    own_b_normed = normalize(own_b, place)
+    y3, far2, own_b_normed = lax.optimization_barrier((y3, far2, own_b_normed))
+
+    y4 = around(y3, None)
+    far_a = jnp.concatenate([mirrored, far1, far2, far3])
+    far_b = send(far_a, CORE)
+    sets = (own_a_normed, normalize(far_a, place), own_b_normed, normalize(far_b, place))
+    normed, resid = zip(*sets)
     acc = jnp.zeros((16 * slot_rows, vlm_weight.shape[0]), f32)
     kv_weights = []
 
@@ -366,31 +377,31 @@
 
     (acc,) = add(0, block, y0, y1, acc)
     (acc,) = add(1, z1, y1, y2, acc)
-    y3, acc = lax.optimization_barrier((y3, acc))
-
-    y4 = around(y3, None)
     (acc,) = add(2, z2, y2, y3, acc)
     feature, featt = add(3, z3, y3, y4, acc)
 
     part_b = project(feature, 1, kv_weights, bf16)
     swapped = send(part_b, CORE)
     part_a = project(feature, 0, kv_weights, f32)
-    both = (part_a + swapped.astype(f32)).reshape(4, 2, slot_rows, 2 * width_act)
-    both, featt = lax.optimization_barrier((both, featt))
-    sums = [send(both[e].astype(bf16), ALONG_X[e]) for e in (1, 2, 3)]
-    featt_all = gather_along(featt, ALONG_Y)
-    sums, featt_all = lax.optimization_barrier((sums, featt_all))
-    mine = both[0]
-    for term in sums:
-        mine = mine + term.astype(f32)
+    both = (part_a + swapped.astype(f32)).reshape(2, 4, slot_rows, 2 * width_act)
+    mine = both[:, 0]
+    for e in (1, 2, 3):
+        mine = mine + send(both[:, e].astype(bf16), ALONG_X[e]).astype(f32)
+    mine, featt = lax.optimization_barrier((mine, featt))
     other = send(mine[1].astype(bf16), MIRROR)
+    feat1, feat3 = send(featt, ALONG_Y[1]), send(featt, ALONG_Y[3])
+    other, feat1, feat3, featt = lax.optimization_barrier((other, feat1, feat3, featt))
 
     context, grads = attention(
         mine[0], other, queries, images, lengths, context_grad[0], place
     )
 
     by_y = jnp.stack([grads[0]] + [send(grads[e], ALONG_Y[e]) for e in (1, 2, 3)])
-    grads_a = gather_along(jnp.stack([by_y, send(by_y, MIRROR)]), ALONG_X)
+    by_y, featt = lax.optimization_barrier((by_y, featt))
+    far, feat2 = send(by_y, MIRROR), send(featt, ALONG_Y[2])
+    far, feat2 = lax.optimization_barrier((far, feat2))
+    featt_all = jnp.stack([featt, feat1, feat2, feat3])
+    grads_a = gather_along(jnp.stack([by_y, far]), ALONG_X)
     grads_b = send(grads_a, CORE)
     kv_weight_grad, sums = weight_grad(grads_a, grads_b, featt_all, place)
     for e in (1, 2, 3):

time: 250 us -> 247 us (0.988); the launches traced: 250 us -> 243 us
  starting transfers between devices: 52.4 us -> 63 us
  local copies, waits for them, and re-layouts: 10.3 us -> 5.22 us
  waiting for transfers between devices: 147 us -> 142 us
  Pallas kernels: 28.3 us -> 23.6 us
  other arithmetic: 7.06 us -> 2.63 us
    ppermute x37 -> x41, starting transfers between devices: 52.4 us -> 63 us  [send(): return lax.ppermute(array, AXES, table)]
    unnamed x58 -> x16, local copies, waits for them, and re-layouts: 9.75 us -> 3.57 us
    ppermute x37 -> x41, waiting for transfers between devices: 147 us -> 142 us  [send(): return lax.ppermute(array, AXES, table)]
    pallas_call x2 -> x4, Pallas kernels: 11.2 us -> 6.53 us  [normalize(): pl.pallas_call(norm_kernel, grid=(height // per,), in_specs=[pl.BlockSpec...]
  transfers between devices with their start and end apart: 37 -> 41, of which waited for: 21 -> 28; matrix products, arithmetic and copies ran while one was open for 2% -> 3% of each run, Pallas kernels for 7% -> 5%
where the time goes in v4:
time: 247 us; the launch traced here: 243 us
  waiting for transfers between devices  142 us (57%)
  starting transfers between devices  63 us (26%)
  Pallas kernels  23.6 us (10%)
  local copies, waits for them, and re-layouts  5.22 us (2%)
  matrix products  3.97 us (2%)
  other arithmetic  2.63 us (1%)
  between operations  2.53 us (1%)
    ppermute x41, waiting for transfers between devices, send(): return lax.ppermute(array, AXES, table)  142 us
    ppermute x41, starting transfers between devices, send(): return lax.ppermute(array, AXES, table)  63 us
    pallas_call x4, Pallas kernels, layer(): pl.pallas_call(functools.partial(layer_kernel, finish=finish), grid_spec=...  7.79 us
    pallas_call x4, Pallas kernels, normalize(): pl.pallas_call(norm_kernel, grid=(height // per,), in_specs=[pl.BlockSpec...  6.53 us
  transfers between devices with their start and end apart: 41, of which 28 were waited for; matrix products, arithmetic and copies ran while one was open for 3% of the time, Pallas kernels for 5%

profile of v4, /device:TPU:32, one launch (start us, length us, event | category | flops | bytes accessed | tf_op | source)
XLA Modules:
  0.0 242.6 jit_solution(4420781442548284000)
XLA Ops:
  3.2 1.7 collective-permute-start
  4.8 2.2 collective-permute-start.1
  8.6 2.1 collective-permute-start.4
  10.8 4.0 %convolution_convert_fusion.q_ref = bf16[128,1536]{1,0:T(8,128)(2,1)S(1)} fusion(bf16[1536,1536]{1,0:T(8,128)(2,1)} %param.14, bf16[1,128,1536]{2,1,0:T(8,128)(2,1)S(1)} %copy-done), kind=kOutput, calls=%fused_computation.1 | convolution fusion | flops 604176384 | bytes 5505024 | tf_op jit(solution)/shard_map/dot_general | solution.py:349
  14.8 4.1 %collective-permute-done.3 = bf16[32,7168]{1,0:T(8,128)(2,1)} collective-permute-done((bf16[32,7168]{1,0:T(8,128)(2,1)S(1)}, bf16[32,7168]{1,0:T(8,128)(2,1)}, u32[]{:S(2)}, u32[]{:S(2)}) %collective-permute-start.3) | collective-permute-done | bytes 458784 | tf_op jit(solution)/shard_map/ppermute | solution.py:39
  18.8 2.4 collective-permute-done.4
  21.2 6.7 %collective-permute-start.8 = (bf16[32,7168]{1,0:T(8,128)(2,1)S(1)}, bf16[32,7168]{1,0:T(8,128)(2,1)S(1)}, u32[]{:S(2)}, u32[]{:S(2)}) collective-permute-start(bf16[32,7168]{1,0:T(8,128)(2,1)S(1)} %bitcast.69), channel_id=1, source_target_pairs={{0,140},{1,141},{2,142},{3,143},{4,136},{5,137},{6,138},{7,139},{8... | collective-permute-start | bytes 1376264 | tf_op jit(solution)/shard_map/ppermute | solution.py:39
  27.9 2.1 collective-permute-start.9
  33.6 11.6 %collective-permute-done.8 = bf16[32,7168]{1,0:T(8,128)(2,1)S(1)} collective-permute-done((bf16[32,7168]{1,0:T(8,128)(2,1)S(1)}, bf16[32,7168]{1,0:T(8,128)(2,1)S(1)}, u32[]{:S(2)}, u32[]{:S(2)}) %collective-permute-start.8) | collective-permute-done | bytes 458784 | tf_op jit(solution)/shard_map/ppermute | solution.py:39
  45.2 9.9 %collective-permute-done.7.refs_4_.refs_5_ = bf16[448,640]{1,0:T(8,128)(2,1)S(1)} collective-permute-done((bf16[448,640]{1,0:T(8,128)(2,1)S(1)}, bf16[448,640]{1,0:T(8,128)(2,1)S(1)}, u32[]{:S(2)}, u32[]{:S(2)}) %collective-permute-start.7) | collective-permute-done | bytes 573472 | tf_op jit(solution)/shard_map/ppermute | solution.py:39
  57.7 1.6 collective-permute-start.11
  61.4 1.6 norm.4
  63.1 3.1 %collective-permute-done.13 = bf16[32,7168]{1,0:T(8,128)(2,1)S(1)} collective-permute-done((bf16[32,7168]{1,0:T(8,128)(2,1)S(1)}, bf16[32,7168]{1,0:T(8,128)(2,1)S(1)}, u32[]{:S(2)}, u32[]{:S(2)}) %collective-permute-start.13) | collective-permute-done | bytes 458784 | tf_op jit(solution)/shard_map/ppermute | solution.py:39
  66.2 1.6 collective-permute-done.14
  67.8 16.4 %collective-permute-done.12.refs_4_.refs_5_ = bf16[448,640]{1,0:T(8,128)(2,1)S(1)} collective-permute-done((bf16[448,640]{1,0:T(8,128)(2,1)S(1)}, bf16[448,640]{1,0:T(8,128)(2,1)S(1)}, u32[]{:S(2)}, u32[]{:S(2)}) %collective-permute-start.12) | collective-permute-done | bytes 573472 | tf_op jit(solution)/shard_map/ppermute | solution.py:39
  86.9 2.6 %collective-permute-start.17 = (bf16[32,7168]{1,0:T(8,128)(2,1)S(1)}, bf16[32,7168]{1,0:T(8,128)(2,1)S(1)}, u32[]{:S(2)}, u32[]{:S(2)}) collective-permute-start(bf16[32,7168]{1,0:T(8,128)(2,1)S(1)} %collective-permute-done.8), channel_id=1, source_target_pairs={{0,64},{1,65},{2,66},{3,67},{4,68},{5,69},{6,70},{7,71},{8,72},{9,... | collective-permute-start | bytes 1376264 | tf_op jit(solution)/shard_map/ppermute | solution.py:39
  89.6 1.6 norm.5
  91.2 9.6 %collective-permute-done.17 = bf16[32,7168]{1,0:T(8,128)(2,1)S(1)} collective-permute-done((bf16[32,7168]{1,0:T(8,128)(2,1)S(1)}, bf16[32,7168]{1,0:T(8,128)(2,1)S(1)}, u32[]{:S(2)}, u32[]{:S(2)}) %collective-permute-start.17) | collective-permute-done | bytes 458784 | tf_op jit(solution)/shard_map/ppermute | solution.py:39
  100.8 5.6 %collective-permute-done.15.refs_8_.refs_6_.refs_7_ = bf16[672,640]{1,0:T(8,128)(2,1)S(1)} collective-permute-done((bf16[672,640]{1,0:T(8,128)(2,1)S(1)}, bf16[672,640]{1,0:T(8,128)(2,1)S(1)}, u32[]{:S(2)}, u32[]{:S(2)}) %collective-permute-start.15) | collective-permute-done | bytes 860192 | tf_op jit(solution)/shard_map/ppermute | solution.py:39
  108.4 1.8 collective-permute-start.21
  111.9 1.6 norm.7
  113.7 1.9 layer.4
  115.5 1.9 layer.5
  117.4 1.9 layer.6
  119.3 2.2 layer.7
  123.9 2.1 collective-permute-done.22
  126.6 10.5 %collective-permute-start.23 = (bf16[2,32,3072]{2,1,0:T(8,128)(2,1)S(1)}, bf16[2,32,3072]{2,1,0:T(8,128)(2,1)S(1)}, u32[]{:S(2)}, u32[]{:S(2)}) collective-permute-start(bf16[2,32,3072]{2,1,0:T(8,128)(2,1)S(1)} %get-tuple-element.120), channel_id=1, source_target_pairs={{0,32},{1,33},{2,34},{3,35},{4,36},{5,37},{6,38},{7,39},{8,40},{9,... | collective-permute-start | bytes 1179656 | tf_op jit(solution)/shard_map/ppermute | solution.py:39
  137.0 2.8 %collective-permute-start.24 = (bf16[2,32,3072]{2,1,0:T(8,128)(2,1)S(1)}, bf16[2,32,3072]{2,1,0:T(8,128)(2,1)S(1)}, u32[]{:S(2)}, u32[]{:S(2)}) collective-permute-start(bf16[2,32,3072]{2,1,0:T(8,128)(2,1)S(1)} %get-tuple-element.122), channel_id=1, source_target_pairs={{0,64},{1,65},{2,66},{3,67},{4,68},{5,69},{6,70},{7,71},{8,72},{9,... | collective-permute-start | bytes 1179656 | tf_op jit(solution)/shard_map/ppermute | solution.py:39
  142.0 5.9 %collective-permute-done.23 = bf16[2,32,3072]{2,1,0:T(8,128)(2,1)S(1)} collective-permute-done((bf16[2,32,3072]{2,1,0:T(8,128)(2,1)S(1)}, bf16[2,32,3072]{2,1,0:T(8,128)(2,1)S(1)}, u32[]{:S(2)}, u32[]{:S(2)}) %collective-permute-start.23) | collective-permute-done | bytes 393248 | tf_op jit(solution)/shard_map/ppermute | solution.py:39
  147.9 9.6 %collective-permute-done.24 = bf16[2,32,3072]{2,1,0:T(8,128)(2,1)S(1)} collective-permute-done((bf16[2,32,3072]{2,1,0:T(8,128)(2,1)S(1)}, bf16[2,32,3072]{2,1,0:T(8,128)(2,1)S(1)}, u32[]{:S(2)}, u32[]{:S(2)}) %collective-permute-start.24) | collective-permute-done | bytes 393248 | tf_op jit(solution)/shard_map/ppermute | solution.py:39
  157.6 2.6 %collective-permute-done.25 = bf16[2,32,3072]{2,1,0:T(8,128)(2,1)S(1)} collective-permute-done((bf16[2,32,3072]{2,1,0:T(8,128)(2,1)S(1)}, bf16[2,32,3072]{2,1,0:T(8,128)(2,1)S(1)}, u32[]{:S(2)}, u32[]{:S(2)}) %collective-permute-start.25) | collective-permute-done | bytes 393248 | tf_op jit(solution)/shard_map/ppermute | solution.py:39
  161.4 1.7 collective-permute-start.28
  164.0 8.0 %collective-permute-done.26.other_ref = bf16[32,3072]{1,0:T(8,128)(2,1)S(1)} collective-permute-done((bf16[32,3072]{1,0:T(8,128)(2,1)S(1)}, bf16[32,3072]{1,0:T(8,128)(2,1)S(1)}, u32[]{:S(2)}, u32[]{:S(2)}) %collective-permute-start.26) | collective-permute-done | bytes 196640 | tf_op jit(solution)/shard_map/ppermute | solution.py:39
  173.6 3.4 %attention.1 = (bf16[128,1536]{1,0:T(8,128)(2,1)}, bf16[4,32,768]{2,1,0:T(8,128)(2,1)S(1)}) custom-call(s32[3]{0:T(128)S(1)} %pad_add_fusion.place_ref, s32[1]{0:T(128)S(6)} %copy.28.images_ref, s32[1]{0:T(128)S(6)} %copy.29.lengths_ref, f32[32,3072]{1,0:T(8,128)S(1)} %slice_bitcast_fusion.4.own_ref, bf16[32,3072]{1,0:T(8,128)(2,1)S(1)} %collective-permute-done.26.other_ref, ...), custom_call_target="tpu_custom_call" | custom-call | tf_op jit(solution)/shard_map/attention/pallas_call | solution.py:241
  177.1 3.2 %collective-permute-start.30 = (bf16[32,768]{1,0:T(8,128)(2,1)S(1)}, bf16[32,768]{1,0:T(8,128)(2,1)S(1)}, u32[]{:S(2)}, u32[]{:S(2)}) collective-permute-start(bf16[32,768]{1,0:T(8,128)(2,1)S(1)} %get-tuple-element.136), channel_id=1, source_target_pairs={{0,2},{1,3},{2,0},{3,1},{4,6},{5,7},{6,4},{7,5},{8,10},{9,11},{10,... | collective-permute-start | bytes 147464 | tf_op jit(solution)/shard_map/ppermute | solution.py:39
  182.8 2.7 %collective-permute-done.31 = bf16[32,768]{1,0:T(8,128)(2,1)S(1)} collective-permute-done((bf16[32,768]{1,0:T(8,128)(2,1)S(1)}, bf16[32,768]{1,0:T(8,128)(2,1)S(1)}, u32[]{:S(2)}, u32[]{:S(2)}) %collective-permute-start.31) | collective-permute-done | bytes 49184 | tf_op jit(solution)/shard_map/ppermute | solution.py:39
  186.6 8.0 %collective-permute-done.32 = bf16[4,32,768]{2,1,0:T(8,128)(2,1)S(1)} collective-permute-done((bf16[4,32,768]{2,1,0:T(8,128)(2,1)S(1)}, bf16[4,32,768]{2,1,0:T(8,128)(2,1)S(1)}, u32[]{:S(2)}, u32[]{:S(2)}) %collective-permute-start.32) | collective-permute-done | bytes 196640 | tf_op jit(solution)/shard_map/ppermute | solution.py:39
  195.8 2.4 collective-permute-start.35
  198.2 2.3 collective-permute-start.36
  200.5 5.3 %collective-permute-done.34 = bf16[2,4,32,768]{3,2,1,0:T(8,128)(2,1)S(1)} collective-permute-done((bf16[2,4,32,768]{3,2,1,0:T(8,128)(2,1)S(1)}, bf16[2,4,32,768]{3,2,1,0:T(8,128)(2,1)S(1)}, u32[]{:S(2)}, u32[]{:S(2)}) %collective-permute-start.34) | collective-permute-done | bytes 393248 | tf_op jit(solution)/shard_map/ppermute | solution.py:39
  205.8 4.7 %collective-permute-done.35 = bf16[2,4,32,768]{3,2,1,0:T(8,128)(2,1)S(1)} collective-permute-done((bf16[2,4,32,768]{3,2,1,0:T(8,128)(2,1)S(1)}, bf16[2,4,32,768]{3,2,1,0:T(8,128)(2,1)S(1)}, u32[]{:S(2)}, u32[]{:S(2)}) %collective-permute-start.35) | collective-permute-done | bytes 393248 | tf_op jit(solution)/shard_map/ppermute | solution.py:39
  210.4 2.5 %collective-permute-done.36 = bf16[2,4,32,768]{3,2,1,0:T(8,128)(2,1)S(1)} collective-permute-done((bf16[2,4,32,768]{3,2,1,0:T(8,128)(2,1)S(1)}, bf16[2,4,32,768]{3,2,1,0:T(8,128)(2,1)S(1)}, u32[]{:S(2)}, u32[]{:S(2)}) %collective-permute-start.36) | collective-permute-done | bytes 393248 | tf_op jit(solution)/shard_map/ppermute | solution.py:39
  213.5 3.2 %collective-permute-done.37.b_ref = bf16[4,2,4,32,768]{4,3,2,1,0:T(8,128)(2,1)S(1)} collective-permute-done((bf16[4,2,4,32,768]{4,3,2,1,0:T(8,128)(2,1)S(1)}, bf16[4,2,4,32,768]{4,3,2,1,0:T(8,128)(2,1)S(1)}, u32[]{:S(2)}, u32[]{:S(2)}) %collective-permute-start.37) | collective-permute-done | bytes 1572896 | tf_op jit(solution)/shard_map/ppermute | solution.py:39
  216.7 3.9 %weight_grad.1 = (f32[192,448]{1,0:T(8,128)S(1)}, bf16[4,192,448]{2,1,0:T(8,128)(2,1)S(1)}) custom-call(s32[3]{0:T(128)S(1)} %pad_add_fusion.place_ref, bf16[4,2,4,32,768]{4,3,2,1,0:T(8,128)(2,1)S(1)} %pad_maximum_fusion.1.a_ref, bf16[4,2,4,32,768]{4,3,2,1,0:T(8,128)(2,1)S(1)} %collective-permute-done.37.b_ref, ...), custom_call_target="tpu_custom_call" | custom-call | tf_op jit(solution)/shard_map/weight_grad/pallas_call | solution.py:289
  220.8 2.5 %collective-permute-start.39 = (bf16[192,448]{1,0:T(8,128)(2,1)S(1)}, bf16[192,448]{1,0:T(8,128)(2,1)S(1)}, u32[]{:S(2)}, u32[]{:S(2)}) collective-permute-start(bf16[192,448]{1,0:T(8,128)(2,1)S(1)} %get-tuple-element.125), channel_id=1, source_target_pairs={{0,8},{1,9},{2,10},{3,11},{4,12},{5,13},{6,14},{7,15},{8,0},{9,1},... | collective-permute-start | bytes 516104 | tf_op jit(solution)/shard_map/ppermute | solution.py:39
  224.2 4.6 %collective-permute-done.38 = bf16[192,448]{1,0:T(8,128)(2,1)S(1)} collective-permute-done((bf16[192,448]{1,0:T(8,128)(2,1)S(1)}, bf16[192,448]{1,0:T(8,128)(2,1)S(1)}, u32[]{:S(2)}, u32[]{:S(2)}) %collective-permute-start.38) | collective-permute-done | bytes 172064 | tf_op jit(solution)/shard_map/ppermute | solution.py:39
  228.8 8.1 %collective-permute-done.39 = bf16[192,448]{1,0:T(8,128)(2,1)S(1)} collective-permute-done((bf16[192,448]{1,0:T(8,128)(2,1)S(1)}, bf16[192,448]{1,0:T(8,128)(2,1)S(1)}, u32[]{:S(2)}, u32[]{:S(2)}) %collective-permute-start.39) | collective-permute-done | bytes 172064 | tf_op jit(solution)/shard_map/ppermute | solution.py:39
  237.0 4.6 %collective-permute-done.40 = bf16[192,448]{1,0:T(8,128)(2,1)S(1)} collective-permute-done((bf16[192,448]{1,0:T(8,128)(2,1)S(1)}, bf16[192,448]{1,0:T(8,128)(2,1)S(1)}, u32[]{:S(2)}, u32[]{:S(2)}) %collective-permute-start.40) | collective-permute-done | bytes 172064 | tf_op jit(solution)/shard_map/ppermute | solution.py:39
  (91 shorter events, 33.9 us)
Async XLA Ops:
  0.6 10.1 %copy-start = (bf16[1,128,1536]{2,1,0:T(8,128)(2,1)S(1)}, bf16[1,128,1536]{2,1,0:T(8,128)(2,1)}, u32[]{:S(2)}) copy-start(bf16[1,128,1536]{2,1,0:T(8,128)(2,1)} %param.10) | copy-start | bytes 1179652
  0.6 6.5 %copy-start.3 = (bf16[1,32,7168]{2,1,0:T(8,128)(2,1)S(1)}, bf16[1,32,7168]{2,1,0:T(8,128)(2,1)}, u32[]{:S(2)}) copy-start(bf16[1,32,7168]{2,1,0:T(8,128)(2,1)} %param.8) | copy-start | bytes 1376260
  3.2 18.1 %collective-permute-start = (bf16[448,640]{1,0:T(8,128)(2,1)S(1)}, bf16[448,640]{1,0:T(8,128)(2,1)S(1)}, u32[]{:S(2)}, u32[]{:S(2)}) collective-permute-start(bf16[448,640]{1,0:T(8,128)(2,1)S(1)} %pad_maximum_fusion.8.refs_4_.refs_5_), channel_id=1, source_target_pairs={{0,1},{1,0},{2,3},{3,2},{4,5},{5,4},{6,7},{7,6},{8,9},{9,8},{10,11... | collective-permute-start | bytes 1720328 | tf_op jit(solution)/shard_map/ppermute | solution.py:39
  4.8 16.4 %collective-permute-start.1 = (bf16[448,640]{1,0:T(8,128)(2,1)S(1)}, bf16[448,640]{1,0:T(8,128)(2,1)S(1)}, u32[]{:S(2)}, u32[]{:S(2)}) collective-permute-start(bf16[448,640]{1,0:T(8,128)(2,1)S(1)} %pad_maximum_fusion.8.refs_4_.refs_5_), channel_id=1, source_target_pairs={{0,3},{1,2},{2,1},{3,0},{4,7},{5,6},{6,5},{7,4},{8,11},{9,10},{10,... | collective-permute-start | bytes 1720328 | tf_op jit(solution)/shard_map/ppermute | solution.py:39
  7.0 14.2 %collective-permute-start.2 = (bf16[448,640]{1,0:T(8,128)(2,1)S(1)}, bf16[448,640]{1,0:T(8,128)(2,1)S(1)}, u32[]{:S(2)}, u32[]{:S(2)}) collective-permute-start(bf16[448,640]{1,0:T(8,128)(2,1)S(1)} %pad_maximum_fusion.8.refs_4_.refs_5_), channel_id=1, source_target_pairs={{0,4},{1,5},{2,6},{3,7},{4,0},{5,1},{6,2},{7,3},{8,12},{9,13},{10,... | collective-permute-start | bytes 1720328 | tf_op jit(solution)/shard_map/ppermute | solution.py:39
  7.1 11.7 %collective-permute-start.3 = (bf16[32,7168]{1,0:T(8,128)(2,1)S(1)}, bf16[32,7168]{1,0:T(8,128)(2,1)}, u32[]{:S(2)}, u32[]{:S(2)}) collective-permute-start(bf16[32,7168]{1,0:T(8,128)(2,1)S(1)} %bitcast.67), channel_id=1, source_target_pairs={{0,32},{1,33},{2,34},{3,35},{4,36},{5,37},{6,38},{7,39},{8,40},{9,... | collective-permute-start | bytes 1376264 | tf_op jit(solution)/shard_map/ppermute | solution.py:39
  8.6 12.6 %collective-permute-start.4 = (bf16[32,7168]{1,0:T(8,128)(2,1)S(1)}, bf16[32,7168]{1,0:T(8,128)(2,1)}, u32[]{:S(2)}, u32[]{:S(2)}) collective-permute-start(bf16[32,7168]{1,0:T(8,128)(2,1)S(1)} %bitcast.68), channel_id=1, source_target_pairs={{0,96},{1,97},{2,98},{3,99},{4,100},{5,101},{6,102},{7,103},{8,104... | collective-permute-start | bytes 1376264 | tf_op jit(solution)/shard_map/ppermute | solution.py:39
  21.2 24.0 %collective-permute-start.8 = (bf16[32,7168]{1,0:T(8,128)(2,1)S(1)}, bf16[32,7168]{1,0:T(8,128)(2,1)S(1)}, u32[]{:S(2)}, u32[]{:S(2)}) collective-permute-start(bf16[32,7168]{1,0:T(8,128)(2,1)S(1)} %bitcast.69), channel_id=1, source_target_pairs={{0,140},{1,141},{2,142},{3,143},{4,136},{5,137},{6,138},{7,139},{8... | collective-permute-start | bytes 1376264 | tf_op jit(solution)/shard_map/ppermute | solution.py:39
  27.9 17.3 %collective-permute-start.9 = (bf16[32,7168]{1,0:T(8,128)(2,1)S(1)}, bf16[32,7168]{1,0:T(8,128)(2,1)S(1)}, u32[]{:S(2)}, u32[]{:S(2)}) collective-permute-start(bf16[32,7168]{1,0:T(8,128)(2,1)S(1)} %bitcast.70), channel_id=1, source_target_pairs={{0,64},{1,65},{2,66},{3,67},{4,68},{5,69},{6,70},{7,71},{8,72},{9,... | collective-permute-start | bytes 1376264 | tf_op jit(solution)/shard_map/ppermute | solution.py:39
  30.2 24.9 %collective-permute-start.5 = (bf16[672,640]{1,0:T(8,128)(2,1)S(1)}, bf16[672,640]{1,0:T(8,128)(2,1)S(1)}, u32[]{:S(2)}, u32[]{:S(2)}) collective-permute-start(bf16[672,640]{1,0:T(8,128)(2,1)S(1)} %get-tuple-element.131), channel_id=1, source_target_pairs={{0,1},{1,0},{2,3},{3,2},{4,5},{5,4},{6,7},{7,6},{8,9},{9,8},{10,11... | collective-permute-start | bytes 2580488 | tf_op jit(solution)/shard_map/ppermute | solution.py:39
  31.0 24.1 %collective-permute-start.6 = (bf16[672,640]{1,0:T(8,128)(2,1)S(1)}, bf16[672,640]{1,0:T(8,128)(2,1)S(1)}, u32[]{:S(2)}, u32[]{:S(2)}) collective-permute-start(bf16[672,640]{1,0:T(8,128)(2,1)S(1)} %get-tuple-element.130), channel_id=1, source_target_pairs={{0,3},{1,2},{2,1},{3,0},{4,7},{5,6},{6,5},{7,4},{8,11},{9,10},{10,... | collective-permute-start | bytes 2580488 | tf_op jit(solution)/shard_map/ppermute | solution.py:39
  32.0 23.2 %collective-permute-start.7 = (bf16[448,640]{1,0:T(8,128)(2,1)S(1)}, bf16[448,640]{1,0:T(8,128)(2,1)S(1)}, u32[]{:S(2)}, u32[]{:S(2)}) collective-permute-start(bf16[448,640]{1,0:T(8,128)(2,1)S(1)} %pad_maximum_fusion.8.refs_4_.refs_5_), channel_id=1, source_target_pairs={{0,8},{1,9},{2,10},{3,11},{4,12},{5,13},{6,14},{7,15},{8,0},{9,1},... | collective-permute-start | bytes 1720328 | tf_op jit(solution)/shard_map/ppermute | solution.py:39
  55.1 11.1 %collective-permute-start.13 = (bf16[32,7168]{1,0:T(8,128)(2,1)S(1)}, bf16[32,7168]{1,0:T(8,128)(2,1)S(1)}, u32[]{:S(2)}, u32[]{:S(2)}) collective-permute-start(bf16[32,7168]{1,0:T(8,128)(2,1)S(1)} %collective-permute-done.8), channel_id=1, source_target_pairs={{0,32},{1,33},{2,34},{3,35},{4,36},{5,37},{6,38},{7,39},{8,40},{9,... | collective-permute-start | bytes 1376264 | tf_op jit(solution)/shard_map/ppermute | solution.py:39
  55.8 12.0 %collective-permute-start.14 = (bf16[32,7168]{1,0:T(8,128)(2,1)S(1)}, bf16[32,7168]{1,0:T(8,128)(2,1)S(1)}, u32[]{:S(2)}, u32[]{:S(2)}) collective-permute-start(bf16[32,7168]{1,0:T(8,128)(2,1)S(1)} %collective-permute-done.8), channel_id=1, source_target_pairs={{0,96},{1,97},{2,98},{3,99},{4,100},{5,101},{6,102},{7,103},{8,104... | collective-permute-start | bytes 1376264 | tf_op jit(solution)/shard_map/ppermute | solution.py:39
  56.6 27.7 %collective-permute-start.10 = (bf16[672,640]{1,0:T(8,128)(2,1)S(1)}, bf16[672,640]{1,0:T(8,128)(2,1)S(1)}, u32[]{:S(2)}, u32[]{:S(2)}) collective-permute-start(bf16[672,640]{1,0:T(8,128)(2,1)S(1)} %get-tuple-element.129), channel_id=1, source_target_pairs={{0,1},{1,0},{2,3},{3,2},{4,5},{5,4},{6,7},{7,6},{8,9},{9,8},{10,11... | collective-permute-start | bytes 2580488 | tf_op jit(solution)/shard_map/ppermute | solution.py:39
  57.7 26.5 %collective-permute-start.11 = (bf16[672,640]{1,0:T(8,128)(2,1)S(1)}, bf16[672,640]{1,0:T(8,128)(2,1)S(1)}, u32[]{:S(2)}, u32[]{:S(2)}) collective-permute-start(bf16[672,640]{1,0:T(8,128)(2,1)S(1)} %get-tuple-element.128), channel_id=1, source_target_pairs={{0,3},{1,2},{2,1},{3,0},{4,7},{5,6},{6,5},{7,4},{8,11},{9,10},{10,... | collective-permute-start | bytes 2580488 | tf_op jit(solution)/shard_map/ppermute | solution.py:39
  59.3 24.9 %collective-permute-start.12 = (bf16[448,640]{1,0:T(8,128)(2,1)S(1)}, bf16[448,640]{1,0:T(8,128)(2,1)S(1)}, u32[]{:S(2)}, u32[]{:S(2)}) collective-permute-start(bf16[448,640]{1,0:T(8,128)(2,1)S(1)} %pad_maximum_fusion.8.refs_4_.refs_5_), channel_id=1, source_target_pairs={{0,12},{1,13},{2,14},{3,15},{4,8},{5,9},{6,10},{7,11},{8,4},{9,5},... | collective-permute-start | bytes 1720328 | tf_op jit(solution)/shard_map/ppermute | solution.py:39
  84.2 5.3 %collective-permute-start.18 = (bf16[128,7168]{1,0:T(8,128)(2,1)S(1)}, bf16[128,7168]{1,0:T(8,128)(2,1)S(1)}, u32[]{:S(2)}, u32[]{:S(2)}) collective-permute-start(bf16[128,7168]{1,0:T(8,128)(2,1)S(1)} %constant_dynamic-update-slice_fusion.rows_ref), channel_id=1, source_target_pairs={{0,16},{1,17},{2,18},{3,19},{4,20},{5,21},{6,22},{7,23},{8,24},{9,... | collective-permute-start | bytes 5505032 | tf_op jit(solution)/shard_map/ppermute | solution.py:39
  84.5 21.9 %collective-permute-start.15 = (bf16[672,640]{1,0:T(8,128)(2,1)S(1)}, bf16[672,640]{1,0:T(8,128)(2,1)S(1)}, u32[]{:S(2)}, u32[]{:S(2)}) collective-permute-start(bf16[672,640]{1,0:T(8,128)(2,1)S(1)} %get-tuple-element.127), channel_id=1, source_target_pairs={{0,1},{1,0},{2,3},{3,2},{4,5},{5,4},{6,7},{7,6},{8,9},{9,8},{10,11... | collective-permute-start | bytes 2580488 | tf_op jit(solution)/shard_map/ppermute | solution.py:39
  85.5 22.5 %collective-permute-start.16 = (bf16[672,640]{1,0:T(8,128)(2,1)S(1)}, bf16[672,640]{1,0:T(8,128)(2,1)S(1)}, u32[]{:S(2)}, u32[]{:S(2)}) collective-permute-start(bf16[672,640]{1,0:T(8,128)(2,1)S(1)} %get-tuple-element.126), channel_id=1, source_target_pairs={{0,3},{1,2},{2,1},{3,0},{4,7},{5,6},{6,5},{7,4},{8,11},{9,10},{10,... | collective-permute-start | bytes 2580488 | tf_op jit(solution)/shard_map/ppermute | solution.py:39
  86.9 13.9 %collective-permute-start.17 = (bf16[32,7168]{1,0:T(8,128)(2,1)S(1)}, bf16[32,7168]{1,0:T(8,128)(2,1)S(1)}, u32[]{:S(2)}, u32[]{:S(2)}) collective-permute-start(bf16[32,7168]{1,0:T(8,128)(2,1)S(1)} %collective-permute-done.8), channel_id=1, source_target_pairs={{0,64},{1,65},{2,66},{3,67},{4,68},{5,69},{6,70},{7,71},{8,72},{9,... | collective-permute-start | bytes 1376264 | tf_op jit(solution)/shard_map/ppermute | solution.py:39
  108.0 3.9 %collective-permute-start.19 = (bf16[128,7168]{1,0:T(8,128)(2,1)S(1)}, bf16[128,7168]{1,0:T(8,128)(2,1)S(1)}, u32[]{:S(2)}, u32[]{:S(2)}) collective-permute-start(bf16[128,7168]{1,0:T(8,128)(2,1)S(1)} %constant_dynamic-update-slice_fusion.4.rows_ref), channel_id=1, source_target_pairs={{0,16},{1,17},{2,18},{3,19},{4,20},{5,21},{6,22},{7,23},{8,24},{9,... | collective-permute-start | bytes 5505032 | tf_op jit(solution)/shard_map/ppermute | solution.py:39
  108.2 11.1 %collective-permute-start.20 = (bf16[224,640]{1,0:T(8,128)(2,1)S(1)}, bf16[224,640]{1,0:T(8,128)(2,1)S(1)}, u32[]{:S(2)}, u32[]{:S(2)}) collective-permute-start(bf16[224,640]{1,0:T(8,128)(2,1)S(1)} %slice.73), channel_id=1, source_target_pairs={{0,1},{1,0},{2,3},{3,2},{4,5},{5,4},{6,7},{7,6},{8,9},{9,8},{10,11... | collective-permute-start | bytes 860168 | tf_op jit(solution)/shard_map/ppermute | solution.py:39
  108.4 10.9 %collective-permute-start.21 = (bf16[224,640]{1,0:T(8,128)(2,1)S(1)}, bf16[224,640]{1,0:T(8,128)(2,1)S(1)}, u32[]{:S(2)}, u32[]{:S(2)}) collective-permute-start(bf16[224,640]{1,0:T(8,128)(2,1)S(1)} %slice.74), channel_id=1, source_target_pairs={{0,3},{1,2},{2,1},{3,0},{4,7},{5,6},{6,5},{7,4},{8,11},{9,10},{10,... | collective-permute-start | bytes 860168 | tf_op jit(solution)/shard_map/ppermute | solution.py:39
  122.5 3.5 %collective-permute-start.22 = (bf16[256,3072]{1,0:T(8,128)(2,1)S(1)}, bf16[256,3072]{1,0:T(8,128)(2,1)S(1)}, u32[]{:S(2)}, u32[]{:S(2)}) collective-permute-start(bf16[256,3072]{1,0:T(8,128)(2,1)S(1)} %project.3), channel_id=1, source_target_pairs={{0,16},{1,17},{2,18},{3,19},{4,20},{5,21},{6,22},{7,23},{8,24},{9,... | collective-permute-start | bytes 4718600 | tf_op jit(solution)/shard_map/ppermute | solution.py:39
  126.6 21.4 %collective-permute-start.23 = (bf16[2,32,3072]{2,1,0:T(8,128)(2,1)S(1)}, bf16[2,32,3072]{2,1,0:T(8,128)(2,1)S(1)}, u32[]{:S(2)}, u32[]{:S(2)}) collective-permute-start(bf16[2,32,3072]{2,1,0:T(8,128)(2,1)S(1)} %get-tuple-element.120), channel_id=1, source_target_pairs={{0,32},{1,33},{2,34},{3,35},{4,36},{5,37},{6,38},{7,39},{8,40},{9,... | collective-permute-start | bytes 1179656 | tf_op jit(solution)/shard_map/ppermute | solution.py:39
  137.0 20.5 %collective-permute-start.24 = (bf16[2,32,3072]{2,1,0:T(8,128)(2,1)S(1)}, bf16[2,32,3072]{2,1,0:T(8,128)(2,1)S(1)}, u32[]{:S(2)}, u32[]{:S(2)}) collective-permute-start(bf16[2,32,3072]{2,1,0:T(8,128)(2,1)S(1)} %get-tuple-element.122), channel_id=1, source_target_pairs={{0,64},{1,65},{2,66},{3,67},{4,68},{5,69},{6,70},{7,71},{8,72},{9,... | collective-permute-start | bytes 1179656 | tf_op jit(solution)/shard_map/ppermute | solution.py:39
  139.8 20.3 %collective-permute-start.25 = (bf16[2,32,3072]{2,1,0:T(8,128)(2,1)S(1)}, bf16[2,32,3072]{2,1,0:T(8,128)(2,1)S(1)}, u32[]{:S(2)}, u32[]{:S(2)}) collective-permute-start(bf16[2,32,3072]{2,1,0:T(8,128)(2,1)S(1)} %get-tuple-element.121), channel_id=1, source_target_pairs={{0,96},{1,97},{2,98},{3,99},{4,100},{5,101},{6,102},{7,103},{8,104... | collective-permute-start | bytes 1179656 | tf_op jit(solution)/shard_map/ppermute | solution.py:39
  142.0 31.6 %copy-start.2 = (bf16[1,128,1536]{2,1,0:T(8,128)(2,1)S(1)}, bf16[1,128,1536]{2,1,0:T(8,128)(2,1)}, u32[]{:S(2)}) copy-start(bf16[1,128,1536]{2,1,0:T(8,128)(2,1)} %param.15) | copy-start | bytes 1179652
  160.4 11.6 %collective-permute-start.27 = (bf16[448,512]{1,0:T(8,128)(2,1)S(1)}, bf16[448,512]{1,0:T(8,128)(2,1)S(1)}, u32[]{:S(2)}, u32[]{:S(2)}) collective-permute-start(bf16[448,512]{1,0:T(8,128)(2,1)S(1)} %get-tuple-element.113), channel_id=1, source_target_pairs={{0,1},{1,0},{2,3},{3,2},{4,5},{5,4},{6,7},{7,6},{8,9},{9,8},{10,11... | collective-permute-start | bytes 1376264 | tf_op jit(solution)/shard_map/ppermute | solution.py:39
  161.4 12.1 %collective-permute-start.28 = (bf16[448,512]{1,0:T(8,128)(2,1)S(1)}, bf16[448,512]{1,0:T(8,128)(2,1)S(1)}, u32[]{:S(2)}, u32[]{:S(2)}) collective-permute-start(bf16[448,512]{1,0:T(8,128)(2,1)S(1)} %get-tuple-element.113), channel_id=1, source_target_pairs={{0,3},{1,2},{2,1},{3,0},{4,7},{5,6},{6,5},{7,4},{8,11},{9,10},{10,... | collective-permute-start | bytes 1376264 | tf_op jit(solution)/shard_map/ppermute | solution.py:39
  163.2 8.8 %collective-permute-start.26 = (bf16[32,3072]{1,0:T(8,128)(2,1)S(1)}, bf16[32,3072]{1,0:T(8,128)(2,1)S(1)}, u32[]{:S(2)}, u32[]{:S(2)}) collective-permute-start(bf16[32,3072]{1,0:T(8,128)(2,1)S(1)} %fusion.4), channel_id=1, source_target_pairs={{0,140},{1,141},{2,142},{3,143},{4,136},{5,137},{6,138},{7,139},{8... | collective-permute-start | bytes 589832 | tf_op jit(solution)/shard_map/ppermute | solution.py:39
  177.0 4.8 %collective-permute-start.29 = (bf16[32,768]{1,0:T(8,128)(2,1)S(1)}, bf16[32,768]{1,0:T(8,128)(2,1)S(1)}, u32[]{:S(2)}, u32[]{:S(2)}) collective-permute-start(bf16[32,768]{1,0:T(8,128)(2,1)S(1)} %get-tuple-element.137), channel_id=1, source_target_pairs={{0,1},{1,0},{2,3},{3,2},{4,5},{5,4},{6,7},{7,6},{8,9},{9,8},{10,11... | collective-permute-start | bytes 147464 | tf_op jit(solution)/shard_map/ppermute | solution.py:39
  177.1 5.8 %collective-permute-start.30 = (bf16[32,768]{1,0:T(8,128)(2,1)S(1)}, bf16[32,768]{1,0:T(8,128)(2,1)S(1)}, u32[]{:S(2)}, u32[]{:S(2)}) collective-permute-start(bf16[32,768]{1,0:T(8,128)(2,1)S(1)} %get-tuple-element.136), channel_id=1, source_target_pairs={{0,2},{1,3},{2,0},{3,1},{4,6},{5,7},{6,4},{7,5},{8,10},{9,11},{10,... | collective-permute-start | bytes 147464 | tf_op jit(solution)/shard_map/ppermute | solution.py:39
  180.2 5.3 %collective-permute-start.31 = (bf16[32,768]{1,0:T(8,128)(2,1)S(1)}, bf16[32,768]{1,0:T(8,128)(2,1)S(1)}, u32[]{:S(2)}, u32[]{:S(2)}) collective-permute-start(bf16[32,768]{1,0:T(8,128)(2,1)S(1)} %get-tuple-element.135), channel_id=1, source_target_pairs={{0,3},{1,2},{2,1},{3,0},{4,7},{5,6},{6,5},{7,4},{8,11},{9,10},{10,... | collective-permute-start | bytes 147464 | tf_op jit(solution)/shard_map/ppermute | solution.py:39
  185.6 10.1 %collective-permute-start.33 = (bf16[448,512]{1,0:T(8,128)(2,1)S(1)}, bf16[448,512]{1,0:T(8,128)(2,1)S(1)}, u32[]{:S(2)}, u32[]{:S(2)}) collective-permute-start(bf16[448,512]{1,0:T(8,128)(2,1)S(1)} %get-tuple-element.113), channel_id=1, source_target_pairs={{0,2},{1,3},{2,0},{3,1},{4,6},{5,7},{6,4},{7,5},{8,10},{9,11},{10,... | collective-permute-start | bytes 1376264 | tf_op jit(solution)/shard_map/ppermute | solution.py:39
  186.0 8.7 %collective-permute-start.32 = (bf16[4,32,768]{2,1,0:T(8,128)(2,1)S(1)}, bf16[4,32,768]{2,1,0:T(8,128)(2,1)S(1)}, u32[]{:S(2)}, u32[]{:S(2)}) collective-permute-start(bf16[4,32,768]{2,1,0:T(8,128)(2,1)S(1)} %pad_maximum_fusion.10), channel_id=1, source_target_pairs={{0,140},{1,141},{2,142},{3,143},{4,136},{5,137},{6,138},{7,139},{8... | collective-permute-start | bytes 589832 | tf_op jit(solution)/shard_map/ppermute | solution.py:39
  195.7 10.1 %collective-permute-start.34 = (bf16[2,4,32,768]{3,2,1,0:T(8,128)(2,1)S(1)}, bf16[2,4,32,768]{3,2,1,0:T(8,128)(2,1)S(1)}, u32[]{:S(2)}, u32[]{:S(2)}) collective-permute-start(bf16[2,4,32,768]{3,2,1,0:T(8,128)(2,1)S(1)} %get-tuple-element.133), channel_id=1, source_target_pairs={{0,32},{1,33},{2,34},{3,35},{4,36},{5,37},{6,38},{7,39},{8,40},{9,... | collective-permute-start | bytes 1179656 | tf_op jit(solution)/shard_map/ppermute | solution.py:39
  195.8 14.6 %collective-permute-start.35 = (bf16[2,4,32,768]{3,2,1,0:T(8,128)(2,1)S(1)}, bf16[2,4,32,768]{3,2,1,0:T(8,128)(2,1)S(1)}, u32[]{:S(2)}, u32[]{:S(2)}) collective-permute-start(bf16[2,4,32,768]{3,2,1,0:T(8,128)(2,1)S(1)} %get-tuple-element.133), channel_id=1, source_target_pairs={{0,64},{1,65},{2,66},{3,67},{4,68},{5,69},{6,70},{7,71},{8,72},{9,... | collective-permute-start | bytes 1179656 | tf_op jit(solution)/shard_map/ppermute | solution.py:39
  198.2 14.8 %collective-permute-start.36 = (bf16[2,4,32,768]{3,2,1,0:T(8,128)(2,1)S(1)}, bf16[2,4,32,768]{3,2,1,0:T(8,128)(2,1)S(1)}, u32[]{:S(2)}, u32[]{:S(2)}) collective-permute-start(bf16[2,4,32,768]{3,2,1,0:T(8,128)(2,1)S(1)} %get-tuple-element.133), channel_id=1, source_target_pairs={{0,96},{1,97},{2,98},{3,99},{4,100},{5,101},{6,102},{7,103},{8,104... | collective-permute-start | bytes 1179656 | tf_op jit(solution)/shard_map/ppermute | solution.py:39
  213.2 3.5 %collective-permute-start.37 = (bf16[4,2,4,32,768]{4,3,2,1,0:T(8,128)(2,1)S(1)}, bf16[4,2,4,32,768]{4,3,2,1,0:T(8,128)(2,1)S(1)}, u32[]{:S(2)}, u32[]{:S(2)}) collective-permute-start(bf16[4,2,4,32,768]{4,3,2,1,0:T(8,128)(2,1)S(1)} %pad_maximum_fusion.1.a_ref), channel_id=1, source_target_pairs={{0,16},{1,17},{2,18},{3,19},{4,20},{5,21},{6,22},{7,23},{8,24},{9,... | collective-permute-start | bytes 4718600 | tf_op jit(solution)/shard_map/ppermute | solution.py:39
  216.7 25.8 %copy-start.1 = (bf16[1,128,1536]{2,1,0:T(8,128)(2,1)S(1)}, bf16[1,128,1536]{2,1,0:T(8,128)(2,1)}, u32[]{:S(2)}) copy-start(bf16[1,128,1536]{2,1,0:T(8,128)(2,1)} %param.10) | copy-start | bytes 1179652
  220.7 8.2 %collective-permute-start.38 = (bf16[192,448]{1,0:T(8,128)(2,1)S(1)}, bf16[192,448]{1,0:T(8,128)(2,1)S(1)}, u32[]{:S(2)}, u32[]{:S(2)}) collective-permute-start(bf16[192,448]{1,0:T(8,128)(2,1)S(1)} %get-tuple-element.123), channel_id=1, source_target_pairs={{0,4},{1,5},{2,6},{3,7},{4,0},{5,1},{6,2},{7,3},{8,12},{9,13},{10,... | collective-permute-start | bytes 516104 | tf_op jit(solution)/shard_map/ppermute | solution.py:39
  220.8 16.2 %collective-permute-start.39 = (bf16[192,448]{1,0:T(8,128)(2,1)S(1)}, bf16[192,448]{1,0:T(8,128)(2,1)S(1)}, u32[]{:S(2)}, u32[]{:S(2)}) collective-permute-start(bf16[192,448]{1,0:T(8,128)(2,1)S(1)} %get-tuple-element.125), channel_id=1, source_target_pairs={{0,8},{1,9},{2,10},{3,11},{4,12},{5,13},{6,14},{7,15},{8,0},{9,1},... | collective-permute-start | bytes 516104 | tf_op jit(solution)/shard_map/ppermute | solution.py:39
  223.2 18.3 %collective-permute-start.40 = (bf16[192,448]{1,0:T(8,128)(2,1)S(1)}, bf16[192,448]{1,0:T(8,128)(2,1)S(1)}, u32[]{:S(2)}, u32[]{:S(2)}) collective-permute-start(bf16[192,448]{1,0:T(8,128)(2,1)S(1)} %get-tuple-element.124), channel_id=1, source_target_pairs={{0,12},{1,13},{2,14},{3,15},{4,8},{5,9},{6,10},{7,11},{8,4},{9,5},... | collective-permute-start | bytes 516104 | tf_op jit(solution)/shard_map/ppermute | solution.py:39

commit v5 on v4

--- a/solution.py
+++ b/solution.py
@@ -48,15 +48,19 @@
 
 
 def norm_kernel(place_ref, rows_ref, normed_ref, resid_ref):
-    widened = rows_ref[...].astype(f32)
-    mean = jnp.mean(widened * widened, axis=-1, keepdims=True)
-    normed_ref[...] = (widened * lax.rsqrt(mean + eps)).astype(bf16)
-    depth = resid_ref.shape[1]
-    for f in range(rows_ref.shape[1] // depth):
-
-        @pl.when(place_ref[0] == f)
-        def _():
-            resid_ref[...] = rows_ref[:, f * depth : (f + 1) * depth]
+    depth, chunk = resid_ref.shape[1], 16
+
+    def step(i, carry):
+        at = pl.ds(pl.multiple_of(i * chunk, chunk), chunk)
+        widened = rows_ref[at].astype(f32)
+        mean = jnp.mean(widened * widened, axis=-1, keepdims=True)
+        normed_ref[at] = (widened * lax.rsqrt(mean + eps)).astype(bf16)
+        return carry
+
+    lax.fori_loop(0, rows_ref.shape[0] // chunk, step, 0)
+    column = pl.multiple_of(place_ref[0] // 2 * (2 * depth), 128)
+    both = rows_ref[:, pl.ds(column, 2 * depth)]
+    resid_ref[...] = jnp.where(place_ref[0] % 2 == 0, both[:, :depth], both[:, depth:])
 
 
 def normalize(rows, place):
@@ -341,9 +345,9 @@
 
     y1, z2 = around(y0, z1), send(block, ALONG_Z[2])
     mirrored, own2 = send(rows, MIRROR), along_x(rows, 2)
-    y1, z2, mirrored, own2, block = lax.optimization_barrier((y1, z2, mirrored, own2, block))
-
-    y2, z3 = around(y1, z2), send(block, ALONG_Z[3])
+    y1, z2, mirrored, own2 = lax.optimization_barrier((y1, z2, mirrored, own2))
+
+    y2, z3 = around(y1, z2), send(z2, ALONG_Z[1])
     far1, far3 = along_x(mirrored, 1), along_x(mirrored, 3)
     own_a = jnp.concatenate([rows, own1, own2, own3])
     queries = lax.dot_general(

time: 247 us -> 231 us (0.935); the launches traced: 243 us -> 230 us
  starting transfers between devices: 63 us -> 54.7 us
  waiting for transfers between devices: 142 us -> 135 us
    ppermute x41, starting transfers between devices: 63 us -> 54.7 us  [send(): return lax.ppermute(array, AXES, table)]
    ppermute x41, waiting for transfers between devices: 142 us -> 135 us  [send(): return lax.ppermute(array, AXES, table)]
  transfers between devices with their start and end apart: 41 -> 41, of which waited for: 28 -> 29; matrix products, arithmetic and copies ran while one was open for 3% -> 3% of each run, Pallas kernels for 5% -> 7%
where the time goes in v5:
time: 231 us; the launch traced here: 230 us
  waiting for transfers between devices  135 us (58%)
  starting transfers between devices  54.7 us (24%)
  Pallas kernels  26 us (11%)
  local copies, waits for them, and re-layouts  5.22 us (2%)
  matrix products  3.96 us (2%)
  other arithmetic  2.63 us (1%)
  between operations  2.35 us (1%)
    ppermute x41, waiting for transfers between devices, send(): return lax.ppermute(array, AXES, table)  135 us
    ppermute x41, starting transfers between devices, send(): return lax.ppermute(array, AXES, table)  54.7 us
    pallas_call x4, Pallas kernels, normalize(): pl.pallas_call(norm_kernel, grid=(height // per,), in_specs=[pl.BlockSpec...  8.94 us
    pallas_call x4, Pallas kernels, layer(): pl.pallas_call(functools.partial(layer_kernel, finish=finish), grid_spec=...  7.79 us
  transfers between devices with their start and end apart: 41, of which 29 were waited for; matrix products, arithmetic and copies ran while one was open for 3% of the time, Pallas kernels for 7%

profile of v5, /device:TPU:32, one launch (start us, length us, event | category | flops | bytes accessed | tf_op | source)
XLA Modules:
  0.0 230.2 jit_solution(12873586315341991635)
XLA Ops:
  3.2 1.7 collective-permute-start
  4.8 2.2 collective-permute-start.1
  8.6 2.1 collective-permute-start.4
  10.8 4.0 %convolution_convert_fusion.q_ref = bf16[128,1536]{1,0:T(8,128)(2,1)S(1)} fusion(bf16[1536,1536]{1,0:T(8,128)(2,1)} %param.14, bf16[1,128,1536]{2,1,0:T(8,128)(2,1)S(1)} %copy-done), kind=kOutput, calls=%fused_computation.1 | convolution fusion | flops 604176384 | bytes 5505024 | tf_op jit(solution)/shard_map/dot_general | solution.py:353
  14.8 4.1 %collective-permute-done.3 = bf16[32,7168]{1,0:T(8,128)(2,1)} collective-permute-done((bf16[32,7168]{1,0:T(8,128)(2,1)S(1)}, bf16[32,7168]{1,0:T(8,128)(2,1)}, u32[]{:S(2)}, u32[]{:S(2)}) %collective-permute-start.3) | collective-permute-done | bytes 458784 | tf_op jit(solution)/shard_map/ppermute | solution.py:39
  18.8 2.4 %collective-permute-done.4 = bf16[32,7168]{1,0:T(8,128)(2,1)} collective-permute-done((bf16[32,7168]{1,0:T(8,128)(2,1)S(1)}, bf16[32,7168]{1,0:T(8,128)(2,1)}, u32[]{:S(2)}, u32[]{:S(2)}) %collective-permute-start.4) | collective-permute-done | bytes 458784 | tf_op jit(solution)/shard_map/ppermute | solution.py:39
  21.2 6.7 %collective-permute-start.8 = (bf16[32,7168]{1,0:T(8,128)(2,1)S(1)}, bf16[32,7168]{1,0:T(8,128)(2,1)S(1)}, u32[]{:S(2)}, u32[]{:S(2)}) collective-permute-start(bf16[32,7168]{1,0:T(8,128)(2,1)S(1)} %bitcast.69), channel_id=1, source_target_pairs={{0,140},{1,141},{2,142},{3,143},{4,136},{5,137},{6,138},{7,139},{8... | collective-permute-start | bytes 1376264 | tf_op jit(solution)/shard_map/ppermute | solution.py:39
  27.9 2.1 collective-permute-start.9
  33.6 11.6 %collective-permute-done.8 = bf16[32,7168]{1,0:T(8,128)(2,1)S(1)} collective-permute-done((bf16[32,7168]{1,0:T(8,128)(2,1)S(1)}, bf16[32,7168]{1,0:T(8,128)(2,1)S(1)}, u32[]{:S(2)}, u32[]{:S(2)}) %collective-permute-start.8) | collective-permute-done | bytes 458784 | tf_op jit(solution)/shard_map/ppermute | solution.py:39
  45.2 9.9 %collective-permute-done.7.refs_4_.refs_5_ = bf16[448,640]{1,0:T(8,128)(2,1)S(1)} collective-permute-done((bf16[448,640]{1,0:T(8,128)(2,1)S(1)}, bf16[448,640]{1,0:T(8,128)(2,1)S(1)}, u32[]{:S(2)}, u32[]{:S(2)}) %collective-permute-start.7) | collective-permute-done | bytes 573472 | tf_op jit(solution)/shard_map/ppermute | solution.py:39
  56.4 3.0 %collective-permute-start.12 = (bf16[448,640]{1,0:T(8,128)(2,1)S(1)}, bf16[448,640]{1,0:T(8,128)(2,1)S(1)}, u32[]{:S(2)}, u32[]{:S(2)}) collective-permute-start(bf16[448,640]{1,0:T(8,128)(2,1)S(1)} %collective-permute-done.7.refs_4_.refs_5_), channel_id=1, source_target_pairs={{0,4},{1,5},{2,6},{3,7},{4,0},{5,1},{6,2},{7,3},{8,12},{9,13},{10,... | collective-permute-start | bytes 1720328 | tf_op jit(solution)/shard_map/ppermute | solution.py:39
  63.4 2.2 norm.4
  67.8 3.2 %collective-permute-done.12.refs_4_.refs_5_ = bf16[448,640]{1,0:T(8,128)(2,1)S(1)} collective-permute-done((bf16[448,640]{1,0:T(8,128)(2,1)S(1)}, bf16[448,640]{1,0:T(8,128)(2,1)S(1)}, u32[]{:S(2)}, u32[]{:S(2)}) %collective-permute-start.12) | collective-permute-done | bytes 573472 | tf_op jit(solution)/shard_map/ppermute | solution.py:39
  71.0 7.8 %collective-permute-done.10.refs_8_.refs_6_.refs_7_ = bf16[672,640]{1,0:T(8,128)(2,1)S(1)} collective-permute-done((bf16[672,640]{1,0:T(8,128)(2,1)S(1)}, bf16[672,640]{1,0:T(8,128)(2,1)S(1)}, u32[]{:S(2)}, u32[]{:S(2)}) %collective-permute-start.10) | collective-permute-done | bytes 860192 | tf_op jit(solution)/shard_map/ppermute | solution.py:39
  78.8 2.0 collective-permute-done.11.refs_9_.refs_10_.refs_11_
  81.1 1.8 collective-permute-start.16
  82.9 2.6 %collective-permute-start.17 = (bf16[32,7168]{1,0:T(8,128)(2,1)S(1)}, bf16[32,7168]{1,0:T(8,128)(2,1)S(1)}, u32[]{:S(2)}, u32[]{:S(2)}) collective-permute-start(bf16[32,7168]{1,0:T(8,128)(2,1)S(1)} %collective-permute-done.8), channel_id=1, source_target_pairs={{0,64},{1,65},{2,66},{3,67},{4,68},{5,69},{6,70},{7,71},{8,72},{9,... | collective-permute-start | bytes 1376264 | tf_op jit(solution)/shard_map/ppermute | solution.py:39
  85.6 2.2 norm.5
  87.9 9.2 %collective-permute-done.17 = bf16[32,7168]{1,0:T(8,128)(2,1)S(1)} collective-permute-done((bf16[32,7168]{1,0:T(8,128)(2,1)S(1)}, bf16[32,7168]{1,0:T(8,128)(2,1)S(1)}, u32[]{:S(2)}, u32[]{:S(2)}) %collective-permute-start.17) | collective-permute-done | bytes 458784 | tf_op jit(solution)/shard_map/ppermute | solution.py:39
  97.1 5.5 %collective-permute-done.15.refs_8_.refs_6_.refs_7_ = bf16[672,640]{1,0:T(8,128)(2,1)S(1)} collective-permute-done((bf16[672,640]{1,0:T(8,128)(2,1)S(1)}, bf16[672,640]{1,0:T(8,128)(2,1)S(1)}, u32[]{:S(2)}, u32[]{:S(2)}) %collective-permute-start.15) | collective-permute-done | bytes 860192 | tf_op jit(solution)/shard_map/ppermute | solution.py:39
  106.3 2.2 norm.6
  108.6 2.2 norm.7
  111.0 1.9 layer.4
  112.8 1.9 layer.5
  114.7 1.9 layer.6
  116.6 2.2 layer.7
  120.9 2.4 %collective-permute-done.22 = bf16[256,3072]{1,0:T(8,128)(2,1)S(1)} collective-permute-done((bf16[256,3072]{1,0:T(8,128)(2,1)S(1)}, bf16[256,3072]{1,0:T(8,128)(2,1)S(1)}, u32[]{:S(2)}, u32[]{:S(2)}) %collective-permute-start.22) | collective-permute-done | bytes 1572896 | tf_op jit(solution)/shard_map/ppermute | solution.py:39
  125.0 2.7 %collective-permute-start.24 = (bf16[2,32,3072]{2,1,0:T(8,128)(2,1)S(1)}, bf16[2,32,3072]{2,1,0:T(8,128)(2,1)S(1)}, u32[]{:S(2)}, u32[]{:S(2)}) collective-permute-start(bf16[2,32,3072]{2,1,0:T(8,128)(2,1)S(1)} %get-tuple-element.120), channel_id=1, source_target_pairs={{0,64},{1,65},{2,66},{3,67},{4,68},{5,69},{6,70},{7,71},{8,72},{9,... | collective-permute-start | bytes 1179656 | tf_op jit(solution)/shard_map/ppermute | solution.py:39
  130.0 5.9 %collective-permute-done.23 = bf16[2,32,3072]{2,1,0:T(8,128)(2,1)S(1)} collective-permute-done((bf16[2,32,3072]{2,1,0:T(8,128)(2,1)S(1)}, bf16[2,32,3072]{2,1,0:T(8,128)(2,1)S(1)}, u32[]{:S(2)}, u32[]{:S(2)}) %collective-permute-start.23) | collective-permute-done | bytes 393248 | tf_op jit(solution)/shard_map/ppermute | solution.py:39
  135.9 9.5 %collective-permute-done.24 = bf16[2,32,3072]{2,1,0:T(8,128)(2,1)S(1)} collective-permute-done((bf16[2,32,3072]{2,1,0:T(8,128)(2,1)S(1)}, bf16[2,32,3072]{2,1,0:T(8,128)(2,1)S(1)}, u32[]{:S(2)}, u32[]{:S(2)}) %collective-permute-start.24) | collective-permute-done | bytes 393248 | tf_op jit(solution)/shard_map/ppermute | solution.py:39
  145.4 2.6 %collective-permute-done.25 = bf16[2,32,3072]{2,1,0:T(8,128)(2,1)S(1)} collective-permute-done((bf16[2,32,3072]{2,1,0:T(8,128)(2,1)S(1)}, bf16[2,32,3072]{2,1,0:T(8,128)(2,1)S(1)}, u32[]{:S(2)}, u32[]{:S(2)}) %collective-permute-start.25) | collective-permute-done | bytes 393248 | tf_op jit(solution)/shard_map/ppermute | solution.py:39
  149.4 1.8 collective-permute-start.28
  151.4 8.7 %collective-permute-done.26.other_ref = bf16[32,3072]{1,0:T(8,128)(2,1)S(1)} collective-permute-done((bf16[32,3072]{1,0:T(8,128)(2,1)S(1)}, bf16[32,3072]{1,0:T(8,128)(2,1)S(1)}, u32[]{:S(2)}, u32[]{:S(2)}) %collective-permute-start.26) | collective-permute-done | bytes 196640 | tf_op jit(solution)/shard_map/ppermute | solution.py:39
  161.4 3.4 %attention.1 = (bf16[128,1536]{1,0:T(8,128)(2,1)}, bf16[4,32,768]{2,1,0:T(8,128)(2,1)S(1)}) custom-call(s32[3]{0:T(128)S(1)} %pad_add_fusion.place_ref, s32[1]{0:T(128)S(6)} %copy.28.images_ref, s32[1]{0:T(128)S(6)} %copy.29.lengths_ref, f32[32,3072]{1,0:T(8,128)S(1)} %slice_bitcast_fusion.4.own_ref, bf16[32,3072]{1,0:T(8,128)(2,1)S(1)} %collective-permute-done.26.other_ref, ...), custom_call_target="tpu_custom_call" | custom-call | tf_op jit(solution)/shard_map/attention/pallas_call | solution.py:245
  164.9 3.2 %collective-permute-start.30 = (bf16[32,768]{1,0:T(8,128)(2,1)S(1)}, bf16[32,768]{1,0:T(8,128)(2,1)S(1)}, u32[]{:S(2)}, u32[]{:S(2)}) collective-permute-start(bf16[32,768]{1,0:T(8,128)(2,1)S(1)} %get-tuple-element.134), channel_id=1, source_target_pairs={{0,2},{1,3},{2,0},{3,1},{4,6},{5,7},{6,4},{7,5},{8,10},{9,11},{10,... | collective-permute-start | bytes 147464 | tf_op jit(solution)/shard_map/ppermute | solution.py:39
  170.8 2.7 %collective-permute-done.31 = bf16[32,768]{1,0:T(8,128)(2,1)S(1)} collective-permute-done((bf16[32,768]{1,0:T(8,128)(2,1)S(1)}, bf16[32,768]{1,0:T(8,128)(2,1)S(1)}, u32[]{:S(2)}, u32[]{:S(2)}) %collective-permute-start.31) | collective-permute-done | bytes 49184 | tf_op jit(solution)/shard_map/ppermute | solution.py:39
  173.9 8.7 %collective-permute-done.32 = bf16[4,32,768]{2,1,0:T(8,128)(2,1)S(1)} collective-permute-done((bf16[4,32,768]{2,1,0:T(8,128)(2,1)S(1)}, bf16[4,32,768]{2,1,0:T(8,128)(2,1)S(1)}, u32[]{:S(2)}, u32[]{:S(2)}) %collective-permute-start.32) | collective-permute-done | bytes 196640 | tf_op jit(solution)/shard_map/ppermute | solution.py:39
  183.7 2.8 %collective-permute-start.34 = (bf16[2,4,32,768]{3,2,1,0:T(8,128)(2,1)S(1)}, bf16[2,4,32,768]{3,2,1,0:T(8,128)(2,1)S(1)}, u32[]{:S(2)}, u32[]{:S(2)}) collective-permute-start(bf16[2,4,32,768]{3,2,1,0:T(8,128)(2,1)S(1)} %get-tuple-element.131), channel_id=1, source_target_pairs={{0,32},{1,33},{2,34},{3,35},{4,36},{5,37},{6,38},{7,39},{8,40},{9,... | collective-permute-start | bytes 1179656 | tf_op jit(solution)/shard_map/ppermute | solution.py:39
  187.2 2.1 collective-permute-start.36
  189.3 4.4 %collective-permute-done.34 = bf16[2,4,32,768]{3,2,1,0:T(8,128)(2,1)S(1)} collective-permute-done((bf16[2,4,32,768]{3,2,1,0:T(8,128)(2,1)S(1)}, bf16[2,4,32,768]{3,2,1,0:T(8,128)(2,1)S(1)}, u32[]{:S(2)}, u32[]{:S(2)}) %collective-permute-start.34) | collective-permute-done | bytes 393248 | tf_op jit(solution)/shard_map/ppermute | solution.py:39
  193.6 4.6 %collective-permute-done.35 = bf16[2,4,32,768]{3,2,1,0:T(8,128)(2,1)S(1)} collective-permute-done((bf16[2,4,32,768]{3,2,1,0:T(8,128)(2,1)S(1)}, bf16[2,4,32,768]{3,2,1,0:T(8,128)(2,1)S(1)}, u32[]{:S(2)}, u32[]{:S(2)}) %collective-permute-start.35) | collective-permute-done | bytes 393248 | tf_op jit(solution)/shard_map/ppermute | solution.py:39
  198.2 2.5 %collective-permute-done.36 = bf16[2,4,32,768]{3,2,1,0:T(8,128)(2,1)S(1)} collective-permute-done((bf16[2,4,32,768]{3,2,1,0:T(8,128)(2,1)S(1)}, bf16[2,4,32,768]{3,2,1,0:T(8,128)(2,1)S(1)}, u32[]{:S(2)}, u32[]{:S(2)}) %collective-permute-start.36) | collective-permute-done | bytes 393248 | tf_op jit(solution)/shard_map/ppermute | solution.py:39
  201.3 3.2 %collective-permute-done.37.b_ref = bf16[4,2,4,32,768]{4,3,2,1,0:T(8,128)(2,1)S(1)} collective-permute-done((bf16[4,2,4,32,768]{4,3,2,1,0:T(8,128)(2,1)S(1)}, bf16[4,2,4,32,768]{4,3,2,1,0:T(8,128)(2,1)S(1)}, u32[]{:S(2)}, u32[]{:S(2)}) %collective-permute-start.37) | collective-permute-done | bytes 1572896 | tf_op jit(solution)/shard_map/ppermute | solution.py:39
  204.4 3.9 %weight_grad.1 = (f32[192,448]{1,0:T(8,128)S(1)}, bf16[4,192,448]{2,1,0:T(8,128)(2,1)S(1)}) custom-call(s32[3]{0:T(128)S(1)} %pad_add_fusion.place_ref, bf16[4,2,4,32,768]{4,3,2,1,0:T(8,128)(2,1)S(1)} %pad_maximum_fusion.1.a_ref, bf16[4,2,4,32,768]{4,3,2,1,0:T(8,128)(2,1)S(1)} %collective-permute-done.37.b_ref, ...), custom_call_target="tpu_custom_call" | custom-call | tf_op jit(solution)/shard_map/weight_grad/pallas_call | solution.py:293
  208.8 2.2 collective-permute-start.39
  212.0 4.6 %collective-permute-done.38 = bf16[192,448]{1,0:T(8,128)(2,1)S(1)} collective-permute-done((bf16[192,448]{1,0:T(8,128)(2,1)S(1)}, bf16[192,448]{1,0:T(8,128)(2,1)S(1)}, u32[]{:S(2)}, u32[]{:S(2)}) %collective-permute-start.38) | collective-permute-done | bytes 172064 | tf_op jit(solution)/shard_map/ppermute | solution.py:39
  216.6 8.1 %collective-permute-done.39 = bf16[192,448]{1,0:T(8,128)(2,1)S(1)} collective-permute-done((bf16[192,448]{1,0:T(8,128)(2,1)S(1)}, bf16[192,448]{1,0:T(8,128)(2,1)S(1)}, u32[]{:S(2)}, u32[]{:S(2)}) %collective-permute-start.39) | collective-permute-done | bytes 172064 | tf_op jit(solution)/shard_map/ppermute | solution.py:39
  224.7 4.6 %collective-permute-done.40 = bf16[192,448]{1,0:T(8,128)(2,1)S(1)} collective-permute-done((bf16[192,448]{1,0:T(8,128)(2,1)S(1)}, bf16[192,448]{1,0:T(8,128)(2,1)S(1)}, u32[]{:S(2)}, u32[]{:S(2)}) %collective-permute-start.40) | collective-permute-done | bytes 172064 | tf_op jit(solution)/shard_map/ppermute | solution.py:39
  (91 shorter events, 34.7 us)
Async XLA Ops:
  0.6 10.1 %copy-start = (bf16[1,128,1536]{2,1,0:T(8,128)(2,1)S(1)}, bf16[1,128,1536]{2,1,0:T(8,128)(2,1)}, u32[]{:S(2)}) copy-start(bf16[1,128,1536]{2,1,0:T(8,128)(2,1)} %param.10) | copy-start | bytes 1179652
  0.6 6.5 %copy-start.3 = (bf16[1,32,7168]{2,1,0:T(8,128)(2,1)S(1)}, bf16[1,32,7168]{2,1,0:T(8,128)(2,1)}, u32[]{:S(2)}) copy-start(bf16[1,32,7168]{2,1,0:T(8,128)(2,1)} %param.8) | copy-start | bytes 1376260
  3.2 18.1 %collective-permute-start = (bf16[448,640]{1,0:T(8,128)(2,1)S(1)}, bf16[448,640]{1,0:T(8,128)(2,1)S(1)}, u32[]{:S(2)}, u32[]{:S(2)}) collective-permute-start(bf16[448,640]{1,0:T(8,128)(2,1)S(1)} %pad_maximum_fusion.8.refs_4_.refs_5_), channel_id=1, source_target_pairs={{0,1},{1,0},{2,3},{3,2},{4,5},{5,4},{6,7},{7,6},{8,9},{9,8},{10,11... | collective-permute-start | bytes 1720328 | tf_op jit(solution)/shard_map/ppermute | solution.py:39
  4.8 16.4 %collective-permute-start.1 = (bf16[448,640]{1,0:T(8,128)(2,1)S(1)}, bf16[448,640]{1,0:T(8,128)(2,1)S(1)}, u32[]{:S(2)}, u32[]{:S(2)}) collective-permute-start(bf16[448,640]{1,0:T(8,128)(2,1)S(1)} %pad_maximum_fusion.8.refs_4_.refs_5_), channel_id=1, source_target_pairs={{0,3},{1,2},{2,1},{3,0},{4,7},{5,6},{6,5},{7,4},{8,11},{9,10},{10,... | collective-permute-start | bytes 1720328 | tf_op jit(solution)/shard_map/ppermute | solution.py:39
  7.0 14.2 %collective-permute-start.2 = (bf16[448,640]{1,0:T(8,128)(2,1)S(1)}, bf16[448,640]{1,0:T(8,128)(2,1)S(1)}, u32[]{:S(2)}, u32[]{:S(2)}) collective-permute-start(bf16[448,640]{1,0:T(8,128)(2,1)S(1)} %pad_maximum_fusion.8.refs_4_.refs_5_), channel_id=1, source_target_pairs={{0,4},{1,5},{2,6},{3,7},{4,0},{5,1},{6,2},{7,3},{8,12},{9,13},{10,... | collective-permute-start | bytes 1720328 | tf_op jit(solution)/shard_map/ppermute | solution.py:39
  7.1 11.7 %collective-permute-start.3 = (bf16[32,7168]{1,0:T(8,128)(2,1)S(1)}, bf16[32,7168]{1,0:T(8,128)(2,1)}, u32[]{:S(2)}, u32[]{:S(2)}) collective-permute-start(bf16[32,7168]{1,0:T(8,128)(2,1)S(1)} %bitcast.67), channel_id=1, source_target_pairs={{0,32},{1,33},{2,34},{3,35},{4,36},{5,37},{6,38},{7,39},{8,40},{9,... | collective-permute-start | bytes 1376264 | tf_op jit(solution)/shard_map/ppermute | solution.py:39
  8.6 12.6 %collective-permute-start.4 = (bf16[32,7168]{1,0:T(8,128)(2,1)S(1)}, bf16[32,7168]{1,0:T(8,128)(2,1)}, u32[]{:S(2)}, u32[]{:S(2)}) collective-permute-start(bf16[32,7168]{1,0:T(8,128)(2,1)S(1)} %bitcast.68), channel_id=1, source_target_pairs={{0,96},{1,97},{2,98},{3,99},{4,100},{5,101},{6,102},{7,103},{8,104... | collective-permute-start | bytes 1376264 | tf_op jit(solution)/shard_map/ppermute | solution.py:39
  21.2 24.0 %collective-permute-start.8 = (bf16[32,7168]{1,0:T(8,128)(2,1)S(1)}, bf16[32,7168]{1,0:T(8,128)(2,1)S(1)}, u32[]{:S(2)}, u32[]{:S(2)}) collective-permute-start(bf16[32,7168]{1,0:T(8,128)(2,1)S(1)} %bitcast.69), channel_id=1, source_target_pairs={{0,140},{1,141},{2,142},{3,143},{4,136},{5,137},{6,138},{7,139},{8... | collective-permute-start | bytes 1376264 | tf_op jit(solution)/shard_map/ppermute | solution.py:39
  27.9 17.3 %collective-permute-start.9 = (bf16[32,7168]{1,0:T(8,128)(2,1)S(1)}, bf16[32,7168]{1,0:T(8,128)(2,1)S(1)}, u32[]{:S(2)}, u32[]{:S(2)}) collective-permute-start(bf16[32,7168]{1,0:T(8,128)(2,1)S(1)} %bitcast.70), channel_id=1, source_target_pairs={{0,64},{1,65},{2,66},{3,67},{4,68},{5,69},{6,70},{7,71},{8,72},{9,... | collective-permute-start | bytes 1376264 | tf_op jit(solution)/shard_map/ppermute | solution.py:39
  30.2 24.9 %collective-permute-start.5 = (bf16[672,640]{1,0:T(8,128)(2,1)S(1)}, bf16[672,640]{1,0:T(8,128)(2,1)S(1)}, u32[]{:S(2)}, u32[]{:S(2)}) collective-permute-start(bf16[672,640]{1,0:T(8,128)(2,1)S(1)} %get-tuple-element.129), channel_id=1, source_target_pairs={{0,1},{1,0},{2,3},{3,2},{4,5},{5,4},{6,7},{7,6},{8,9},{9,8},{10,11... | collective-permute-start | bytes 2580488 | tf_op jit(solution)/shard_map/ppermute | solution.py:39
  31.0 24.1 %collective-permute-start.6 = (bf16[672,640]{1,0:T(8,128)(2,1)S(1)}, bf16[672,640]{1,0:T(8,128)(2,1)S(1)}, u32[]{:S(2)}, u32[]{:S(2)}) collective-permute-start(bf16[672,640]{1,0:T(8,128)(2,1)S(1)} %get-tuple-element.128), channel_id=1, source_target_pairs={{0,3},{1,2},{2,1},{3,0},{4,7},{5,6},{6,5},{7,4},{8,11},{9,10},{10,... | collective-permute-start | bytes 2580488 | tf_op jit(solution)/shard_map/ppermute | solution.py:39
  32.0 23.2 %collective-permute-start.7 = (bf16[448,640]{1,0:T(8,128)(2,1)S(1)}, bf16[448,640]{1,0:T(8,128)(2,1)S(1)}, u32[]{:S(2)}, u32[]{:S(2)}) collective-permute-start(bf16[448,640]{1,0:T(8,128)(2,1)S(1)} %pad_maximum_fusion.8.refs_4_.refs_5_), channel_id=1, source_target_pairs={{0,8},{1,9},{2,10},{3,11},{4,12},{5,13},{6,14},{7,15},{8,0},{9,1},... | collective-permute-start | bytes 1720328 | tf_op jit(solution)/shard_map/ppermute | solution.py:39
  55.1 11.1 %collective-permute-start.13 = (bf16[32,7168]{1,0:T(8,128)(2,1)S(1)}, bf16[32,7168]{1,0:T(8,128)(2,1)S(1)}, u32[]{:S(2)}, u32[]{:S(2)}) collective-permute-start(bf16[32,7168]{1,0:T(8,128)(2,1)S(1)} %collective-permute-done.8), channel_id=1, source_target_pairs={{0,32},{1,33},{2,34},{3,35},{4,36},{5,37},{6,38},{7,39},{8,40},{9,... | collective-permute-start | bytes 1376264 | tf_op jit(solution)/shard_map/ppermute | solution.py:39
  55.8 12.0 %collective-permute-start.14 = (bf16[32,7168]{1,0:T(8,128)(2,1)S(1)}, bf16[32,7168]{1,0:T(8,128)(2,1)S(1)}, u32[]{:S(2)}, u32[]{:S(2)}) collective-permute-start(bf16[32,7168]{1,0:T(8,128)(2,1)S(1)} %collective-permute-done.8), channel_id=1, source_target_pairs={{0,96},{1,97},{2,98},{3,99},{4,100},{5,101},{6,102},{7,103},{8,104... | collective-permute-start | bytes 1376264 | tf_op jit(solution)/shard_map/ppermute | solution.py:39
  56.4 14.5 %collective-permute-start.12 = (bf16[448,640]{1,0:T(8,128)(2,1)S(1)}, bf16[448,640]{1,0:T(8,128)(2,1)S(1)}, u32[]{:S(2)}, u32[]{:S(2)}) collective-permute-start(bf16[448,640]{1,0:T(8,128)(2,1)S(1)} %collective-permute-done.7.refs_4_.refs_5_), channel_id=1, source_target_pairs={{0,4},{1,5},{2,6},{3,7},{4,0},{5,1},{6,2},{7,3},{8,12},{9,13},{10,... | collective-permute-start | bytes 1720328 | tf_op jit(solution)/shard_map/ppermute | solution.py:39
  59.6 19.2 %collective-permute-start.10 = (bf16[672,640]{1,0:T(8,128)(2,1)S(1)}, bf16[672,640]{1,0:T(8,128)(2,1)S(1)}, u32[]{:S(2)}, u32[]{:S(2)}) collective-permute-start(bf16[672,640]{1,0:T(8,128)(2,1)S(1)} %get-tuple-element.127), channel_id=1, source_target_pairs={{0,1},{1,0},{2,3},{3,2},{4,5},{5,4},{6,7},{7,6},{8,9},{9,8},{10,11... | collective-permute-start | bytes 2580488 | tf_op jit(solution)/shard_map/ppermute | solution.py:39
  60.7 20.0 %collective-permute-start.11 = (bf16[672,640]{1,0:T(8,128)(2,1)S(1)}, bf16[672,640]{1,0:T(8,128)(2,1)S(1)}, u32[]{:S(2)}, u32[]{:S(2)}) collective-permute-start(bf16[672,640]{1,0:T(8,128)(2,1)S(1)} %get-tuple-element.126), channel_id=1, source_target_pairs={{0,3},{1,2},{2,1},{3,0},{4,7},{5,6},{6,5},{7,4},{8,11},{9,10},{10,... | collective-permute-start | bytes 2580488 | tf_op jit(solution)/shard_map/ppermute | solution.py:39
  80.8 4.8 %collective-permute-start.18 = (bf16[128,7168]{1,0:T(8,128)(2,1)S(1)}, bf16[128,7168]{1,0:T(8,128)(2,1)S(1)}, u32[]{:S(2)}, u32[]{:S(2)}) collective-permute-start(bf16[128,7168]{1,0:T(8,128)(2,1)S(1)} %constant_dynamic-update-slice_fusion.rows_ref), channel_id=1, source_target_pairs={{0,16},{1,17},{2,18},{3,19},{4,20},{5,21},{6,22},{7,23},{8,24},{9,... | collective-permute-start | bytes 5505032 | tf_op jit(solution)/shard_map/ppermute | solution.py:39
  81.0 21.6 %collective-permute-start.15 = (bf16[672,640]{1,0:T(8,128)(2,1)S(1)}, bf16[672,640]{1,0:T(8,128)(2,1)S(1)}, u32[]{:S(2)}, u32[]{:S(2)}) collective-permute-start(bf16[672,640]{1,0:T(8,128)(2,1)S(1)} %get-tuple-element.125), channel_id=1, source_target_pairs={{0,1},{1,0},{2,3},{3,2},{4,5},{5,4},{6,7},{7,6},{8,9},{9,8},{10,11... | collective-permute-start | bytes 2580488 | tf_op jit(solution)/shard_map/ppermute | solution.py:39
  81.1 23.0 %collective-permute-start.16 = (bf16[672,640]{1,0:T(8,128)(2,1)S(1)}, bf16[672,640]{1,0:T(8,128)(2,1)S(1)}, u32[]{:S(2)}, u32[]{:S(2)}) collective-permute-start(bf16[672,640]{1,0:T(8,128)(2,1)S(1)} %get-tuple-element.124), channel_id=1, source_target_pairs={{0,3},{1,2},{2,1},{3,0},{4,7},{5,6},{6,5},{7,4},{8,11},{9,10},{10,... | collective-permute-start | bytes 2580488 | tf_op jit(solution)/shard_map/ppermute | solution.py:39
  82.9 14.2 %collective-permute-start.17 = (bf16[32,7168]{1,0:T(8,128)(2,1)S(1)}, bf16[32,7168]{1,0:T(8,128)(2,1)S(1)}, u32[]{:S(2)}, u32[]{:S(2)}) collective-permute-start(bf16[32,7168]{1,0:T(8,128)(2,1)S(1)} %collective-permute-done.8), channel_id=1, source_target_pairs={{0,64},{1,65},{2,66},{3,67},{4,68},{5,69},{6,70},{7,71},{8,72},{9,... | collective-permute-start | bytes 1376264 | tf_op jit(solution)/shard_map/ppermute | solution.py:39
  104.2 4.4 %collective-permute-start.19 = (bf16[128,7168]{1,0:T(8,128)(2,1)S(1)}, bf16[128,7168]{1,0:T(8,128)(2,1)S(1)}, u32[]{:S(2)}, u32[]{:S(2)}) collective-permute-start(bf16[128,7168]{1,0:T(8,128)(2,1)S(1)} %constant_dynamic-update-slice_fusion.4.rows_ref), channel_id=1, source_target_pairs={{0,16},{1,17},{2,18},{3,19},{4,20},{5,21},{6,22},{7,23},{8,24},{9,... | collective-permute-start | bytes 5505032 | tf_op jit(solution)/shard_map/ppermute | solution.py:39
  104.3 12.2 %collective-permute-start.20 = (bf16[224,640]{1,0:T(8,128)(2,1)S(1)}, bf16[224,640]{1,0:T(8,128)(2,1)S(1)}, u32[]{:S(2)}, u32[]{:S(2)}) collective-permute-start(bf16[224,640]{1,0:T(8,128)(2,1)S(1)} %slice.73), channel_id=1, source_target_pairs={{0,1},{1,0},{2,3},{3,2},{4,5},{5,4},{6,7},{7,6},{8,9},{9,8},{10,11... | collective-permute-start | bytes 860168 | tf_op jit(solution)/shard_map/ppermute | solution.py:39
  104.7 11.9 %collective-permute-start.21 = (bf16[224,640]{1,0:T(8,128)(2,1)S(1)}, bf16[224,640]{1,0:T(8,128)(2,1)S(1)}, u32[]{:S(2)}, u32[]{:S(2)}) collective-permute-start(bf16[224,640]{1,0:T(8,128)(2,1)S(1)} %slice.74), channel_id=1, source_target_pairs={{0,3},{1,2},{2,1},{3,0},{4,7},{5,6},{6,5},{7,4},{8,11},{9,10},{10,... | collective-permute-start | bytes 860168 | tf_op jit(solution)/shard_map/ppermute | solution.py:39
  119.8 3.5 %collective-permute-start.22 = (bf16[256,3072]{1,0:T(8,128)(2,1)S(1)}, bf16[256,3072]{1,0:T(8,128)(2,1)S(1)}, u32[]{:S(2)}, u32[]{:S(2)}) collective-permute-start(bf16[256,3072]{1,0:T(8,128)(2,1)S(1)} %project.3), channel_id=1, source_target_pairs={{0,16},{1,17},{2,18},{3,19},{4,20},{5,21},{6,22},{7,23},{8,24},{9,... | collective-permute-start | bytes 4718600 | tf_op jit(solution)/shard_map/ppermute | solution.py:39
  123.9 12.0 %collective-permute-start.23 = (bf16[2,32,3072]{2,1,0:T(8,128)(2,1)S(1)}, bf16[2,32,3072]{2,1,0:T(8,128)(2,1)S(1)}, u32[]{:S(2)}, u32[]{:S(2)}) collective-permute-start(bf16[2,32,3072]{2,1,0:T(8,128)(2,1)S(1)} %get-tuple-element.118), channel_id=1, source_target_pairs={{0,32},{1,33},{2,34},{3,35},{4,36},{5,37},{6,38},{7,39},{8,40},{9,... | collective-permute-start | bytes 1179656 | tf_op jit(solution)/shard_map/ppermute | solution.py:39
  125.0 20.4 %collective-permute-start.24 = (bf16[2,32,3072]{2,1,0:T(8,128)(2,1)S(1)}, bf16[2,32,3072]{2,1,0:T(8,128)(2,1)S(1)}, u32[]{:S(2)}, u32[]{:S(2)}) collective-permute-start(bf16[2,32,3072]{2,1,0:T(8,128)(2,1)S(1)} %get-tuple-element.120), channel_id=1, source_target_pairs={{0,64},{1,65},{2,66},{3,67},{4,68},{5,69},{6,70},{7,71},{8,72},{9,... | collective-permute-start | bytes 1179656 | tf_op jit(solution)/shard_map/ppermute | solution.py:39
  127.7 20.2 %collective-permute-start.25 = (bf16[2,32,3072]{2,1,0:T(8,128)(2,1)S(1)}, bf16[2,32,3072]{2,1,0:T(8,128)(2,1)S(1)}, u32[]{:S(2)}, u32[]{:S(2)}) collective-permute-start(bf16[2,32,3072]{2,1,0:T(8,128)(2,1)S(1)} %get-tuple-element.119), channel_id=1, source_target_pairs={{0,96},{1,97},{2,98},{3,99},{4,100},{5,101},{6,102},{7,103},{8,104... | collective-permute-start | bytes 1179656 | tf_op jit(solution)/shard_map/ppermute | solution.py:39
  130.0 31.5 %copy-start.2 = (bf16[1,128,1536]{2,1,0:T(8,128)(2,1)S(1)}, bf16[1,128,1536]{2,1,0:T(8,128)(2,1)}, u32[]{:S(2)}) copy-start(bf16[1,128,1536]{2,1,0:T(8,128)(2,1)} %param.15) | copy-start | bytes 1179652
  148.2 11.9 %collective-permute-start.27 = (bf16[448,512]{1,0:T(8,128)(2,1)S(1)}, bf16[448,512]{1,0:T(8,128)(2,1)S(1)}, u32[]{:S(2)}, u32[]{:S(2)}) collective-permute-start(bf16[448,512]{1,0:T(8,128)(2,1)S(1)} %get-tuple-element.111), channel_id=1, source_target_pairs={{0,1},{1,0},{2,3},{3,2},{4,5},{5,4},{6,7},{7,6},{8,9},{9,8},{10,11... | collective-permute-start | bytes 1376264 | tf_op jit(solution)/shard_map/ppermute | solution.py:39
  149.4 12.0 %collective-permute-start.28 = (bf16[448,512]{1,0:T(8,128)(2,1)S(1)}, bf16[448,512]{1,0:T(8,128)(2,1)S(1)}, u32[]{:S(2)}, u32[]{:S(2)}) collective-permute-start(bf16[448,512]{1,0:T(8,128)(2,1)S(1)} %get-tuple-element.111), channel_id=1, source_target_pairs={{0,3},{1,2},{2,1},{3,0},{4,7},{5,6},{6,5},{7,4},{8,11},{9,10},{10,... | collective-permute-start | bytes 1376264 | tf_op jit(solution)/shard_map/ppermute | solution.py:39
  151.2 8.8 %collective-permute-start.26 = (bf16[32,3072]{1,0:T(8,128)(2,1)S(1)}, bf16[32,3072]{1,0:T(8,128)(2,1)S(1)}, u32[]{:S(2)}, u32[]{:S(2)}) collective-permute-start(bf16[32,3072]{1,0:T(8,128)(2,1)S(1)} %fusion.4), channel_id=1, source_target_pairs={{0,140},{1,141},{2,142},{3,143},{4,136},{5,137},{6,138},{7,139},{8... | collective-permute-start | bytes 589832 | tf_op jit(solution)/shard_map/ppermute | solution.py:39
  164.8 4.8 %collective-permute-start.29 = (bf16[32,768]{1,0:T(8,128)(2,1)S(1)}, bf16[32,768]{1,0:T(8,128)(2,1)S(1)}, u32[]{:S(2)}, u32[]{:S(2)}) collective-permute-start(bf16[32,768]{1,0:T(8,128)(2,1)S(1)} %get-tuple-element.135), channel_id=1, source_target_pairs={{0,1},{1,0},{2,3},{3,2},{4,5},{5,4},{6,7},{7,6},{8,9},{9,8},{10,11... | collective-permute-start | bytes 147464 | tf_op jit(solution)/shard_map/ppermute | solution.py:39
  164.9 5.8 %collective-permute-start.30 = (bf16[32,768]{1,0:T(8,128)(2,1)S(1)}, bf16[32,768]{1,0:T(8,128)(2,1)S(1)}, u32[]{:S(2)}, u32[]{:S(2)}) collective-permute-start(bf16[32,768]{1,0:T(8,128)(2,1)S(1)} %get-tuple-element.134), channel_id=1, source_target_pairs={{0,2},{1,3},{2,0},{3,1},{4,6},{5,7},{6,4},{7,5},{8,10},{9,11},{10,... | collective-permute-start | bytes 147464 | tf_op jit(solution)/shard_map/ppermute | solution.py:39
  168.2 5.3 %collective-permute-start.31 = (bf16[32,768]{1,0:T(8,128)(2,1)S(1)}, bf16[32,768]{1,0:T(8,128)(2,1)S(1)}, u32[]{:S(2)}, u32[]{:S(2)}) collective-permute-start(bf16[32,768]{1,0:T(8,128)(2,1)S(1)} %get-tuple-element.133), channel_id=1, source_target_pairs={{0,3},{1,2},{2,1},{3,0},{4,7},{5,6},{6,5},{7,4},{8,11},{9,10},{10,... | collective-permute-start | bytes 147464 | tf_op jit(solution)/shard_map/ppermute | solution.py:39
  173.5 10.1 %collective-permute-start.33 = (bf16[448,512]{1,0:T(8,128)(2,1)S(1)}, bf16[448,512]{1,0:T(8,128)(2,1)S(1)}, u32[]{:S(2)}, u32[]{:S(2)}) collective-permute-start(bf16[448,512]{1,0:T(8,128)(2,1)S(1)} %get-tuple-element.111), channel_id=1, source_target_pairs={{0,2},{1,3},{2,0},{3,1},{4,6},{5,7},{6,4},{7,5},{8,10},{9,11},{10,... | collective-permute-start | bytes 1376264 | tf_op jit(solution)/shard_map/ppermute | solution.py:39
  173.9 8.7 %collective-permute-start.32 = (bf16[4,32,768]{2,1,0:T(8,128)(2,1)S(1)}, bf16[4,32,768]{2,1,0:T(8,128)(2,1)S(1)}, u32[]{:S(2)}, u32[]{:S(2)}) collective-permute-start(bf16[4,32,768]{2,1,0:T(8,128)(2,1)S(1)} %pad_maximum_fusion.10), channel_id=1, source_target_pairs={{0,140},{1,141},{2,142},{3,143},{4,136},{5,137},{6,138},{7,139},{8... | collective-permute-start | bytes 589832 | tf_op jit(solution)/shard_map/ppermute | solution.py:39
  183.7 10.0 %collective-permute-start.34 = (bf16[2,4,32,768]{3,2,1,0:T(8,128)(2,1)S(1)}, bf16[2,4,32,768]{3,2,1,0:T(8,128)(2,1)S(1)}, u32[]{:S(2)}, u32[]{:S(2)}) collective-permute-start(bf16[2,4,32,768]{3,2,1,0:T(8,128)(2,1)S(1)} %get-tuple-element.131), channel_id=1, source_target_pairs={{0,32},{1,33},{2,34},{3,35},{4,36},{5,37},{6,38},{7,39},{8,40},{9,... | collective-permute-start | bytes 1179656 | tf_op jit(solution)/shard_map/ppermute | solution.py:39
  186.5 11.7 %collective-permute-start.35 = (bf16[2,4,32,768]{3,2,1,0:T(8,128)(2,1)S(1)}, bf16[2,4,32,768]{3,2,1,0:T(8,128)(2,1)S(1)}, u32[]{:S(2)}, u32[]{:S(2)}) collective-permute-start(bf16[2,4,32,768]{3,2,1,0:T(8,128)(2,1)S(1)} %get-tuple-element.131), channel_id=1, source_target_pairs={{0,64},{1,65},{2,66},{3,67},{4,68},{5,69},{6,70},{7,71},{8,72},{9,... | collective-permute-start | bytes 1179656 | tf_op jit(solution)/shard_map/ppermute | solution.py:39
  187.2 13.6 %collective-permute-start.36 = (bf16[2,4,32,768]{3,2,1,0:T(8,128)(2,1)S(1)}, bf16[2,4,32,768]{3,2,1,0:T(8,128)(2,1)S(1)}, u32[]{:S(2)}, u32[]{:S(2)}) collective-permute-start(bf16[2,4,32,768]{3,2,1,0:T(8,128)(2,1)S(1)} %get-tuple-element.131), channel_id=1, source_target_pairs={{0,96},{1,97},{2,98},{3,99},{4,100},{5,101},{6,102},{7,103},{8,104... | collective-permute-start | bytes 1179656 | tf_op jit(solution)/shard_map/ppermute | solution.py:39
  200.9 3.5 %collective-permute-start.37 = (bf16[4,2,4,32,768]{4,3,2,1,0:T(8,128)(2,1)S(1)}, bf16[4,2,4,32,768]{4,3,2,1,0:T(8,128)(2,1)S(1)}, u32[]{:S(2)}, u32[]{:S(2)}) collective-permute-start(bf16[4,2,4,32,768]{4,3,2,1,0:T(8,128)(2,1)S(1)} %pad_maximum_fusion.1.a_ref), channel_id=1, source_target_pairs={{0,16},{1,17},{2,18},{3,19},{4,20},{5,21},{6,22},{7,23},{8,24},{9,... | collective-permute-start | bytes 4718600 | tf_op jit(solution)/shard_map/ppermute | solution.py:39
  204.4 25.8 %copy-start.1 = (bf16[1,128,1536]{2,1,0:T(8,128)(2,1)S(1)}, bf16[1,128,1536]{2,1,0:T(8,128)(2,1)}, u32[]{:S(2)}) copy-start(bf16[1,128,1536]{2,1,0:T(8,128)(2,1)} %param.10) | copy-start | bytes 1179652
  208.4 8.1 %collective-permute-start.38 = (bf16[192,448]{1,0:T(8,128)(2,1)S(1)}, bf16[192,448]{1,0:T(8,128)(2,1)S(1)}, u32[]{:S(2)}, u32[]{:S(2)}) collective-permute-start(bf16[192,448]{1,0:T(8,128)(2,1)S(1)} %get-tuple-element.121), channel_id=1, source_target_pairs={{0,4},{1,5},{2,6},{3,7},{4,0},{5,1},{6,2},{7,3},{8,12},{9,13},{10,... | collective-permute-start | bytes 516104 | tf_op jit(solution)/shard_map/ppermute | solution.py:39
  208.8 15.9 %collective-permute-start.39 = (bf16[192,448]{1,0:T(8,128)(2,1)S(1)}, bf16[192,448]{1,0:T(8,128)(2,1)S(1)}, u32[]{:S(2)}, u32[]{:S(2)}) collective-permute-start(bf16[192,448]{1,0:T(8,128)(2,1)S(1)} %get-tuple-element.123), channel_id=1, source_target_pairs={{0,8},{1,9},{2,10},{3,11},{4,12},{5,13},{6,14},{7,15},{8,0},{9,1},... | collective-permute-start | bytes 516104 | tf_op jit(solution)/shard_map/ppermute | solution.py:39
  211.0 18.4 %collective-permute-start.40 = (bf16[192,448]{1,0:T(8,128)(2,1)S(1)}, bf16[192,448]{1,0:T(8,128)(2,1)S(1)}, u32[]{:S(2)}, u32[]{:S(2)}) collective-permute-start(bf16[192,448]{1,0:T(8,128)(2,1)S(1)} %get-tuple-element.122), channel_id=1, source_target_pairs={{0,12},{1,13},{2,14},{3,15},{4,8},{5,9},{6,10},{7,11},{8,4},{9,5},... | collective-permute-start | bytes 516104 | tf_op jit(solution)/shard_map/ppermute | solution.py:39

commit v6 on v5

--- a/solution.py
+++ b/solution.py
@@ -343,7 +343,7 @@
         (y0, z1, own1, own3, block, rows)
     )
 
-    y1, z2 = around(y0, z1), send(block, ALONG_Z[2])
+    y1, z2 = around(y0, z1), send(z1, ALONG_Z[3])
     mirrored, own2 = send(rows, MIRROR), along_x(rows, 2)
     y1, z2, mirrored, own2 = lax.optimization_barrier((y1, z2, mirrored, own2))
 
@@ -361,7 +361,7 @@
     y3, far2 = around(y2, z3), along_x(mirrored, 2)
     own_b = send(own_a, CORE)
     own_b_normed = normalize(own_b, place)
-    y3, far2, own_b_normed = lax.optimization_barrier((y3, far2, own_b_normed))
+    y3, own_b_normed = lax.optimization_barrier((y3, own_b_normed))
 
     y4 = around(y3, None)
     far_a = jnp.concatenate([mirrored, far1, far2, far3])

time: 231 us -> 241 us (1.043)
  starting transfers between devices: 54.7 us -> 65.3 us
    ppermute x41, starting transfers between devices: 54.7 us -> 65.3 us  [send(): return lax.ppermute(array, AXES, table)]
  transfers between devices with their start and end apart: 41 -> 41, of which waited for: 29 -> 30; matrix products, arithmetic and copies ran while one was open for 3% -> 3% of each run, Pallas kernels for 7% -> 6%
where the time goes in v6:
time: 241 us
  waiting for transfers between devices  136 us (56%)
  starting transfers between devices  65.3 us (27%)
  Pallas kernels  26 us (11%)
  local copies, waits for them, and re-layouts  5.22 us (2%)
  matrix products  3.96 us (2%)
  other arithmetic  2.63 us (1%)
    ppermute x41, waiting for transfers between devices, send(): return lax.ppermute(array, AXES, table)  136 us
    ppermute x41, starting transfers between devices, send(): return lax.ppermute(array, AXES, table)  65.3 us
    pallas_call x4, Pallas kernels, normalize(): pl.pallas_call(norm_kernel, grid=(height // per,), in_specs=[pl.BlockSpec...  8.92 us
    pallas_call x4, Pallas kernels, layer(): pl.pallas_call(functools.partial(layer_kernel, finish=finish), grid_spec=...  7.79 us
  transfers between devices with their start and end apart: 41, of which 30 were waited for; matrix products, arithmetic and copies ran while one was open for 3% of the time, Pallas kernels for 6%

profile of v6, /device:TPU:32, one launch (start us, length us, event | category | flops | bytes accessed | tf_op | source)
XLA Modules:
  0.0 241.1 jit_solution(1627096862627581246)
XLA Ops:
  4.8 2.2 collective-permute-start.1
  8.6 2.1 collective-permute-start.4
  10.8 4.0 %convolution_convert_fusion.q_ref = bf16[128,1536]{1,0:T(8,128)(2,1)S(1)} fusion(bf16[1536,1536]{1,0:T(8,128)(2,1)} %param.14, bf16[1,128,1536]{2,1,0:T(8,128)(2,1)S(1)} %copy-done), kind=kOutput, calls=%fused_computation.1 | convolution fusion | flops 604176384 | bytes 5505024 | tf_op jit(solution)/shard_map/dot_general | solution.py:353
  14.8 4.1 %collective-permute-done.3 = bf16[32,7168]{1,0:T(8,128)(2,1)} collective-permute-done((bf16[32,7168]{1,0:T(8,128)(2,1)S(1)}, bf16[32,7168]{1,0:T(8,128)(2,1)}, u32[]{:S(2)}, u32[]{:S(2)}) %collective-permute-start.3) | collective-permute-done | bytes 458784 | tf_op jit(solution)/shard_map/ppermute | solution.py:39
  18.8 2.4 %collective-permute-done.4 = bf16[32,7168]{1,0:T(8,128)(2,1)} collective-permute-done((bf16[32,7168]{1,0:T(8,128)(2,1)S(1)}, bf16[32,7168]{1,0:T(8,128)(2,1)}, u32[]{:S(2)}, u32[]{:S(2)}) %collective-permute-start.4) | collective-permute-done | bytes 458784 | tf_op jit(solution)/shard_map/ppermute | solution.py:39
  21.2 6.7 %collective-permute-start.8 = (bf16[32,7168]{1,0:T(8,128)(2,1)S(1)}, bf16[32,7168]{1,0:T(8,128)(2,1)S(1)}, u32[]{:S(2)}, u32[]{:S(2)}) collective-permute-start(bf16[32,7168]{1,0:T(8,128)(2,1)S(1)} %bitcast.69), channel_id=1, source_target_pairs={{0,140},{1,141},{2,142},{3,143},{4,136},{5,137},{6,138},{7,139},{8... | collective-permute-start | bytes 1376264 | tf_op jit(solution)/shard_map/ppermute | solution.py:39
  27.9 2.1 collective-permute-start.9
  34.1 2.5 %collective-permute-done.8 = bf16[32,7168]{1,0:T(8,128)(2,1)S(1)} collective-permute-done((bf16[32,7168]{1,0:T(8,128)(2,1)S(1)}, bf16[32,7168]{1,0:T(8,128)(2,1)S(1)}, u32[]{:S(2)}, u32[]{:S(2)}) %collective-permute-start.8) | collective-permute-done | bytes 458784 | tf_op jit(solution)/shard_map/ppermute | solution.py:39
  36.6 2.8 %collective-permute-done.9 = bf16[32,7168]{1,0:T(8,128)(2,1)S(1)} collective-permute-done((bf16[32,7168]{1,0:T(8,128)(2,1)S(1)}, bf16[32,7168]{1,0:T(8,128)(2,1)S(1)}, u32[]{:S(2)}, u32[]{:S(2)}) %collective-permute-start.9) | collective-permute-done | bytes 458784 | tf_op jit(solution)/shard_map/ppermute | solution.py:39
  39.4 15.9 %collective-permute-done.7.refs_4_.refs_5_ = bf16[448,640]{1,0:T(8,128)(2,1)S(1)} collective-permute-done((bf16[448,640]{1,0:T(8,128)(2,1)S(1)}, bf16[448,640]{1,0:T(8,128)(2,1)S(1)}, u32[]{:S(2)}, u32[]{:S(2)}) %collective-permute-start.7) | collective-permute-done | bytes 573472 | tf_op jit(solution)/shard_map/ppermute | solution.py:39
  59.9 2.2 norm.4
  62.1 2.6 %collective-permute-done.13 = bf16[32,7168]{1,0:T(8,128)(2,1)S(1)} collective-permute-done((bf16[32,7168]{1,0:T(8,128)(2,1)S(1)}, bf16[32,7168]{1,0:T(8,128)(2,1)S(1)}, u32[]{:S(2)}, u32[]{:S(2)}) %collective-permute-start.13) | collective-permute-done | bytes 458784 | tf_op jit(solution)/shard_map/ppermute | solution.py:39
  66.1 3.1 %collective-permute-done.12.refs_4_.refs_5_ = bf16[448,640]{1,0:T(8,128)(2,1)S(1)} collective-permute-done((bf16[448,640]{1,0:T(8,128)(2,1)S(1)}, bf16[448,640]{1,0:T(8,128)(2,1)S(1)}, u32[]{:S(2)}, u32[]{:S(2)}) %collective-permute-start.12) | collective-permute-done | bytes 573472 | tf_op jit(solution)/shard_map/ppermute | solution.py:39
  69.2 6.4 %collective-permute-done.10.refs_8_.refs_6_.refs_7_ = bf16[672,640]{1,0:T(8,128)(2,1)S(1)} collective-permute-done((bf16[672,640]{1,0:T(8,128)(2,1)S(1)}, bf16[672,640]{1,0:T(8,128)(2,1)S(1)}, u32[]{:S(2)}, u32[]{:S(2)}) %collective-permute-start.10) | collective-permute-done | bytes 860192 | tf_op jit(solution)/shard_map/ppermute | solution.py:39
  79.0 8.6 %collective-permute-done.15 = bf16[32,7168]{1,0:T(8,128)(2,1)S(1)} collective-permute-done((bf16[32,7168]{1,0:T(8,128)(2,1)S(1)}, bf16[32,7168]{1,0:T(8,128)(2,1)S(1)}, u32[]{:S(2)}, u32[]{:S(2)}) %collective-permute-start.15) | collective-permute-done | bytes 458784 | tf_op jit(solution)/shard_map/ppermute | solution.py:39
  88.5 2.4 collective-permute-start.17
  90.8 2.2 norm.6
  93.1 16.8 %collective-permute-done.16.refs_8_.refs_6_.refs_7_ = bf16[672,640]{1,0:T(8,128)(2,1)S(1)} collective-permute-done((bf16[672,640]{1,0:T(8,128)(2,1)S(1)}, bf16[672,640]{1,0:T(8,128)(2,1)S(1)}, u32[]{:S(2)}, u32[]{:S(2)}) %collective-permute-start.16) | collective-permute-done | bytes 860192 | tf_op jit(solution)/shard_map/ppermute | solution.py:39
  111.7 2.3 collective-permute-start.21
  114.0 2.2 norm.5
  116.3 2.2 norm.7
  118.6 1.9 layer.4
  120.5 1.9 layer.5
  122.4 1.9 layer.6
  124.2 2.2 layer.7
  128.6 2.4 collective-permute-done.22
  133.8 2.5 %collective-permute-start.25 = (bf16[2,32,3072]{2,1,0:T(8,128)(2,1)S(1)}, bf16[2,32,3072]{2,1,0:T(8,128)(2,1)S(1)}, u32[]{:S(2)}, u32[]{:S(2)}) collective-permute-start(bf16[2,32,3072]{2,1,0:T(8,128)(2,1)S(1)} %get-tuple-element.117), channel_id=1, source_target_pairs={{0,96},{1,97},{2,98},{3,99},{4,100},{5,101},{6,102},{7,103},{8,104... | collective-permute-start | bytes 1179656 | tf_op jit(solution)/shard_map/ppermute | solution.py:39
  137.6 5.9 %collective-permute-done.23 = bf16[2,32,3072]{2,1,0:T(8,128)(2,1)S(1)} collective-permute-done((bf16[2,32,3072]{2,1,0:T(8,128)(2,1)S(1)}, bf16[2,32,3072]{2,1,0:T(8,128)(2,1)S(1)}, u32[]{:S(2)}, u32[]{:S(2)}) %collective-permute-start.23) | collective-permute-done | bytes 393248 | tf_op jit(solution)/shard_map/ppermute | solution.py:39
  143.6 7.9 %collective-permute-done.24 = bf16[2,32,3072]{2,1,0:T(8,128)(2,1)S(1)} collective-permute-done((bf16[2,32,3072]{2,1,0:T(8,128)(2,1)S(1)}, bf16[2,32,3072]{2,1,0:T(8,128)(2,1)S(1)}, u32[]{:S(2)}, u32[]{:S(2)}) %collective-permute-start.24) | collective-permute-done | bytes 393248 | tf_op jit(solution)/shard_map/ppermute | solution.py:39
  151.4 2.6 %collective-permute-done.25 = bf16[2,32,3072]{2,1,0:T(8,128)(2,1)S(1)} collective-permute-done((bf16[2,32,3072]{2,1,0:T(8,128)(2,1)S(1)}, bf16[2,32,3072]{2,1,0:T(8,128)(2,1)S(1)}, u32[]{:S(2)}, u32[]{:S(2)}) %collective-permute-start.25) | collective-permute-done | bytes 393248 | tf_op jit(solution)/shard_map/ppermute | solution.py:39
  156.6 5.2 %collective-permute-start.26 = (bf16[32,3072]{1,0:T(8,128)(2,1)S(1)}, bf16[32,3072]{1,0:T(8,128)(2,1)S(1)}, u32[]{:S(2)}, u32[]{:S(2)}) collective-permute-start(bf16[32,3072]{1,0:T(8,128)(2,1)S(1)} %fusion.4), channel_id=1, source_target_pairs={{0,140},{1,141},{2,142},{3,143},{4,136},{5,137},{6,138},{7,139},{8... | collective-permute-start | bytes 589832 | tf_op jit(solution)/shard_map/ppermute | solution.py:39
  161.8 3.7 %collective-permute-done.26.other_ref = bf16[32,3072]{1,0:T(8,128)(2,1)S(1)} collective-permute-done((bf16[32,3072]{1,0:T(8,128)(2,1)S(1)}, bf16[32,3072]{1,0:T(8,128)(2,1)S(1)}, u32[]{:S(2)}, u32[]{:S(2)}) %collective-permute-start.26) | collective-permute-done | bytes 196640 | tf_op jit(solution)/shard_map/ppermute | solution.py:39
  167.4 3.4 %attention.1 = (bf16[128,1536]{1,0:T(8,128)(2,1)}, bf16[4,32,768]{2,1,0:T(8,128)(2,1)S(1)}) custom-call(s32[3]{0:T(128)S(1)} %pad_add_fusion.place_ref, s32[1]{0:T(128)S(6)} %copy.28.images_ref, s32[1]{0:T(128)S(6)} %copy.29.lengths_ref, f32[32,3072]{1,0:T(8,128)S(1)} %slice_bitcast_fusion.4.own_ref, bf16[32,3072]{1,0:T(8,128)(2,1)S(1)} %collective-permute-done.26.other_ref, ...), custom_call_target="tpu_custom_call" | custom-call | tf_op jit(solution)/shard_map/attention/pallas_call | solution.py:245
  170.9 2.7 %collective-permute-start.30 = (bf16[32,768]{1,0:T(8,128)(2,1)S(1)}, bf16[32,768]{1,0:T(8,128)(2,1)S(1)}, u32[]{:S(2)}, u32[]{:S(2)}) collective-permute-start(bf16[32,768]{1,0:T(8,128)(2,1)S(1)} %get-tuple-element.132), channel_id=1, source_target_pairs={{0,2},{1,3},{2,0},{3,1},{4,6},{5,7},{6,4},{7,5},{8,10},{9,11},{10,... | collective-permute-start | bytes 147464 | tf_op jit(solution)/shard_map/ppermute | solution.py:39
  173.6 2.0 collective-permute-start.31
  176.5 2.3 collective-permute-done.31
  179.3 5.1 %collective-permute-start.32 = (bf16[4,32,768]{2,1,0:T(8,128)(2,1)S(1)}, bf16[4,32,768]{2,1,0:T(8,128)(2,1)S(1)}, u32[]{:S(2)}, u32[]{:S(2)}) collective-permute-start(bf16[4,32,768]{2,1,0:T(8,128)(2,1)S(1)} %pad_maximum_fusion.10), channel_id=1, source_target_pairs={{0,140},{1,141},{2,142},{3,143},{4,136},{5,137},{6,138},{7,139},{8... | collective-permute-start | bytes 589832 | tf_op jit(solution)/shard_map/ppermute | solution.py:39
  184.4 3.6 %collective-permute-done.32 = bf16[4,32,768]{2,1,0:T(8,128)(2,1)S(1)} collective-permute-done((bf16[4,32,768]{2,1,0:T(8,128)(2,1)S(1)}, bf16[4,32,768]{2,1,0:T(8,128)(2,1)S(1)}, u32[]{:S(2)}, u32[]{:S(2)}) %collective-permute-start.32) | collective-permute-done | bytes 196640 | tf_op jit(solution)/shard_map/ppermute | solution.py:39
  189.1 4.7 %collective-permute-start.35 = (bf16[2,4,32,768]{3,2,1,0:T(8,128)(2,1)S(1)}, bf16[2,4,32,768]{3,2,1,0:T(8,128)(2,1)S(1)}, u32[]{:S(2)}, u32[]{:S(2)}) collective-permute-start(bf16[2,4,32,768]{3,2,1,0:T(8,128)(2,1)S(1)} %get-tuple-element.129), channel_id=1, source_target_pairs={{0,64},{1,65},{2,66},{3,67},{4,68},{5,69},{6,70},{7,71},{8,72},{9,... | collective-permute-start | bytes 1179656 | tf_op jit(solution)/shard_map/ppermute | solution.py:39
  194.3 4.7 %collective-permute-done.34 = bf16[2,4,32,768]{3,2,1,0:T(8,128)(2,1)S(1)} collective-permute-done((bf16[2,4,32,768]{3,2,1,0:T(8,128)(2,1)S(1)}, bf16[2,4,32,768]{3,2,1,0:T(8,128)(2,1)S(1)}, u32[]{:S(2)}, u32[]{:S(2)}) %collective-permute-start.34) | collective-permute-done | bytes 393248 | tf_op jit(solution)/shard_map/ppermute | solution.py:39
  199.0 6.0 %collective-permute-done.35 = bf16[2,4,32,768]{3,2,1,0:T(8,128)(2,1)S(1)} collective-permute-done((bf16[2,4,32,768]{3,2,1,0:T(8,128)(2,1)S(1)}, bf16[2,4,32,768]{3,2,1,0:T(8,128)(2,1)S(1)}, u32[]{:S(2)}, u32[]{:S(2)}) %collective-permute-start.35) | collective-permute-done | bytes 393248 | tf_op jit(solution)/shard_map/ppermute | solution.py:39
  205.1 2.5 %collective-permute-done.36 = bf16[2,4,32,768]{3,2,1,0:T(8,128)(2,1)S(1)} collective-permute-done((bf16[2,4,32,768]{3,2,1,0:T(8,128)(2,1)S(1)}, bf16[2,4,32,768]{3,2,1,0:T(8,128)(2,1)S(1)}, u32[]{:S(2)}, u32[]{:S(2)}) %collective-permute-start.36) | collective-permute-done | bytes 393248 | tf_op jit(solution)/shard_map/ppermute | solution.py:39
  208.1 3.2 %collective-permute-done.37.b_ref = bf16[4,2,4,32,768]{4,3,2,1,0:T(8,128)(2,1)S(1)} collective-permute-done((bf16[4,2,4,32,768]{4,3,2,1,0:T(8,128)(2,1)S(1)}, bf16[4,2,4,32,768]{4,3,2,1,0:T(8,128)(2,1)S(1)}, u32[]{:S(2)}, u32[]{:S(2)}) %collective-permute-start.37) | collective-permute-done | bytes 1572896 | tf_op jit(solution)/shard_map/ppermute | solution.py:39
  211.3 3.9 %weight_grad.1 = (f32[192,448]{1,0:T(8,128)S(1)}, bf16[4,192,448]{2,1,0:T(8,128)(2,1)S(1)}) custom-call(s32[3]{0:T(128)S(1)} %pad_add_fusion.place_ref, bf16[4,2,4,32,768]{4,3,2,1,0:T(8,128)(2,1)S(1)} %pad_maximum_fusion.1.a_ref, bf16[4,2,4,32,768]{4,3,2,1,0:T(8,128)(2,1)S(1)} %collective-permute-done.37.b_ref, ...), custom_call_target="tpu_custom_call" | custom-call | tf_op jit(solution)/shard_map/weight_grad/pallas_call | solution.py:293
  215.3 5.8 %collective-permute-start.38 = (bf16[192,448]{1,0:T(8,128)(2,1)S(1)}, bf16[192,448]{1,0:T(8,128)(2,1)S(1)}, u32[]{:S(2)}, u32[]{:S(2)}) collective-permute-start(bf16[192,448]{1,0:T(8,128)(2,1)S(1)} %get-tuple-element.119), channel_id=1, source_target_pairs={{0,4},{1,5},{2,6},{3,7},{4,0},{5,1},{6,2},{7,3},{8,12},{9,13},{10,... | collective-permute-start | bytes 516104 | tf_op jit(solution)/shard_map/ppermute | solution.py:39
  222.6 6.3 %collective-permute-done.38 = bf16[192,448]{1,0:T(8,128)(2,1)S(1)} collective-permute-done((bf16[192,448]{1,0:T(8,128)(2,1)S(1)}, bf16[192,448]{1,0:T(8,128)(2,1)S(1)}, u32[]{:S(2)}, u32[]{:S(2)}) %collective-permute-start.38) | collective-permute-done | bytes 172064 | tf_op jit(solution)/shard_map/ppermute | solution.py:39
  229.0 6.4 %collective-permute-done.39 = bf16[192,448]{1,0:T(8,128)(2,1)S(1)} collective-permute-done((bf16[192,448]{1,0:T(8,128)(2,1)S(1)}, bf16[192,448]{1,0:T(8,128)(2,1)S(1)}, u32[]{:S(2)}, u32[]{:S(2)}) %collective-permute-start.39) | collective-permute-done | bytes 172064 | tf_op jit(solution)/shard_map/ppermute | solution.py:39
  235.4 4.9 %collective-permute-done.40 = bf16[192,448]{1,0:T(8,128)(2,1)S(1)} collective-permute-done((bf16[192,448]{1,0:T(8,128)(2,1)S(1)}, bf16[192,448]{1,0:T(8,128)(2,1)S(1)}, u32[]{:S(2)}, u32[]{:S(2)}) %collective-permute-start.40) | collective-permute-done | bytes 172064 | tf_op jit(solution)/shard_map/ppermute | solution.py:39
  (91 shorter events, 37.5 us)
Async XLA Ops:
  0.6 10.1 %copy-start = (bf16[1,128,1536]{2,1,0:T(8,128)(2,1)S(1)}, bf16[1,128,1536]{2,1,0:T(8,128)(2,1)}, u32[]{:S(2)}) copy-start(bf16[1,128,1536]{2,1,0:T(8,128)(2,1)} %param.10) | copy-start | bytes 1179652
  0.6 6.5 %copy-start.3 = (bf16[1,32,7168]{2,1,0:T(8,128)(2,1)S(1)}, bf16[1,32,7168]{2,1,0:T(8,128)(2,1)}, u32[]{:S(2)}) copy-start(bf16[1,32,7168]{2,1,0:T(8,128)(2,1)} %param.8) | copy-start | bytes 1376260
  3.2 18.1 %collective-permute-start = (bf16[448,640]{1,0:T(8,128)(2,1)S(1)}, bf16[448,640]{1,0:T(8,128)(2,1)S(1)}, u32[]{:S(2)}, u32[]{:S(2)}) collective-permute-start(bf16[448,640]{1,0:T(8,128)(2,1)S(1)} %pad_maximum_fusion.8.refs_4_.refs_5_), channel_id=1, source_target_pairs={{0,1},{1,0},{2,3},{3,2},{4,5},{5,4},{6,7},{7,6},{8,9},{9,8},{10,11... | collective-permute-start | bytes 1720328 | tf_op jit(solution)/shard_map/ppermute | solution.py:39
  4.8 16.4 %collective-permute-start.1 = (bf16[448,640]{1,0:T(8,128)(2,1)S(1)}, bf16[448,640]{1,0:T(8,128)(2,1)S(1)}, u32[]{:S(2)}, u32[]{:S(2)}) collective-permute-start(bf16[448,640]{1,0:T(8,128)(2,1)S(1)} %pad_maximum_fusion.8.refs_4_.refs_5_), channel_id=1, source_target_pairs={{0,3},{1,2},{2,1},{3,0},{4,7},{5,6},{6,5},{7,4},{8,11},{9,10},{10,... | collective-permute-start | bytes 1720328 | tf_op jit(solution)/shard_map/ppermute | solution.py:39
  7.0 14.2 %collective-permute-start.2 = (bf16[448,640]{1,0:T(8,128)(2,1)S(1)}, bf16[448,640]{1,0:T(8,128)(2,1)S(1)}, u32[]{:S(2)}, u32[]{:S(2)}) collective-permute-start(bf16[448,640]{1,0:T(8,128)(2,1)S(1)} %pad_maximum_fusion.8.refs_4_.refs_5_), channel_id=1, source_target_pairs={{0,4},{1,5},{2,6},{3,7},{4,0},{5,1},{6,2},{7,3},{8,12},{9,13},{10,... | collective-permute-start | bytes 1720328 | tf_op jit(solution)/shard_map/ppermute | solution.py:39
  7.1 11.7 %collective-permute-start.3 = (bf16[32,7168]{1,0:T(8,128)(2,1)S(1)}, bf16[32,7168]{1,0:T(8,128)(2,1)}, u32[]{:S(2)}, u32[]{:S(2)}) collective-permute-start(bf16[32,7168]{1,0:T(8,128)(2,1)S(1)} %bitcast.67), channel_id=1, source_target_pairs={{0,32},{1,33},{2,34},{3,35},{4,36},{5,37},{6,38},{7,39},{8,40},{9,... | collective-permute-start | bytes 1376264 | tf_op jit(solution)/shard_map/ppermute | solution.py:39
  8.6 12.6 %collective-permute-start.4 = (bf16[32,7168]{1,0:T(8,128)(2,1)S(1)}, bf16[32,7168]{1,0:T(8,128)(2,1)}, u32[]{:S(2)}, u32[]{:S(2)}) collective-permute-start(bf16[32,7168]{1,0:T(8,128)(2,1)S(1)} %bitcast.68), channel_id=1, source_target_pairs={{0,96},{1,97},{2,98},{3,99},{4,100},{5,101},{6,102},{7,103},{8,104... | collective-permute-start | bytes 1376264 | tf_op jit(solution)/shard_map/ppermute | solution.py:39
  21.2 15.3 %collective-permute-start.8 = (bf16[32,7168]{1,0:T(8,128)(2,1)S(1)}, bf16[32,7168]{1,0:T(8,128)(2,1)S(1)}, u32[]{:S(2)}, u32[]{:S(2)}) collective-permute-start(bf16[32,7168]{1,0:T(8,128)(2,1)S(1)} %bitcast.69), channel_id=1, source_target_pairs={{0,140},{1,141},{2,142},{3,143},{4,136},{5,137},{6,138},{7,139},{8... | collective-permute-start | bytes 1376264 | tf_op jit(solution)/shard_map/ppermute | solution.py:39
  27.9 11.4 %collective-permute-start.9 = (bf16[32,7168]{1,0:T(8,128)(2,1)S(1)}, bf16[32,7168]{1,0:T(8,128)(2,1)S(1)}, u32[]{:S(2)}, u32[]{:S(2)}) collective-permute-start(bf16[32,7168]{1,0:T(8,128)(2,1)S(1)} %bitcast.70), channel_id=1, source_target_pairs={{0,64},{1,65},{2,66},{3,67},{4,68},{5,69},{6,70},{7,71},{8,72},{9,... | collective-permute-start | bytes 1376264 | tf_op jit(solution)/shard_map/ppermute | solution.py:39
  30.1 25.2 %collective-permute-start.7 = (bf16[448,640]{1,0:T(8,128)(2,1)S(1)}, bf16[448,640]{1,0:T(8,128)(2,1)S(1)}, u32[]{:S(2)}, u32[]{:S(2)}) collective-permute-start(bf16[448,640]{1,0:T(8,128)(2,1)S(1)} %collective-permute-done.2.refs_4_.refs_5_), channel_id=1, source_target_pairs={{0,12},{1,13},{2,14},{3,15},{4,8},{5,9},{6,10},{7,11},{8,4},{9,5},... | collective-permute-start | bytes 1720328 | tf_op jit(solution)/shard_map/ppermute | solution.py:39
  31.3 23.9 %collective-permute-start.5 = (bf16[672,640]{1,0:T(8,128)(2,1)S(1)}, bf16[672,640]{1,0:T(8,128)(2,1)S(1)}, u32[]{:S(2)}, u32[]{:S(2)}) collective-permute-start(bf16[672,640]{1,0:T(8,128)(2,1)S(1)} %get-tuple-element.127), channel_id=1, source_target_pairs={{0,1},{1,0},{2,3},{3,2},{4,5},{5,4},{6,7},{7,6},{8,9},{9,8},{10,11... | collective-permute-start | bytes 2580488 | tf_op jit(solution)/shard_map/ppermute | solution.py:39
  32.1 23.2 %collective-permute-start.6 = (bf16[672,640]{1,0:T(8,128)(2,1)S(1)}, bf16[672,640]{1,0:T(8,128)(2,1)S(1)}, u32[]{:S(2)}, u32[]{:S(2)}) collective-permute-start(bf16[672,640]{1,0:T(8,128)(2,1)S(1)} %get-tuple-element.126), channel_id=1, source_target_pairs={{0,3},{1,2},{2,1},{3,0},{4,7},{5,6},{6,5},{7,4},{8,11},{9,10},{10,... | collective-permute-start | bytes 2580488 | tf_op jit(solution)/shard_map/ppermute | solution.py:39
  55.3 9.5 %collective-permute-start.13 = (bf16[32,7168]{1,0:T(8,128)(2,1)S(1)}, bf16[32,7168]{1,0:T(8,128)(2,1)S(1)}, u32[]{:S(2)}, u32[]{:S(2)}) collective-permute-start(bf16[32,7168]{1,0:T(8,128)(2,1)S(1)} %collective-permute-done.8), channel_id=1, source_target_pairs={{0,32},{1,33},{2,34},{3,35},{4,36},{5,37},{6,38},{7,39},{8,40},{9,... | collective-permute-start | bytes 1376264 | tf_op jit(solution)/shard_map/ppermute | solution.py:39
  55.8 10.3 %collective-permute-start.14 = (bf16[32,7168]{1,0:T(8,128)(2,1)S(1)}, bf16[32,7168]{1,0:T(8,128)(2,1)S(1)}, u32[]{:S(2)}, u32[]{:S(2)}) collective-permute-start(bf16[32,7168]{1,0:T(8,128)(2,1)S(1)} %collective-permute-done.8), channel_id=1, source_target_pairs={{0,96},{1,97},{2,98},{3,99},{4,100},{5,101},{6,102},{7,103},{8,104... | collective-permute-start | bytes 1376264 | tf_op jit(solution)/shard_map/ppermute | solution.py:39
  56.6 12.6 %collective-permute-start.12 = (bf16[448,640]{1,0:T(8,128)(2,1)S(1)}, bf16[448,640]{1,0:T(8,128)(2,1)S(1)}, u32[]{:S(2)}, u32[]{:S(2)}) collective-permute-start(bf16[448,640]{1,0:T(8,128)(2,1)S(1)} %collective-permute-done.7.refs_4_.refs_5_), channel_id=1, source_target_pairs={{0,4},{1,5},{2,6},{3,7},{4,0},{5,1},{6,2},{7,3},{8,12},{9,13},{10,... | collective-permute-start | bytes 1720328 | tf_op jit(solution)/shard_map/ppermute | solution.py:39
  56.9 18.7 %collective-permute-start.10 = (bf16[672,640]{1,0:T(8,128)(2,1)S(1)}, bf16[672,640]{1,0:T(8,128)(2,1)S(1)}, u32[]{:S(2)}, u32[]{:S(2)}) collective-permute-start(bf16[672,640]{1,0:T(8,128)(2,1)S(1)} %get-tuple-element.125), channel_id=1, source_target_pairs={{0,1},{1,0},{2,3},{3,2},{4,5},{5,4},{6,7},{7,6},{8,9},{9,8},{10,11... | collective-permute-start | bytes 2580488 | tf_op jit(solution)/shard_map/ppermute | solution.py:39
  57.6 19.6 %collective-permute-start.11 = (bf16[672,640]{1,0:T(8,128)(2,1)S(1)}, bf16[672,640]{1,0:T(8,128)(2,1)S(1)}, u32[]{:S(2)}, u32[]{:S(2)}) collective-permute-start(bf16[672,640]{1,0:T(8,128)(2,1)S(1)} %get-tuple-element.124), channel_id=1, source_target_pairs={{0,3},{1,2},{2,1},{3,0},{4,7},{5,6},{6,5},{7,4},{8,11},{9,10},{10,... | collective-permute-start | bytes 2580488 | tf_op jit(solution)/shard_map/ppermute | solution.py:39
  77.2 10.4 %collective-permute-start.15 = (bf16[32,7168]{1,0:T(8,128)(2,1)S(1)}, bf16[32,7168]{1,0:T(8,128)(2,1)S(1)}, u32[]{:S(2)}, u32[]{:S(2)}) collective-permute-start(bf16[32,7168]{1,0:T(8,128)(2,1)S(1)} %collective-permute-done.8), channel_id=1, source_target_pairs={{0,64},{1,65},{2,66},{3,67},{4,68},{5,69},{6,70},{7,71},{8,72},{9,... | collective-permute-start | bytes 1376264 | tf_op jit(solution)/shard_map/ppermute | solution.py:39
  79.0 11.8 %collective-permute-start.18 = (bf16[128,7168]{1,0:T(8,128)(2,1)S(1)}, bf16[128,7168]{1,0:T(8,128)(2,1)S(1)}, u32[]{:S(2)}, u32[]{:S(2)}) collective-permute-start(bf16[128,7168]{1,0:T(8,128)(2,1)S(1)} %constant_dynamic-update-slice_fusion.rows_ref), channel_id=1, source_target_pairs={{0,16},{1,17},{2,18},{3,19},{4,20},{5,21},{6,22},{7,23},{8,24},{9,... | collective-permute-start | bytes 5505032 | tf_op jit(solution)/shard_map/ppermute | solution.py:39
  87.7 28.5 %collective-permute-start.19 = (bf16[128,7168]{1,0:T(8,128)(2,1)S(1)}, bf16[128,7168]{1,0:T(8,128)(2,1)S(1)}, u32[]{:S(2)}, u32[]{:S(2)}) collective-permute-start(bf16[128,7168]{1,0:T(8,128)(2,1)S(1)} %constant_dynamic-update-slice_fusion.4.rows_ref), channel_id=1, source_target_pairs={{0,16},{1,17},{2,18},{3,19},{4,20},{5,21},{6,22},{7,23},{8,24},{9,... | collective-permute-start | bytes 5505032 | tf_op jit(solution)/shard_map/ppermute | solution.py:39
  88.2 21.6 %collective-permute-start.16 = (bf16[672,640]{1,0:T(8,128)(2,1)S(1)}, bf16[672,640]{1,0:T(8,128)(2,1)S(1)}, u32[]{:S(2)}, u32[]{:S(2)}) collective-permute-start(bf16[672,640]{1,0:T(8,128)(2,1)S(1)} %get-tuple-element.123), channel_id=1, source_target_pairs={{0,1},{1,0},{2,3},{3,2},{4,5},{5,4},{6,7},{7,6},{8,9},{9,8},{10,11... | collective-permute-start | bytes 2580488 | tf_op jit(solution)/shard_map/ppermute | solution.py:39
  88.5 22.7 %collective-permute-start.17 = (bf16[672,640]{1,0:T(8,128)(2,1)S(1)}, bf16[672,640]{1,0:T(8,128)(2,1)S(1)}, u32[]{:S(2)}, u32[]{:S(2)}) collective-permute-start(bf16[672,640]{1,0:T(8,128)(2,1)S(1)} %get-tuple-element.122), channel_id=1, source_target_pairs={{0,3},{1,2},{2,1},{3,0},{4,7},{5,6},{6,5},{7,4},{8,11},{9,10},{10,... | collective-permute-start | bytes 2580488 | tf_op jit(solution)/shard_map/ppermute | solution.py:39
  111.2 13.1 %collective-permute-start.20 = (bf16[224,640]{1,0:T(8,128)(2,1)S(1)}, bf16[224,640]{1,0:T(8,128)(2,1)S(1)}, u32[]{:S(2)}, u32[]{:S(2)}) collective-permute-start(bf16[224,640]{1,0:T(8,128)(2,1)S(1)} %slice.73), channel_id=1, source_target_pairs={{0,1},{1,0},{2,3},{3,2},{4,5},{5,4},{6,7},{7,6},{8,9},{9,8},{10,11... | collective-permute-start | bytes 860168 | tf_op jit(solution)/shard_map/ppermute | solution.py:39
  111.7 12.5 %collective-permute-start.21 = (bf16[224,640]{1,0:T(8,128)(2,1)S(1)}, bf16[224,640]{1,0:T(8,128)(2,1)S(1)}, u32[]{:S(2)}, u32[]{:S(2)}) collective-permute-start(bf16[224,640]{1,0:T(8,128)(2,1)S(1)} %slice.74), channel_id=1, source_target_pairs={{0,3},{1,2},{2,1},{3,0},{4,7},{5,6},{6,5},{7,4},{8,11},{9,10},{10,... | collective-permute-start | bytes 860168 | tf_op jit(solution)/shard_map/ppermute | solution.py:39
  127.5 3.5 %collective-permute-start.22 = (bf16[256,3072]{1,0:T(8,128)(2,1)S(1)}, bf16[256,3072]{1,0:T(8,128)(2,1)S(1)}, u32[]{:S(2)}, u32[]{:S(2)}) collective-permute-start(bf16[256,3072]{1,0:T(8,128)(2,1)S(1)} %project.3), channel_id=1, source_target_pairs={{0,16},{1,17},{2,18},{3,19},{4,20},{5,21},{6,22},{7,23},{8,24},{9,... | collective-permute-start | bytes 4718600 | tf_op jit(solution)/shard_map/ppermute | solution.py:39
  131.5 12.0 %collective-permute-start.23 = (bf16[2,32,3072]{2,1,0:T(8,128)(2,1)S(1)}, bf16[2,32,3072]{2,1,0:T(8,128)(2,1)S(1)}, u32[]{:S(2)}, u32[]{:S(2)}) collective-permute-start(bf16[2,32,3072]{2,1,0:T(8,128)(2,1)S(1)} %get-tuple-element.116), channel_id=1, source_target_pairs={{0,32},{1,33},{2,34},{3,35},{4,36},{5,37},{6,38},{7,39},{8,40},{9,... | collective-permute-start | bytes 1179656 | tf_op jit(solution)/shard_map/ppermute | solution.py:39
  132.5 19.0 %collective-permute-start.24 = (bf16[2,32,3072]{2,1,0:T(8,128)(2,1)S(1)}, bf16[2,32,3072]{2,1,0:T(8,128)(2,1)S(1)}, u32[]{:S(2)}, u32[]{:S(2)}) collective-permute-start(bf16[2,32,3072]{2,1,0:T(8,128)(2,1)S(1)} %get-tuple-element.118), channel_id=1, source_target_pairs={{0,64},{1,65},{2,66},{3,67},{4,68},{5,69},{6,70},{7,71},{8,72},{9,... | collective-permute-start | bytes 1179656 | tf_op jit(solution)/shard_map/ppermute | solution.py:39
  133.8 20.2 %collective-permute-start.25 = (bf16[2,32,3072]{2,1,0:T(8,128)(2,1)S(1)}, bf16[2,32,3072]{2,1,0:T(8,128)(2,1)S(1)}, u32[]{:S(2)}, u32[]{:S(2)}) collective-permute-start(bf16[2,32,3072]{2,1,0:T(8,128)(2,1)S(1)} %get-tuple-element.117), channel_id=1, source_target_pairs={{0,96},{1,97},{2,98},{3,99},{4,100},{5,101},{6,102},{7,103},{8,104... | collective-permute-start | bytes 1179656 | tf_op jit(solution)/shard_map/ppermute | solution.py:39
  137.6 29.7 %copy-start.2 = (bf16[1,128,1536]{2,1,0:T(8,128)(2,1)S(1)}, bf16[1,128,1536]{2,1,0:T(8,128)(2,1)}, u32[]{:S(2)}) copy-start(bf16[1,128,1536]{2,1,0:T(8,128)(2,1)} %param.15) | copy-start | bytes 1179652
  154.2 11.3 %collective-permute-start.27 = (bf16[448,512]{1,0:T(8,128)(2,1)S(1)}, bf16[448,512]{1,0:T(8,128)(2,1)S(1)}, u32[]{:S(2)}, u32[]{:S(2)}) collective-permute-start(bf16[448,512]{1,0:T(8,128)(2,1)S(1)} %get-tuple-element.109), channel_id=1, source_target_pairs={{0,1},{1,0},{2,3},{3,2},{4,5},{5,4},{6,7},{7,6},{8,9},{9,8},{10,11... | collective-permute-start | bytes 1376264 | tf_op jit(solution)/shard_map/ppermute | solution.py:39
  155.3 12.0 %collective-permute-start.28 = (bf16[448,512]{1,0:T(8,128)(2,1)S(1)}, bf16[448,512]{1,0:T(8,128)(2,1)S(1)}, u32[]{:S(2)}, u32[]{:S(2)}) collective-permute-start(bf16[448,512]{1,0:T(8,128)(2,1)S(1)} %get-tuple-element.109), channel_id=1, source_target_pairs={{0,3},{1,2},{2,1},{3,0},{4,7},{5,6},{6,5},{7,4},{8,11},{9,10},{10,... | collective-permute-start | bytes 1376264 | tf_op jit(solution)/shard_map/ppermute | solution.py:39
  156.6 8.9 %collective-permute-start.26 = (bf16[32,3072]{1,0:T(8,128)(2,1)S(1)}, bf16[32,3072]{1,0:T(8,128)(2,1)S(1)}, u32[]{:S(2)}, u32[]{:S(2)}) collective-permute-start(bf16[32,3072]{1,0:T(8,128)(2,1)S(1)} %fusion.4), channel_id=1, source_target_pairs={{0,140},{1,141},{2,142},{3,143},{4,136},{5,137},{6,138},{7,139},{8... | collective-permute-start | bytes 589832 | tf_op jit(solution)/shard_map/ppermute | solution.py:39
  170.8 4.8 %collective-permute-start.29 = (bf16[32,768]{1,0:T(8,128)(2,1)S(1)}, bf16[32,768]{1,0:T(8,128)(2,1)S(1)}, u32[]{:S(2)}, u32[]{:S(2)}) collective-permute-start(bf16[32,768]{1,0:T(8,128)(2,1)S(1)} %get-tuple-element.133), channel_id=1, source_target_pairs={{0,1},{1,0},{2,3},{3,2},{4,5},{5,4},{6,7},{7,6},{8,9},{9,8},{10,11... | collective-permute-start | bytes 147464 | tf_op jit(solution)/shard_map/ppermute | solution.py:39
  170.9 5.7 %collective-permute-start.30 = (bf16[32,768]{1,0:T(8,128)(2,1)S(1)}, bf16[32,768]{1,0:T(8,128)(2,1)S(1)}, u32[]{:S(2)}, u32[]{:S(2)}) collective-permute-start(bf16[32,768]{1,0:T(8,128)(2,1)S(1)} %get-tuple-element.132), channel_id=1, source_target_pairs={{0,2},{1,3},{2,0},{3,1},{4,6},{5,7},{6,4},{7,5},{8,10},{9,11},{10,... | collective-permute-start | bytes 147464 | tf_op jit(solution)/shard_map/ppermute | solution.py:39
  173.6 5.3 %collective-permute-start.31 = (bf16[32,768]{1,0:T(8,128)(2,1)S(1)}, bf16[32,768]{1,0:T(8,128)(2,1)S(1)}, u32[]{:S(2)}, u32[]{:S(2)}) collective-permute-start(bf16[32,768]{1,0:T(8,128)(2,1)S(1)} %get-tuple-element.131), channel_id=1, source_target_pairs={{0,3},{1,2},{2,1},{3,0},{4,7},{5,6},{6,5},{7,4},{8,11},{9,10},{10,... | collective-permute-start | bytes 147464 | tf_op jit(solution)/shard_map/ppermute | solution.py:39
  178.9 10.1 %collective-permute-start.33 = (bf16[448,512]{1,0:T(8,128)(2,1)S(1)}, bf16[448,512]{1,0:T(8,128)(2,1)S(1)}, u32[]{:S(2)}, u32[]{:S(2)}) collective-permute-start(bf16[448,512]{1,0:T(8,128)(2,1)S(1)} %get-tuple-element.109), channel_id=1, source_target_pairs={{0,2},{1,3},{2,0},{3,1},{4,6},{5,7},{6,4},{7,5},{8,10},{9,11},{10,... | collective-permute-start | bytes 1376264 | tf_op jit(solution)/shard_map/ppermute | solution.py:39
  179.3 8.7 %collective-permute-start.32 = (bf16[4,32,768]{2,1,0:T(8,128)(2,1)S(1)}, bf16[4,32,768]{2,1,0:T(8,128)(2,1)S(1)}, u32[]{:S(2)}, u32[]{:S(2)}) collective-permute-start(bf16[4,32,768]{2,1,0:T(8,128)(2,1)S(1)} %pad_maximum_fusion.10), channel_id=1, source_target_pairs={{0,140},{1,141},{2,142},{3,143},{4,136},{5,137},{6,138},{7,139},{8... | collective-permute-start | bytes 589832 | tf_op jit(solution)/shard_map/ppermute | solution.py:39
  189.0 10.0 %collective-permute-start.34 = (bf16[2,4,32,768]{3,2,1,0:T(8,128)(2,1)S(1)}, bf16[2,4,32,768]{3,2,1,0:T(8,128)(2,1)S(1)}, u32[]{:S(2)}, u32[]{:S(2)}) collective-permute-start(bf16[2,4,32,768]{3,2,1,0:T(8,128)(2,1)S(1)} %get-tuple-element.129), channel_id=1, source_target_pairs={{0,32},{1,33},{2,34},{3,35},{4,36},{5,37},{6,38},{7,39},{8,40},{9,... | collective-permute-start | bytes 1179656 | tf_op jit(solution)/shard_map/ppermute | solution.py:39
  189.1 15.9 %collective-permute-start.35 = (bf16[2,4,32,768]{3,2,1,0:T(8,128)(2,1)S(1)}, bf16[2,4,32,768]{3,2,1,0:T(8,128)(2,1)S(1)}, u32[]{:S(2)}, u32[]{:S(2)}) collective-permute-start(bf16[2,4,32,768]{3,2,1,0:T(8,128)(2,1)S(1)} %get-tuple-element.129), channel_id=1, source_target_pairs={{0,64},{1,65},{2,66},{3,67},{4,68},{5,69},{6,70},{7,71},{8,72},{9,... | collective-permute-start | bytes 1179656 | tf_op jit(solution)/shard_map/ppermute | solution.py:39
  193.8 13.8 %collective-permute-start.36 = (bf16[2,4,32,768]{3,2,1,0:T(8,128)(2,1)S(1)}, bf16[2,4,32,768]{3,2,1,0:T(8,128)(2,1)S(1)}, u32[]{:S(2)}, u32[]{:S(2)}) collective-permute-start(bf16[2,4,32,768]{3,2,1,0:T(8,128)(2,1)S(1)} %get-tuple-element.129), channel_id=1, source_target_pairs={{0,96},{1,97},{2,98},{3,99},{4,100},{5,101},{6,102},{7,103},{8,104... | collective-permute-start | bytes 1179656 | tf_op jit(solution)/shard_map/ppermute | solution.py:39
  207.8 3.5 %collective-permute-start.37 = (bf16[4,2,4,32,768]{4,3,2,1,0:T(8,128)(2,1)S(1)}, bf16[4,2,4,32,768]{4,3,2,1,0:T(8,128)(2,1)S(1)}, u32[]{:S(2)}, u32[]{:S(2)}) collective-permute-start(bf16[4,2,4,32,768]{4,3,2,1,0:T(8,128)(2,1)S(1)} %pad_maximum_fusion.1.a_ref), channel_id=1, source_target_pairs={{0,16},{1,17},{2,18},{3,19},{4,20},{5,21},{6,22},{7,23},{8,24},{9,... | collective-permute-start | bytes 4718600 | tf_op jit(solution)/shard_map/ppermute | solution.py:39
  211.3 29.8 %copy-start.1 = (bf16[1,128,1536]{2,1,0:T(8,128)(2,1)S(1)}, bf16[1,128,1536]{2,1,0:T(8,128)(2,1)}, u32[]{:S(2)}) copy-start(bf16[1,128,1536]{2,1,0:T(8,128)(2,1)} %param.10) | copy-start | bytes 1179652
  215.3 13.7 %collective-permute-start.38 = (bf16[192,448]{1,0:T(8,128)(2,1)S(1)}, bf16[192,448]{1,0:T(8,128)(2,1)S(1)}, u32[]{:S(2)}, u32[]{:S(2)}) collective-permute-start(bf16[192,448]{1,0:T(8,128)(2,1)S(1)} %get-tuple-element.119), channel_id=1, source_target_pairs={{0,4},{1,5},{2,6},{3,7},{4,0},{5,1},{6,2},{7,3},{8,12},{9,13},{10,... | collective-permute-start | bytes 516104 | tf_op jit(solution)/shard_map/ppermute | solution.py:39
  221.1 14.3 %collective-permute-start.39 = (bf16[192,448]{1,0:T(8,128)(2,1)S(1)}, bf16[192,448]{1,0:T(8,128)(2,1)S(1)}, u32[]{:S(2)}, u32[]{:S(2)}) collective-permute-start(bf16[192,448]{1,0:T(8,128)(2,1)S(1)} %get-tuple-element.121), channel_id=1, source_target_pairs={{0,8},{1,9},{2,10},{3,11},{4,12},{5,13},{6,14},{7,15},{8,0},{9,1},... | collective-permute-start | bytes 516104 | tf_op jit(solution)/shard_map/ppermute | solution.py:39
  221.6 18.6 %collective-permute-start.40 = (bf16[192,448]{1,0:T(8,128)(2,1)S(1)}, bf16[192,448]{1,0:T(8,128)(2,1)S(1)}, u32[]{:S(2)}, u32[]{:S(2)}) collective-permute-start(bf16[192,448]{1,0:T(8,128)(2,1)S(1)} %get-tuple-element.120), channel_id=1, source_target_pairs={{0,12},{1,13},{2,14},{3,15},{4,8},{5,9},{6,10},{7,11},{8,4},{9,5},... | collective-permute-start | bytes 516104 | tf_op jit(solution)/shard_map/ppermute | solution.py:39
